TPU v7x, 32 devices: a whole 2x2x4 slice. The times are simulated.
32 devices in a mesh: grp: 4 (over y, core), dev: 8 (over z, x).
Axes of the slice: x: 2, y: 2, z: 4, core: 2. Of those that a mesh axis runs over, the one named last changes fastest.
Arguments:
- velocity: float32 [3, 512, 8192], P(None, None, ('grp', 'dev'))
- density: float32 [512, 8192], P(None, ('grp', 'dev')), may hold values from 0.1 to 3
- inverse_density: float32 [512, 8192], P(None, ('grp', 'dev')), may hold values from 0.25 to 4
- neighbours: int32 [6, 8192], P(None, ('grp', 'dev')), may hold values from -1 to 8191, as said below
- leaf_layer: int32 [8192], P(('grp', 'dev')), may hold values from 0 to 31, as said below
- leaf_tile: int32 [8192, 1], P(('grp', 'dev')), may hold values from 0 to 7; in each aligned block of 256 rows (0 to 255, 256 to 511, ...) at most 64 rows name the same one
- leaf_block: int32 [8192], P(('grp', 'dev')), may hold values from 0 to 255
- samples: int32 [8], replicated, may hold values from 1 to 32
Outputs:
- projected_velocity: float32 [3, 512, 8192], P(None, None, ('grp', 'dev'))
- rendered: float32 [8, 16384], P('dev', 'grp')
Inputs may be any that keep to these rules, and one draw needn't show every extreme that they name: `neighbours`: A neighbour in direction -x or +x lies on the same device or on the device with dev index one lower or higher in the same group; one in -y or +y on the same device or on the device with the same dev index in the group one lower or higher; one in -z or +z on the same device. The relation is symmetric: leaf m is beside l in direction f exactly when l is beside m in the opposite direction. A device's leaves are distinct places of a brick of 8 x 8 x 8 leaf places. `leaf_layer`: the layer of a leaf of group g lies in g * 8 to g * 8 + 7. `leaf_tile`: among the 256 leaves of one device, no tile is named by more than 64, a bound that some block reaches.
All inputs are finite; a program needn't handle non-finite values.
Results may differ from a plain program's by a relative error of at most 0.0001.
Values sent between devices are 32-bit elements; how exact they have to be, the bound alone decides.
No kernel may reach another device: no remote copies, remote signals or barrier semaphores. Data moves between devices by JAX's collectives and lax.ppermute only.
A program may use at most 64 MiB of HBM per device.

v0:
```python
import jax
import jax.numpy as jnp
from jax import lax
from jax.sharding import PartitionSpec as P

ITERS = 3
BLOCKS = 256


advect_step = 0.2
ray_step = 0.03


def extended(block, sides, width):
    for axis, dim in sides:
        count = lax.axis_size(axis)
        forward = [(i, i + 1) for i in range(count - 1)]
        backward = [(target, source) for source, target in forward]
        low = lax.ppermute(
            lax.slice_in_dim(block, block.shape[dim] - width, None, axis=dim), axis, forward
        )
        high = lax.ppermute(lax.slice_in_dim(block, 0, width, axis=dim), axis, backward)
        block = jnp.concatenate([low, block, high], axis=dim)
    return block


def shifted(first, second, third, face_list):
    leaf_count = first.shape[-1]
    minus_x = jnp.concatenate([face_list[0].reshape(1, 8, 8, leaf_count), first[:-1]], axis=0)
    plus_x = jnp.concatenate([first[1:], face_list[1].reshape(1, 8, 8, leaf_count)], axis=0)
    minus_y = jnp.concatenate([face_list[2].reshape(8, 1, 8, leaf_count), second[:, :-1]], axis=1)
    plus_y = jnp.concatenate([second[:, 1:], face_list[3].reshape(8, 1, 8, leaf_count)], axis=1)
    minus_z = jnp.concatenate([face_list[4].reshape(8, 8, 1, leaf_count), third[:, :, :-1]], axis=2)
    plus_z = jnp.concatenate([third[:, :, 1:], face_list[5].reshape(8, 8, 1, leaf_count)], axis=2)
    return [minus_x, plus_x, minus_y, plus_y, minus_z, plus_z]


def energy_sum(residual, precond):
    return lax.psum(jnp.sum(residual * precond), ("grp", "dev"))


def blend_faces(base_list, factor, added_list):
    return [base_list[face_id] + factor * added_list[face_id] for face_id in range(6)]


def shards(
    velocity, density, inverse_density, neighbours, leaf_layer, leaf_tile, leaf_block, samples
):
    leaf_count = density.shape[1]
    members = lax.axis_size("dev")
    myself = lax.axis_index("grp") * members + lax.axis_index("dev")
    owner_id = neighbours // leaf_count
    slot_index = neighbours % leaf_count
    present = neighbours >= 0
    lookup = jnp.where(
        present, jnp.where(owner_id == myself, slot_index, slot_index + leaf_count), 0
    )
    grid_shape = (8, 8, 8, leaf_count)

    def face_values(first, second, third):
        x_stack = jnp.stack([first[0].reshape(64, leaf_count), first[7].reshape(64, leaf_count)])
        x_rim = extended(x_stack, (("dev", 0),), 1)
        y_stack = jnp.stack(
            [second[:, 0].reshape(64, leaf_count), second[:, 7].reshape(64, leaf_count)]
        )
        y_rim = extended(y_stack, (("grp", 0),), 1)
        tables = [
            jnp.concatenate([x_stack[1], x_rim[0]], axis=1),
            jnp.concatenate([x_stack[0], x_rim[3]], axis=1),
            jnp.concatenate([y_stack[1], y_rim[0]], axis=1),
            jnp.concatenate([y_stack[0], y_rim[3]], axis=1),
            third[:, :, 7].reshape(64, leaf_count),
            third[:, :, 0].reshape(64, leaf_count),
        ]
        return [
            jnp.where(
                present[face_id][None, :], jnp.take(tables[face_id], lookup[face_id], axis=1), 0.0
            )
            for face_id in range(6)
        ]

    def beside_all(first, second, third):
        return shifted(first, second, third, face_values(first, second, third))

    inverse = inverse_density.reshape(grid_shape)
    dens_grid = density.reshape(grid_shape)
    velocity_grid = velocity.reshape((3,) + grid_shape)
    ones_grid = jnp.ones(grid_shape, jnp.float32)
    presence_faces = [
        jnp.broadcast_to(present[face_id][None, :].astype(jnp.float32), (64, leaf_count))
        for face_id in range(6)
    ]
    presence = shifted(ones_grid, ones_grid, ones_grid, presence_faces)
    inverse_near = beside_all(inverse, inverse, inverse)
    coupling = [
        0.5 * (inverse + inverse_near[face_id]) + 0.5 * inverse * (1.0 - presence[face_id])
        for face_id in range(6)
    ]
    diagonal = coupling[0] + coupling[1] + coupling[2] + coupling[3] + coupling[4] + coupling[5]
    vel_near = beside_all(velocity_grid[0], velocity_grid[1], velocity_grid[2])
    source = -0.5 * (
        vel_near[1] - vel_near[0] + (vel_near[3] - vel_near[2]) + (vel_near[5] - vel_near[4])
    )
    pressure = jnp.zeros(grid_shape, jnp.float32)
    press_faces = [jnp.zeros((64, leaf_count), jnp.float32) for face_id in range(6)]
    residual = source
    precond = residual / diagonal
    energy = energy_sum(residual, precond)
    direction = precond
    for iteration in range(ITERS):
        face_list = face_values(direction, direction, direction)
        near_list = shifted(direction, direction, direction, face_list)
        total = diagonal * direction
        for operate_face_id in range(6):
            total = total - coupling[operate_face_id] * near_list[operate_face_id]
        curvature = lax.psum(jnp.sum(direction * total), ("grp", "dev"))
        step_size = energy / curvature
        pressure = pressure + step_size * direction
        press_faces = blend_faces(press_faces, step_size, face_list)
        residual = residual - step_size * total
        if iteration + 1 < ITERS:
            precond = residual / diagonal
            fresh = energy_sum(residual, precond)
            direction = precond + fresh / energy * direction
            energy = fresh
    press_near = beside_all(pressure, pressure, pressure)
    gradient = (
        jnp.stack(
            [
                press_near[1] - press_near[0],
                press_near[3] - press_near[2],
                press_near[5] - press_near[4],
            ]
        )
        * 0.5
    )
    new_velocity = velocity_grid - inverse[None] * gradient
    flux = dens_grid[None] * new_velocity
    flux_near = beside_all(flux[0], flux[1], flux[2])
    change = 0.5 * (
        flux_near[1] - flux_near[0] + (flux_near[3] - flux_near[2]) + (flux_near[5] - flux_near[4])
    )
    advected = dens_grid - advect_step * change
    column = ray_step * jnp.sum(advected, axis=1).reshape(64, leaf_count)
    tile_count = samples.shape[0]
    tile_ids = leaf_tile[:, 0]
    tile_hot = (tile_ids[:, None] == jnp.arange(tile_count, dtype=jnp.int32)[None, :]).astype(
        jnp.int32
    )
    march_limit = jnp.sum(tile_hot * samples[None, :], axis=1)
    marched = (leaf_layer < march_limit).astype(jnp.float32)
    contrib = column * marched[None, :]
    target_cell = tile_ids * BLOCKS + leaf_block
    block_hot = (
        target_cell[:, None] == jnp.arange(tile_count * BLOCKS, dtype=jnp.int32)[None, :]
    ).astype(jnp.float32)
    full_image = jnp.dot(
        contrib, block_hot, precision=lax.Precision.HIGHEST, preferred_element_type=jnp.float32
    )
    partial_value = lax.psum_scatter(
        full_image.reshape(64, tile_count, BLOCKS), "dev", scatter_dimension=1, tiled=True
    )[:, 0, :]
    optical = lax.psum_scatter(partial_value, "grp", scatter_dimension=0, tiled=True)
    rendered = (1.0 - jnp.exp(-optical)).reshape(1, -1)
    return (new_velocity.reshape(3, 512, leaf_count), rendered)


def solution(mesh):
    return jax.shard_map(
        shards,
        mesh=mesh,
        in_specs=(
            P(None, None, ("grp", "dev")),
            P(None, ("grp", "dev")),
            P(None, ("grp", "dev")),
            P(None, ("grp", "dev")),
            P(("grp", "dev")),
            P(("grp", "dev"), None),
            P(("grp", "dev")),
            P(),
        ),
        out_specs=(P(None, None, ("grp", "dev")), P("dev", "grp")),
        check_vma=False,
    )
```

profile of v0, /device:TPU:0, one launch (start us, length us, event | category | flops | bytes accessed | tf_op | source)
XLA Modules:
  0.0 638.2 jit_solution(236446409696689988)
XLA Ops:
  8.9 1.4 collective-permute-start.7
  15.0 4.3 collective-permute-start.6
  20.1 4.5 collective-permute-start.3
  26.1 4.7 collective-permute-start.1
  54.8 2.8 collective-permute-start.4
  73.6 4.6 fusion.56
  84.0 5.8 collective-permute-start.8
  92.6 1.9 collective-permute-start.10
  102.0 1.6 copy.431
  103.6 1.6 copy.434
  105.2 1.6 copy.438
  107.4 1.5 copy.443
  115.4 1.7 bitcast_select_fusion.28
  118.1 1.3 gather_fusion.14
  121.2 1.6 copy.432
  126.1 4.5 multiply_reduce_fusion.3
  130.6 43.5 %all-reduce.6 = (f32[]{:T(128)}, f32[]{:T(128)}) all-reduce(f32[]{:T(128)} %get-tuple-element.5, f32[]{:T(128)} %get-tuple-element.4), channel_id=1, replica_groups=mesh['grp'=4,'dev'=8] {'grp','dev'}, use_global_device_ids=true, to_apply=%region_1.4 | all-reduce | flops 2 | bytes 16 | tf_op jit(solution)/shard_map/psum | solution.py:39
  175.3 2.9 multiply_reduce_fusion.2
  178.2 41.3 %psum.44 = f32[]{:T(128)} all-reduce(f32[]{:T(128)} %get-tuple-element.16), channel_id=1, replica_groups=mesh['grp'=4,'dev'=8] {'grp','dev'}, use_global_device_ids=true, to_apply=%region_5.8 | all-reduce | flops 1 | bytes 8 | tf_op jit(solution)/shard_map/psum | solution.py:39
  227.7 4.8 collective-permute-start.12
  235.3 1.9 collective-permute-start.14
  244.6 1.6 copy.451
  246.2 1.6 copy.454
  247.8 1.6 copy.458
  250.1 1.5 copy.463
  258.0 1.7 bitcast_select_fusion.22
  260.7 1.3 gather_fusion.20
  263.8 1.6 copy.452
  268.7 4.5 multiply_reduce_fusion.1
  273.2 42.3 %psum.45 = f32[]{:T(128)} all-reduce(f32[]{:T(128)} %get-tuple-element.14), channel_id=1, replica_groups=mesh['grp'=4,'dev'=8] {'grp','dev'}, use_global_device_ids=true, to_apply=%region_7.10 | all-reduce | flops 1 | bytes 8 | tf_op jit(solution)/shard_map/psum | solution.py:116
  316.8 1.9 multiply_reduce_fusion
  319.4 41.6 %psum.46 = f32[]{:T(128)} all-reduce(f32[]{:T(128)} %multiply_reduce_fusion), channel_id=1, replica_groups=mesh['grp'=4,'dev'=8] {'grp','dev'}, use_global_device_ids=true, to_apply=%region_9.12 | all-reduce | flops 1 | bytes 8 | tf_op jit(solution)/shard_map/psum | solution.py:39
  362.3 1.3 multiply_add_fusion.1
  369.5 4.8 collective-permute-start.16
  377.1 1.9 collective-permute-start.18
  386.4 1.6 copy.471
  388.0 1.6 copy.474
  389.6 1.6 copy.478
  391.9 1.5 copy.483
  399.9 1.7 bitcast_select_fusion.16
  402.6 1.3 gather_fusion.26
  405.7 1.6 copy.472
  410.5 3.8 fusion.46
  415.0 42.2 %psum.47 = f32[]{:T(128)} all-reduce(f32[]{:T(128)} %fusion.46), channel_id=1, replica_groups=mesh['grp'=4,'dev'=8] {'grp','dev'}, use_global_device_ids=true, to_apply=%region_11.14 | all-reduce | flops 1 | bytes 8 | tf_op jit(solution)/shard_map/psum | solution.py:116
  461.9 4.8 collective-permute-start.21
  469.0 1.6 copy.497
  470.6 1.9 collective-permute-start.23
  499.4 1.5 gather_fusion.41
  504.1 1.6 slice_bitcast_fusion.15
  507.2 1.6 copy.514
  508.8 1.6 copy.517
  510.4 5.9 collective-permute-start.27
  516.3 1.6 copy.518
  517.8 1.6 copy.507
  520.7 1.6 copy.508
  523.1 5.8 collective-permute-start.25
  530.0 1.3 gather_fusion.38
  532.3 1.3 gather_fusion.39
  537.3 1.3 gather_fusion.36
  541.6 2.3 fusion.45
  544.0 2.1 fusion
  547.0 62.0 %reduce-scatter.3.cloned.1.call-done = f32[64,1,256]{2,0,1:T(8,128)} async-done(((f32[64,8,256]{2,0,1:T(8,128)}), f32[64,1,256]{2,0,1:T(8,128)}) %reduce-scatter.3.cloned.1.call-update) | async-done | bytes 65552 | tf_op jit(solution)/shard_map/reduce_scatter | solution.py:160
  609.0 2.6 fusion.2
  611.6 18.4 %reduce-scatter.5.cloned.1.call-done = f32[16,256]{1,0:T(8,128)} async-done(((f32[64,256]{1,0:T(8,128)}), f32[16,256]{1,0:T(8,128)}) %reduce-scatter.5.cloned.1.call-update) | async-done | bytes 16400 | tf_op jit(solution)/shard_map/reduce_scatter | solution.py:163
  (456 shorter events, 187.2 us)
Async XLA Ops:
  7.2 601.8 %reduce-scatter.3.cloned.1.call-start = ((), (), s32[]{:S(2)}) async-start(), calls=%async_computation.2 | async-start | bytes 589824 | tf_op jit(solution)/shard_map/reduce_scatter | solution.py:160
  8.9 15.7 %copy-start.1 = (f32[3,512,256]{2,1,0:T(8,128)S(1)}, f32[3,512,256]{2,1,0:T(8,128)}, u32[]{:S(2)}) copy-start(f32[3,512,256]{2,1,0:T(8,128)} %param.12) | copy-start | bytes 4718596
  8.9 21.9 %copy-start.19 = (s32[6,256]{1,0:T(8,128)S(1)}, s32[6,256]{1,0:T(8,128)}, u32[]{:S(2)}) copy-start(s32[6,256]{1,0:T(8,128)} %param.15) | copy-start | bytes 18436
  8.9 24.2 %copy-start = (f32[512,256]{1,0:T(8,128)S(1)}, f32[512,256]{1,0:T(8,128)}, u32[]{:S(2)}) copy-start(f32[512,256]{1,0:T(8,128)} %param.14) | copy-start | bytes 1572868
  8.9 45.9 %collective-permute-start.7 = (f32[1,64,256]{1,2,0:T(8,128)}, f32[1,64,256]{1,2,0:T(8,128)}, u32[]{:S(2)}, u32[]{:S(2)}) collective-permute-start(f32[1,64,256]{1,2,0:T(8,128)} %copy.417), channel_id=1, source_target_pairs={{8,0},{16,8},{24,16},{9,1},{17,9},{25,17},{10,2},{18,10},{26,18},{... | collective-permute-start | bytes 196616 | tf_op jit(solution)/shard_map/ppermute | solution.py:22
  13.0 46.3 %collective-permute-start.2 = (f32[1,64,256]{1,2,0:T(8,128)}, f32[1,64,256]{1,2,0:T(8,128)}, u32[]{:S(2)}, u32[]{:S(2)}) collective-permute-start(f32[1,64,256]{1,2,0:T(8,128)} %copy.395), channel_id=1, source_target_pairs={{8,0},{16,8},{24,16},{9,1},{17,9},{25,17},{10,2},{18,10},{26,18},{... | collective-permute-start | bytes 196616 | tf_op jit(solution)/shard_map/ppermute | solution.py:22
  15.0 47.3 %collective-permute-start.6 = (f32[1,64,256]{1,2,0:T(8,128)}, f32[1,64,256]{1,2,0:T(8,128)}, u32[]{:S(2)}, u32[]{:S(2)}) collective-permute-start(f32[1,64,256]{1,2,0:T(8,128)} %copy.413), channel_id=1, source_target_pairs={{0,8},{8,16},{16,24},{1,9},{9,17},{17,25},{2,10},{10,18},{18,26},{... | collective-permute-start | bytes 196616 | tf_op jit(solution)/shard_map/ppermute | solution.py:19
  20.1 45.2 %collective-permute-start.3 = (f32[1,64,256]{1,2,0:T(8,128)}, f32[1,64,256]{1,2,0:T(8,128)}, u32[]{:S(2)}, u32[]{:S(2)}) collective-permute-start(f32[1,64,256]{1,2,0:T(8,128)} %copy.399), channel_id=1, source_target_pairs={{0,8},{8,16},{16,24},{1,9},{9,17},{17,25},{2,10},{10,18},{18,26},{... | collective-permute-start | bytes 196616 | tf_op jit(solution)/shard_map/ppermute | solution.py:19
  26.1 40.8 %collective-permute-start.1 = (f32[1,64,256]{1,2,0:T(8,128)S(1)}, f32[1,64,256]{1,2,0:T(8,128)}, u32[]{:S(2)}, u32[]{:S(2)}) collective-permute-start(f32[1,64,256]{1,2,0:T(8,128)S(1)} %copy.542), channel_id=1, source_target_pairs={{0,1},{1,2},{2,3},{3,4},{4,5},{5,6},{6,7},{8,9},{9,10},{10,11},{11... | collective-permute-start | bytes 196616 | tf_op jit(solution)/shard_map/ppermute | solution.py:19
  34.3 13.7 %copy-start.40 = (pred[256]{0:T(512)(128)(4,1)}, pred[256]{0:T(512)(128)(4,1)S(1)}, u32[]{:S(2)}) copy-start(pred[256]{0:T(512)(128)(4,1)S(1)} %compare_and_fusion.1) | copy-start | bytes 772
  34.9 15.9 %copy-start.41 = (pred[256]{0:T(512)(128)(4,1)}, pred[256]{0:T(512)(128)(4,1)S(1)}, u32[]{:S(2)}) copy-start(pred[256]{0:T(512)(128)(4,1)S(1)} %compare_and_fusion) | copy-start | bytes 772
  46.0 4.8 copy-start.31
  46.0 23.3 %copy-start.29 = (pred[256]{0:T(512)(128)(4,1)}, pred[256]{0:T(512)(128)(4,1)S(1)}, u32[]{:S(2)}) copy-start(pred[256]{0:T(512)(128)(4,1)S(1)} %get-tuple-element.9) | copy-start | bytes 772
  46.0 23.5 %copy-start.27 = (pred[256]{0:T(512)(128)(4,1)}, pred[256]{0:T(512)(128)(4,1)S(1)}, u32[]{:S(2)}) copy-start(pred[256]{0:T(512)(128)(4,1)S(1)} %get-tuple-element.8) | copy-start | bytes 772
  46.0 23.6 %copy-start.22 = (pred[256]{0:T(512)(128)(4,1)}, pred[256]{0:T(512)(128)(4,1)S(1)}, u32[]{:S(2)}) copy-start(pred[256]{0:T(512)(128)(4,1)S(1)} %get-tuple-element.10) | copy-start | bytes 772
  46.0 25.9 %copy-start.24 = (pred[256]{0:T(512)(128)(4,1)}, pred[256]{0:T(512)(128)(4,1)S(1)}, u32[]{:S(2)}) copy-start(pred[256]{0:T(512)(128)(4,1)S(1)} %get-tuple-element.11) | copy-start | bytes 772
  49.0 4.2 copy-start.46
  49.0 4.2 copy-start.10
  49.2 4.2 copy-start.9
  49.3 4.4 copy-start.43
  49.3 4.4 copy-start.55
  49.3 5.0 copy-start.51
  49.3 5.5 copy-start.45
  54.8 12.1 %collective-permute-start.4 = (f32[1,64,256]{1,2,0:T(8,128)S(1)}, f32[1,64,256]{1,2,0:T(8,128)S(1)}, u32[]{:S(2)}, u32[]{:S(2)}) collective-permute-start(f32[1,64,256]{1,2,0:T(8,128)S(1)} %bitcast.399), channel_id=1, source_target_pairs={{0,1},{1,2},{2,3},{3,4},{4,5},{5,6},{6,7},{8,9},{9,10},{10,11},{11... | collective-permute-start | bytes 196616 | tf_op jit(solution)/shard_map/ppermute | solution.py:19
  59.3 11.1 %collective-permute-start.5 = (f32[1,64,256]{1,2,0:T(8,128)S(1)}, f32[1,64,256]{1,2,0:T(8,128)S(1)}, u32[]{:S(2)}, u32[]{:S(2)}) collective-permute-start(f32[1,64,256]{1,2,0:T(8,128)S(1)} %bitcast.398), channel_id=1, source_target_pairs={{1,0},{2,1},{3,2},{4,3},{5,4},{6,5},{7,6},{9,8},{10,9},{11,10},{12... | collective-permute-start | bytes 196616 | tf_op jit(solution)/shard_map/ppermute | solution.py:22
  62.3 8.9 %collective-permute-start = (f32[1,64,256]{1,2,0:T(8,128)S(1)}, f32[1,64,256]{1,2,0:T(8,128)S(1)}, u32[]{:S(2)}, u32[]{:S(2)}) collective-permute-start(f32[1,64,256]{1,2,0:T(8,128)S(1)} %copy.541), channel_id=1, source_target_pairs={{1,0},{2,1},{3,2},{4,3},{5,4},{6,5},{7,6},{9,8},{10,9},{11,10},{12... | collective-permute-start | bytes 196616 | tf_op jit(solution)/shard_map/ppermute | solution.py:22
  65.2 4.1 copy-start.36
  78.2 47.9 %copy-start.5 = (f32[8,8,8,256]{3,2,1,0:T(8,128)}, f32[8,8,8,256]{3,2,1,0:T(8,128)S(1)}, u32[]{:S(2)}) copy-start(f32[8,8,8,256]{3,2,1,0:T(8,128)S(1)} %get-tuple-element.24) | copy-start | bytes 1572868
  78.2 190.5 %copy-start.4 = (f32[8,8,8,256]{3,2,1,0:T(8,128)}, f32[8,8,8,256]{3,2,1,0:T(8,128)S(1)}, u32[]{:S(2)}) copy-start(f32[8,8,8,256]{3,2,1,0:T(8,128)S(1)} %get-tuple-element.23) | copy-start | bytes 1572868
  84.0 25.7 %collective-permute-start.8 = (f32[1,64,256]{1,2,0:T(8,128)}, f32[1,64,256]{1,2,0:T(8,128)}, u32[]{:S(2)}, u32[]{:S(2)}) collective-permute-start(f32[1,64,256]{1,2,0:T(8,128)} %copy.427), channel_id=1, source_target_pairs={{0,1},{1,2},{2,3},{3,4},{4,5},{5,6},{6,7},{8,9},{9,10},{10,11},{11... | collective-permute-start | bytes 196616 | tf_op jit(solution)/shard_map/ppermute | solution.py:19
  90.6 22.4 %collective-permute-start.9 = (f32[1,64,256]{1,2,0:T(8,128)}, f32[1,64,256]{1,2,0:T(8,128)}, u32[]{:S(2)}, u32[]{:S(2)}) collective-permute-start(f32[1,64,256]{1,2,0:T(8,128)} %copy.430), channel_id=1, source_target_pairs={{1,0},{2,1},{3,2},{4,3},{5,4},{6,5},{7,6},{9,8},{10,9},{11,10},{12... | collective-permute-start | bytes 196616 | tf_op jit(solution)/shard_map/ppermute | solution.py:22
  92.6 24.4 %collective-permute-start.10 = (f32[1,64,256]{1,2,0:T(8,128)}, f32[1,64,256]{1,2,0:T(8,128)}, u32[]{:S(2)}, u32[]{:S(2)}) collective-permute-start(f32[1,64,256]{1,2,0:T(8,128)} %copy.433), channel_id=1, source_target_pairs={{0,8},{8,16},{16,24},{1,9},{9,17},{17,25},{2,10},{10,18},{18,26},{... | collective-permute-start | bytes 196616 | tf_op jit(solution)/shard_map/ppermute | solution.py:19
  95.3 28.1 %collective-permute-start.11 = (f32[1,64,256]{1,2,0:T(8,128)}, f32[1,64,256]{1,2,0:T(8,128)}, u32[]{:S(2)}, u32[]{:S(2)}) collective-permute-start(f32[1,64,256]{1,2,0:T(8,128)} %copy.437), channel_id=1, source_target_pairs={{8,0},{16,8},{24,16},{9,1},{17,9},{25,17},{10,2},{18,10},{26,18},{... | collective-permute-start | bytes 196616 | tf_op jit(solution)/shard_map/ppermute | solution.py:22
  227.7 24.7 %collective-permute-start.12 = (f32[1,64,256]{1,2,0:T(8,128)}, f32[1,64,256]{1,2,0:T(8,128)}, u32[]{:S(2)}, u32[]{:S(2)}) collective-permute-start(f32[1,64,256]{1,2,0:T(8,128)} %copy.447), channel_id=1, source_target_pairs={{0,1},{1,2},{2,3},{3,4},{4,5},{5,6},{6,7},{8,9},{9,10},{10,11},{11... | collective-permute-start | bytes 196616 | tf_op jit(solution)/shard_map/ppermute | solution.py:19
  233.3 22.4 %collective-permute-start.13 = (f32[1,64,256]{1,2,0:T(8,128)}, f32[1,64,256]{1,2,0:T(8,128)}, u32[]{:S(2)}, u32[]{:S(2)}) collective-permute-start(f32[1,64,256]{1,2,0:T(8,128)} %copy.450), channel_id=1, source_target_pairs={{1,0},{2,1},{3,2},{4,3},{5,4},{6,5},{7,6},{9,8},{10,9},{11,10},{12... | collective-permute-start | bytes 196616 | tf_op jit(solution)/shard_map/ppermute | solution.py:22
  235.3 24.4 %collective-permute-start.14 = (f32[1,64,256]{1,2,0:T(8,128)}, f32[1,64,256]{1,2,0:T(8,128)}, u32[]{:S(2)}, u32[]{:S(2)}) collective-permute-start(f32[1,64,256]{1,2,0:T(8,128)} %copy.453), channel_id=1, source_target_pairs={{0,8},{8,16},{16,24},{1,9},{9,17},{17,25},{2,10},{10,18},{18,26},{... | collective-permute-start | bytes 196616 | tf_op jit(solution)/shard_map/ppermute | solution.py:19
  238.0 28.1 %collective-permute-start.15 = (f32[1,64,256]{1,2,0:T(8,128)}, f32[1,64,256]{1,2,0:T(8,128)}, u32[]{:S(2)}, u32[]{:S(2)}) collective-permute-start(f32[1,64,256]{1,2,0:T(8,128)} %copy.457), channel_id=1, source_target_pairs={{8,0},{16,8},{24,16},{9,1},{17,9},{25,17},{10,2},{18,10},{26,18},{... | collective-permute-start | bytes 196616 | tf_op jit(solution)/shard_map/ppermute | solution.py:22
  273.2 45.6 %copy-start.44 = (s32[256]{0:T(256)S(1)}, s32[256]{0:T(256)}, u32[]{:S(2)}) copy-start(s32[256]{0:T(256)} %select_reduce_fusion) | copy-start | bytes 3076
  273.2 45.6 %copy-start.52 = (s32[256]{0:T(256)S(1)}, s32[256]{0:T(256)}, u32[]{:S(2)}) copy-start(s32[256]{0:T(256)} %param.16) | copy-start | bytes 3076
  369.5 24.7 %collective-permute-start.16 = (f32[1,64,256]{1,2,0:T(8,128)}, f32[1,64,256]{1,2,0:T(8,128)}, u32[]{:S(2)}, u32[]{:S(2)}) collective-permute-start(f32[1,64,256]{1,2,0:T(8,128)} %copy.467), channel_id=1, source_target_pairs={{0,1},{1,2},{2,3},{3,4},{4,5},{5,6},{6,7},{8,9},{9,10},{10,11},{11... | collective-permute-start | bytes 196616 | tf_op jit(solution)/shard_map/ppermute | solution.py:19
  375.1 22.5 %collective-permute-start.17 = (f32[1,64,256]{1,2,0:T(8,128)}, f32[1,64,256]{1,2,0:T(8,128)}, u32[]{:S(2)}, u32[]{:S(2)}) collective-permute-start(f32[1,64,256]{1,2,0:T(8,128)} %copy.470), channel_id=1, source_target_pairs={{1,0},{2,1},{3,2},{4,3},{5,4},{6,5},{7,6},{9,8},{10,9},{11,10},{12... | collective-permute-start | bytes 196616 | tf_op jit(solution)/shard_map/ppermute | solution.py:22
  377.1 24.5 %collective-permute-start.18 = (f32[1,64,256]{1,2,0:T(8,128)}, f32[1,64,256]{1,2,0:T(8,128)}, u32[]{:S(2)}, u32[]{:S(2)}) collective-permute-start(f32[1,64,256]{1,2,0:T(8,128)} %copy.473), channel_id=1, source_target_pairs={{0,8},{8,16},{16,24},{1,9},{9,17},{17,25},{2,10},{10,18},{18,26},{... | collective-permute-start | bytes 196616 | tf_op jit(solution)/shard_map/ppermute | solution.py:19
  379.8 28.2 %collective-permute-start.19 = (f32[1,64,256]{1,2,0:T(8,128)}, f32[1,64,256]{1,2,0:T(8,128)}, u32[]{:S(2)}, u32[]{:S(2)}) collective-permute-start(f32[1,64,256]{1,2,0:T(8,128)} %copy.477), channel_id=1, source_target_pairs={{8,0},{16,8},{24,16},{9,1},{17,9},{25,17},{10,2},{18,10},{26,18},{... | collective-permute-start | bytes 196616 | tf_op jit(solution)/shard_map/ppermute | solution.py:22
  461.2 12.9 %copy-start.18 = (f32[8,8,1,256]{3,2,1,0:T(1,128)S(1)}, f32[8,8,1,256]{3,2,1,0:T(1,128)}, u32[]{:S(2)}) copy-start(f32[8,8,1,256]{3,2,1,0:T(1,128)} %get-tuple-element.65) | copy-start | bytes 196612
  461.2 14.9 %copy-start.16 = (f32[8,8,1,256]{3,2,1,0:T(1,128)S(1)}, f32[8,8,1,256]{3,2,1,0:T(1,128)}, u32[]{:S(2)}) copy-start(f32[8,8,1,256]{3,2,1,0:T(1,128)} %get-tuple-element.66) | copy-start | bytes 196612
  461.9 17.2 %collective-permute-start.21 = (f32[1,64,256]{1,2,0:T(8,128)}, f32[1,64,256]{1,2,0:T(8,128)}, u32[]{:S(2)}, u32[]{:S(2)}) collective-permute-start(f32[1,64,256]{1,2,0:T(8,128)} %copy.490), channel_id=1, source_target_pairs={{0,1},{1,2},{2,3},{3,4},{4,5},{5,6},{6,7},{8,9},{9,10},{10,11},{11... | collective-permute-start | bytes 196616 | tf_op jit(solution)/shard_map/ppermute | solution.py:19
  467.6 13.9 %collective-permute-start.20 = (f32[1,64,256]{1,2,0:T(8,128)}, f32[1,64,256]{1,2,0:T(8,128)}, u32[]{:S(2)}, u32[]{:S(2)}) collective-permute-start(f32[1,64,256]{1,2,0:T(8,128)} %copy.487), channel_id=1, source_target_pairs={{1,0},{2,1},{3,2},{4,3},{5,4},{6,5},{7,6},{9,8},{10,9},{11,10},{12... | collective-permute-start | bytes 196616 | tf_op jit(solution)/shard_map/ppermute | solution.py:22
  470.6 12.8 %collective-permute-start.23 = (f32[1,64,256]{1,2,0:T(8,128)}, f32[1,64,256]{1,2,0:T(8,128)}, u32[]{:S(2)}, u32[]{:S(2)}) collective-permute-start(f32[1,64,256]{1,2,0:T(8,128)} %copy.497), channel_id=1, source_target_pairs={{0,8},{8,16},{16,24},{1,9},{9,17},{17,25},{2,10},{10,18},{18,26},{... | collective-permute-start | bytes 196616 | tf_op jit(solution)/shard_map/ppermute | solution.py:19
  472.7 14.6 %collective-permute-start.22 = (f32[1,64,256]{1,2,0:T(8,128)S(1)}, f32[1,64,256]{1,2,0:T(8,128)}, u32[]{:S(2)}, u32[]{:S(2)}) collective-permute-start(f32[1,64,256]{1,2,0:T(8,128)S(1)} %copy.493), channel_id=1, source_target_pairs={{8,0},{16,8},{24,16},{9,1},{17,9},{25,17},{10,2},{18,10},{26,18},{... | collective-permute-start | bytes 196616 | tf_op jit(solution)/shard_map/ppermute | solution.py:22
  479.1 4.1 copy-start.25
  479.1 4.1 copy-start.35
  480.0 5.0 copy-start.28
  480.0 5.0 copy-start.39
  483.4 5.6 copy-start.30
  483.4 5.6 copy-start.37
  492.7 3.8 copy-start.3
  501.6 27.3 %collective-permute-start.26 = (f32[1,64,256]{1,2,0:T(8,128)}, f32[1,64,256]{1,2,0:T(8,128)}, u32[]{:S(2)}, u32[]{:S(2)}) collective-permute-start(f32[1,64,256]{1,2,0:T(8,128)} %copy.513), channel_id=1, source_target_pairs={{8,0},{16,8},{24,16},{9,1},{17,9},{25,17},{10,2},{18,10},{26,18},{... | collective-permute-start | bytes 196616 | tf_op jit(solution)/shard_map/ppermute | solution.py:22
  505.7 23.2 %copy-start.12 = (f32[64,256]{1,0:T(8,128)S(1)}, f32[64,256]{1,0:T(8,128)}, u32[]{:S(2)}) copy-start(f32[64,256]{1,0:T(8,128)} %get-tuple-element.31) | copy-start | bytes 196612
  510.4 21.0 %collective-permute-start.27 = (f32[1,64,256]{1,2,0:T(8,128)}, f32[1,64,256]{1,2,0:T(8,128)}, u32[]{:S(2)}, u32[]{:S(2)}) collective-permute-start(f32[1,64,256]{1,2,0:T(8,128)} %copy.517), channel_id=1, source_target_pairs={{0,8},{8,16},{16,24},{1,9},{9,17},{17,25},{2,10},{10,18},{18,26},{... | collective-permute-start | bytes 196616 | tf_op jit(solution)/shard_map/ppermute | solution.py:19
  519.4 16.8 %collective-permute-start.24 = (f32[1,64,256]{1,2,0:T(8,128)}, f32[1,64,256]{1,2,0:T(8,128)}, u32[]{:S(2)}, u32[]{:S(2)}) collective-permute-start(f32[1,64,256]{1,2,0:T(8,128)} %copy.507), channel_id=1, source_target_pairs={{1,0},{2,1},{3,2},{4,3},{5,4},{6,5},{7,6},{9,8},{10,9},{11,10},{12... | collective-permute-start | bytes 196616 | tf_op jit(solution)/shard_map/ppermute | solution.py:22
  523.1 15.5 %collective-permute-start.25 = (f32[1,64,256]{1,2,0:T(8,128)}, f32[1,64,256]{1,2,0:T(8,128)}, u32[]{:S(2)}, u32[]{:S(2)}) collective-permute-start(f32[1,64,256]{1,2,0:T(8,128)} %copy.510), channel_id=1, source_target_pairs={{0,1},{1,2},{2,3},{3,4},{4,5},{5,6},{6,7},{8,9},{9,10},{10,11},{11... | collective-permute-start | bytes 196616 | tf_op jit(solution)/shard_map/ppermute | solution.py:19
  533.7 6.6 %copy-start.23 = (pred[256]{0:T(512)(128)(4,1)S(1)}, pred[256]{0:T(512)(128)(4,1)}, u32[]{:S(2)}) copy-start(pred[256]{0:T(512)(128)(4,1)} %copy-done.22) | copy-start | bytes 772
  533.7 6.6 %copy-start.26 = (pred[256]{0:T(512)(128)(4,1)S(1)}, pred[256]{0:T(512)(128)(4,1)}, u32[]{:S(2)}) copy-start(pred[256]{0:T(512)(128)(4,1)} %copy-done.24) | copy-start | bytes 772
  546.1 83.9 %reduce-scatter.5.cloned.1.call-start = ((), (), s32[]{:S(2)}) async-start(), calls=%async_computation.3 | async-start | bytes 81920 | tf_op jit(solution)/shard_map/reduce_scatter | solution.py:163
  (22 other events, 54.1 us)
Sparse Core Ops, SparseCore 0:
  546.2 62.7 reduce-scatter.2
  611.5 18.4 reduce-scatter.4
where the time goes:
time: 642 us; the launch traced here: 638 us
  blocking collectives  211 us (33%)
  local copies, waits for them, and re-layouts  155 us (24%)
  other arithmetic  93.4 us (15%)
  waiting for transfers between devices  80.5 us (13%)
  starting transfers between devices  74.2 us (12%)
  between operations  22.3 us (3%)
    psum x3, blocking collectives, energy_sum(): return lax.psum(jnp.sum(residual * precond), ('grp', 'dev'))  126 us
    psum x2, blocking collectives, shards(): curvature = lax.psum(jnp.sum(direction * total), ('grp', 'dev'))  84.5 us
    reduce_scatter x1, waiting for transfers between devices, shards(): lax.psum_scatter(full_image.reshape(64, tile_count, BLOCKS), 'dev', scatt...  62 us
    ppermute x14, starting transfers between devices, extended(): lax.ppermute(lax.slice_in_dim(block, block.shape[dim] - width, None, axis...  56 us
    gather x42, local copies, waits for them, and re-layouts, face_values(): jnp.take(tables[face_id], lookup[face_id], axis=1)  39.9 us
    select_n x33, other arithmetic, face_values(): jnp.where(present[face_id][None, :], jnp.take(tables[face_id], lookup[fac...  25.5 us
    select_n x42, local copies, waits for them, and re-layouts, face_values(): jnp.where(present[face_id][None, :], jnp.take(tables[face_id], lookup[fac...  18.4 us
    reduce_scatter x1, waiting for transfers between devices, shards(): lax.psum_scatter(partial_value, 'grp', scatter_dimension=0, tiled=True)  18.4 us
  transfers between devices with their start and end apart: 30, of which 2 were waited for; matrix products, arithmetic and copies ran while one was open for 26% of the time, Pallas kernels for 0%

commit v1 on v0

v1 whole, which is shorter than its diff:
```python
import functools

import jax
import jax.numpy as jnp
from jax import lax
from jax.experimental import pallas as pl
from jax.experimental.pallas import tpu as pltpu
from jax.sharding import PartitionSpec as P

BLOCKS = 256
HALF = 128
SLOTS = 64
ADVECT = 0.2
RAY = 0.03

f32 = jnp.float32
bf16 = jnp.bfloat16
i32 = jnp.int32


def iota(shape, axis):
    return lax.broadcasted_iota(i32, shape, axis)


def take(table, lane):
    index = jnp.broadcast_to(lane, table.shape)
    return jnp.take_along_axis(table, index, axis=1, mode="promise_in_bounds")


def pick(low, high, lane, code, other):
    near = jnp.where(code == 1, take(low, lane), take(high, lane))
    return jnp.where((code == 1) | (code == 2), near, other)


def pick_remote(packed, lane, second):
    return take(packed, lane + second * SLOTS)


def packed_pair(first, second, lane, code):
    ga = jnp.where(code == 2, take(first[1], lane), take(first[0], lane))
    gb = jnp.where(code == 2, take(second[1], lane), take(second[0], lane))
    left = iota((1, HALF), 1) < SLOTS
    return jnp.where(left, ga, gb)


def ends(slab, low, high):
    down = jnp.concatenate([low, slab[:-8]], axis=0)
    up = jnp.concatenate([slab[8:], high], axis=0)
    return down, up


def turns(slab, low, high):
    n = slab.shape[0]
    row = iota((1, 8, 1), 1)
    down = jnp.where(row == 0, low.reshape(n, 1, HALF), pltpu.roll(slab, 1, 1))
    up = jnp.where(row == 7, high.reshape(n, 1, HALF), pltpu.roll(slab, 7, 1))
    return down, up


def zturns(slab, low, high):
    down, up = turns(slab.reshape(8, 8, HALF), low, high)
    return down.reshape(64, HALF), up.reshape(64, HALF)


def face_y(read, j):
    return jnp.concatenate([read(64 * i + 8 * j, 8) for i in range(8)], axis=0)


def odd_on(axis):
    return lax.axis_index(axis) & 1


def slot_of(n, odd):
    return (n + 1 + odd) & 1


def both_sides(first_ref, second_ref, odd):
    first, second = first_ref[...], second_ref[...]
    is_odd = jnp.broadcast_to(odd, first.shape) == 1
    return jnp.where(is_odd, first, second), jnp.where(is_odd, second, first)


def lanes(h):
    return slice(h * HALF, (h + 1) * HALF)


def link_lists(nb, dirs, dev_size):
    count = nb.shape[1]
    me = lax.axis_index("grp") * dev_size + lax.axis_index("dev")
    base = nb - me * count
    present = nb >= 0
    local = present & (base >= 0) & (base < count)
    remote = present & jnp.logical_not(local)
    slot = nb & (count - 1)
    code = jnp.where(local, jnp.where(slot < HALF, 1, 2), jnp.where(remote, 3, 0))
    rem = remote[0:4].astype(f32)
    key = jnp.where(remote[0:4], slot[0:4], 2 * count).astype(f32)
    cols = jnp.concatenate([rem, key], axis=0).T
    tri = (iota((count, count), 1) <= iota((count, count), 0)).astype(bf16)
    upto = jnp.dot(tri, cols.astype(bf16), preferred_element_type=f32)
    target = (iota((1, HALF), 1) & (SLOTS - 1)).astype(f32)
    lists = []
    for f in dirs:
        listed = (upto[:, f : f + 1] <= target).astype(f32)
        lists.append(jnp.sum(listed, axis=0, keepdims=True).astype(i32))
    listing = jnp.concatenate(lists, axis=0)
    clane = listing & (HALF - 1)
    ccode = jnp.where(listing < HALF, 1, jnp.where(listing < count, 2, 0))
    return code, slot, remote, key, cols, clane, ccode


def load_kernel(
    dev_size, v_any, w_any, nb_any, vy_ref, w_ref, nb_ref, send_ref, sems,
):
    copies = [
        pltpu.make_async_copy(nb_any, nb_ref, sems.at[0]),
        pltpu.make_async_copy(v_any.at[1], vy_ref, sems.at[1]),
        pltpu.make_async_copy(w_any, w_ref, sems.at[2]),
    ]
    for c in copies:
        c.start()
    copies[0].wait()
    clane, ccode = link_lists(nb_ref[...], (2, 3), dev_size)[-2:]
    copies[1].wait()
    copies[2].wait()
    for n, j in ((0, 0), (1, 7)):
        send_ref[slot_of(n, odd_on("grp"))] = packed_pair(
            [face_y(lambda r, m: vy_ref[r : r + m, lanes(h)], j) for h in range(2)],
            [face_y(lambda r, m: w_ref[r : r + m, lanes(h)], j) for h in range(2)],
            clane[n : n + 1], ccode[n : n + 1])


def index_kernel(
    dev_size, v_any, dens_any, layer_any, tile_any, block_any, samples_any, nb_ref,
    vxz_ref, dens_ref, idx_ref, cidx_ref, small_ref, samples_ref, sems,
):
    copies = [
        pltpu.make_async_copy(layer_any, small_ref.at[0:1], sems.at[3]),
        pltpu.make_async_copy(tile_any, small_ref.at[1:2], sems.at[4]),
        pltpu.make_async_copy(block_any, small_ref.at[2:3], sems.at[5]),
        pltpu.make_async_copy(samples_any, samples_ref, sems.at[6]),
        pltpu.make_async_copy(v_any.at[0], vxz_ref.at[0], sems.at[0]),
        pltpu.make_async_copy(v_any.at[2], vxz_ref.at[1], sems.at[1]),
        pltpu.make_async_copy(dens_any, dens_ref, sems.at[2]),
    ]
    for c in copies:
        c.start()
    count = nb_ref.shape[1]
    code, slot, remote, key, cols, clane, ccode = link_lists(nb_ref[...], range(4), dev_size)
    lane = slot & (HALF - 1)
    ranks = []
    for f in range(4):
        below = (cols[:, 4 + f : 5 + f] < key[f : f + 1, :]).astype(f32)
        ranks.append(jnp.sum(below, axis=0, keepdims=True).astype(i32))
    rank = jnp.concatenate(ranks, axis=0)
    lane4 = jnp.where(remote[0:4], rank & (SLOTS - 1), lane[0:4])
    zero2 = jnp.zeros((2, count), i32)
    idx_ref[0:8, :] = jnp.concatenate([lane4, lane[4:6], zero2], axis=0)
    idx_ref[8:16, :] = jnp.concatenate([code, zero2], axis=0)
    cidx_ref[...] = jnp.concatenate([clane, ccode], axis=0)
    for c in copies:
        c.wait()


def tile_kernel(cap, reps, small, samples_ref, after_ref, tidx_ref, ids_ref):
    count = small.shape[1]
    tiles = samples_ref.shape[1]
    rows = jnp.concatenate([small[0:1], small[1:2], small[2:3], jnp.zeros((5, count), i32)], axis=0)
    rows = rows.astype(f32)
    cols = rows.T
    tile = cols[:, 1:2]
    hot = tile == iota((count, tiles), 1).astype(f32)
    limit = jnp.sum(jnp.where(hot, samples_ref[...].astype(f32), 0.0), axis=1, keepdims=True)
    marched = cols[:, 0:1] < limit
    hot = hot & marched
    tri = (iota((count, count), 1) <= iota((count, count), 0)).astype(bf16)
    upto = jnp.dot(tri, hot.astype(bf16), preferred_element_type=f32)
    rank = jnp.sum(jnp.where(hot, upto, 0.0), axis=1, keepdims=True) - 1.0
    place = jnp.where(marched, tile * cap + rank, -1.0)
    place = jnp.broadcast_to(place, (count, HALF))
    lane_id = iota((1, HALF), 1)
    used = lane_id < cap * reps
    slot = (lane_id & (cap - 1)).astype(f32)
    listed = jnp.concatenate(
        [(place == jnp.where(used, slot + float(t * cap), -2.0)).astype(bf16)
         for t in range(tiles)], axis=1)
    leaf = iota((1, count), 1).astype(f32)
    table = jnp.concatenate([leaf, rows[2:3], jnp.ones((1, count), f32),
                             jnp.zeros((13, count), f32)], axis=0).astype(bf16)
    found = jnp.dot(table, listed, preferred_element_type=f32)
    for t in range(tiles):
        at = slice(t * HALF, (t + 1) * HALF)
        there = found[2:3, at] > 0.5
        listing = found[0:1, at].astype(i32)
        tidx_ref[t : t + 1, :] = listing & (HALF - 1)
        tidx_ref[tiles + t : tiles + t + 1, :] = jnp.where(
            there, jnp.where(listing < HALF, 1, 2), 0)
        ids_ref[t : t + 1, :] = jnp.where(there, found[1:2, at], -1.0)


def tables(idx_ref):
    lane = [[idx_ref[f : f + 1, lanes(h)] for h in range(2)] for f in range(6)]
    code = [[idx_ref[8 + f : 9 + f, lanes(h)] for h in range(2)] for f in range(6)]
    return lane, code


def edge_kernel(
    vxz_ref, vy_ref, w_ref, first_ref, second_ref, idx_ref, cidx_ref,
    src_ref, dia_ref, send_ref, zs,
):
    lane, code = tables(idx_ref)
    sides = both_sides(first_ref, second_ref, odd_on("grp"))
    for h in range(2):
        for n, start in ((0, 0), (1, 448)):
            rows = slice(start, start + 64)
            zs[0, h, 64 * n : 64 * n + 64] = vxz_ref[1, rows, lanes(h)]
            zs[1, h, 64 * n : 64 * n + 64] = w_ref[rows, lanes(h)]
    for n, start, inner, far_side in ((0, 0, 64, 448), (1, 448, 384, 0)):
        rows = slice(start, start + 64)
        small = slice(start // 8, start // 8 + 8)

        def tabs(read):
            return [read(h) for h in range(2)]

        for h in range(2):
            def face(f, v_tab, w_tab, w_own):
                ln, cd = lane[f][h], code[f][h]
                v_far, w_far = 0.0, jnp.where(cd == 3, 0.0, w_own)
                if f in (2, 3):
                    got = sides[f - 2][small]
                    v_far = jnp.where(cd == 3, pick_remote(got, ln, 0), 0.0)
                    w_far = jnp.where(cd == 3, pick_remote(got, ln, 1), w_own)
                return (pick(v_tab[0], v_tab[1], ln, cd, v_far),
                        pick(w_tab[0], w_tab[1], ln, cd, w_far))

            w = w_ref[rows, lanes(h)]
            far = slice(far_side, far_side + 64)
            next_rows = slice(inner, inner + 64)
            vx, wx = face(n, tabs(lambda g: vxz_ref[0, far, lanes(g)]),
                          tabs(lambda g: w_ref[far, lanes(g)]), w)
            sign = 1.0 if n == 0 else -1.0
            src = sign * (vxz_ref[0, next_rows, lanes(h)] - vx)
            dia = wx + w_ref[next_rows, lanes(h)]
            faces = []
            for f, j in ((2, 7), (3, 0)):
                at = slice(start + 8 * j, start + 8 * j + 8)
                mine = start + 56 - 8 * j
                faces.append(face(f, tabs(lambda g: vy_ref[ at, lanes(g)]),
                                  tabs(lambda g: w_ref[at, lanes(g)]),
                                  w_ref[mine : mine + 8, lanes(h)]))
            v_dn, v_up = ends(vy_ref[ rows, lanes(h)], faces[0][0], faces[1][0])
            w_dn, w_up = ends(w, faces[0][1], faces[1][1])
            src = src + (v_up - v_dn)
            dia = dia + (w_up + w_dn)
            faces = []
            for f, k in ((4, 7), (5, 0)):
                faces.append(face(f, tabs(lambda g: zs[0, g, pl.ds(64 * n + k, 8, stride=8), :]),
                                  tabs(lambda g: zs[1, g, pl.ds(64 * n + k, 8, stride=8), :]),
                                  zs[1, h, pl.ds(64 * n + 7 - k, 8, stride=8), :]))
            v_dn, v_up = zturns(vxz_ref[1, rows, lanes(h)], faces[0][0], faces[1][0])
            w_dn, w_up = zturns(w, faces[0][1], faces[1][1])
            src_ref[n, h] = -0.5 * (src + (v_up - v_dn))
            dia_ref[n, h] = 3.0 * w + 0.5 * (dia + (w_up + w_dn))
        cl, cc = cidx_ref[n : n + 1, :], cidx_ref[4 + n : 5 + n, :]
        slot = slot_of(n, odd_on("dev"))
        send_ref[slot, 0] = packed_pair(
            [vxz_ref[0, rows, lanes(h)] for h in range(2)],
            [w_ref[rows, lanes(h)] for h in range(2)], cl, cc)
        send_ref[slot, 1] = packed_pair(
            [src_ref[n, h] for h in range(2)], [dia_ref[n, h] for h in range(2)], cl, cc)


def inner_kernel(
    vxz_ref, vy_ref, w_ref, dens_ref, first_ref, second_ref, idx_ref, cidx_ref,
    psrc_ref, pdia_ref, aux_ref, xface_ref, zs, vface, face,
):
    lane, code = tables(idx_ref)
    sides = both_sides(first_ref, second_ref, odd_on("grp"))
    for h in range(2):
        zs[0, h] = vxz_ref[1, :, lanes(h)]
        zs[1, h] = w_ref[:, lanes(h)]
    v_tab, w_tab, w_own = {}, {}, {}
    for h in range(2):
        for f, start in ((0, 448), (1, 0)):
            w_tab[f, h] = w_ref[start : start + 64, lanes(h)]
            w_own[1 - f, h] = w_tab[f, h]
        for f, j in ((2, 7), (3, 0)):
            v_tab[f, h] = face_y(lambda r, n: vy_ref[ r : r + n, lanes(h)], j)
            w_tab[f, h] = face_y(lambda r, n: w_ref[r : r + n, lanes(h)], j)
            w_own[5 - f, h] = w_tab[f, h]
        for f, k in ((4, 7), (5, 0)):
            v_tab[f, h] = zs[0, h, pl.ds(k, 64, stride=8), :]
            w_tab[f, h] = zs[1, h, pl.ds(k, 64, stride=8), :]
            w_own[9 - f, h] = w_tab[f, h]
    for f in range(6):
        for h in range(2):
            ln, cd = lane[f][h], code[f][h]
            w_far = jnp.where(cd == 3, 0.0, w_own[f, h])
            v_far = 0.0
            if f in (2, 3):
                got = sides[f - 2]
                v_far = jnp.where(cd == 3, pick_remote(got, ln, 0), 0.0)
                w_far = jnp.where(cd == 3, pick_remote(got, ln, 1), w_own[f, h])
            w_face = pick(w_tab[f, 0], w_tab[f, 1], ln, cd, w_far)
            if f < 2:
                xface_ref[f, h] = w_face
            else:
                face[f - 2, h] = w_face
                vface[f - 2, h] = pick(v_tab[f, 0], v_tab[f, 1], ln, cd, v_far)
    for h in range(2):
        for i in range(8):
            rows = slice(64 * i, 64 * i + 64)
            small = slice(8 * i, 8 * i + 8)
            w = w_ref[rows, lanes(h)]
            wy_dn, wy_up = ends(w, face[0, h, small], face[1, h, small])
            wz_dn, wz_up = zturns(w, face[2, h, small], face[3, h, small])
            aux_ref[1, h, rows] = w + wy_dn
            aux_ref[2, h, rows] = w + wy_up
            aux_ref[3, h, rows] = w + wz_dn
            aux_ref[4, h, rows] = w + wz_up
            aux_ref[5, h, rows] = 0.5 * dens_ref[rows, lanes(h)] * w
            if i < 7:
                aux_ref[0, h, rows] = w + w_ref[64 * i + 64 : 64 * i + 128, lanes(h)]
            if i in (0, 7):
                continue
            below, above = slice(64 * i - 64, 64 * i), slice(64 * i + 64, 64 * i + 128)
            vy_dn, vy_up = ends(vy_ref[ rows, lanes(h)], vface[0, h, small], vface[1, h, small])
            vz_dn, vz_up = zturns(vxz_ref[1, rows, lanes(h)], vface[2, h, small], vface[3, h, small])
            vx = vxz_ref[0, above, lanes(h)] - vxz_ref[0, below, lanes(h)]
            psrc_ref[h, rows] = -0.5 * (vx + (vy_up - vy_dn) + (vz_up - vz_dn))
            wx = w_ref[above, lanes(h)] + w_ref[below, lanes(h)]
            pdia_ref[h, rows] = 3.0 * w + 0.5 * (wx + (wy_up + wy_dn) + (wz_up + wz_dn))


def z_faces(q_ref, lane, code, zface, layers=()):
    for i in layers:
        for f, k in ((4, 7), (5, 0)):
            tabs = [q_ref[h, pl.ds(64 * i + k, 8, stride=8), :] for h in range(2)]
            for h in range(2):
                zface[f - 4, h, 8 * i : 8 * i + 8] = pick(
                    tabs[0], tabs[1], lane[f][h], code[f][h], 0.0)
    if layers:
        return
    for f, k in ((4, 7), (5, 0)):
        tabs = [q_ref[h, pl.ds(k, 64, stride=8), :] for h in range(2)]
        for h in range(2):
            zface[f - 4, h] = pick(tabs[0], tabs[1], lane[f][h], code[f][h], 0.0)


def x_terms(q_ref, aux_ref, xsum_ref, xface, h, i):
    if i == 0:
        dn, c_dn = xface[0, h], xsum_ref[0, h]
    else:
        below = slice(64 * i - 64, 64 * i)
        dn, c_dn = q_ref[h, below], aux_ref[0, h, below]
    if i == 7:
        up, c_up = xface[1, h], xsum_ref[1, h]
    else:
        up, c_up = q_ref[h, 64 * i + 64 : 64 * i + 128], aux_ref[0, h, 64 * i : 64 * i + 64]
    return dn, up, c_dn * dn + c_up * up


def products(q_ref, aux_ref, xsum_ref, rdia_ref, xface, yface, zface, out_ref, layers=range(8)):
    for h in range(2):
        for i in layers:
            rows = slice(64 * i, 64 * i + 64)
            small = slice(8 * i, 8 * i + 8)
            q = q_ref[h, rows]
            total = x_terms(q_ref, aux_ref, xsum_ref, xface, h, i)[2]
            dn, up = ends(q, yface[0, h, small], yface[1, h, small])
            total = total + (aux_ref[1, h, rows] * dn + aux_ref[2, h, rows] * up)
            dn, up = zturns(q, zface[0, h, small], zface[1, h, small])
            total = total + (aux_ref[3, h, rows] * dn + aux_ref[4, h, rows] * up)
            out_ref[h, rows] = (0.5 * rdia_ref[h, rows]) * total


def first_kernel(
    vxz_ref, w_ref, psrc_ref, pdia_ref, esrc_ref, edia_ref, aux_ref, xface_ref,
    first_ref, second_ref, idx_ref, cidx_ref, after_ref,
    dia_ref, z0_ref, rdia_ref, xsum_ref, xq_ref, xhr_ref, send_ref,
):
    lane, code = tables(idx_ref)
    sides = both_sides(first_ref, second_ref, odd_on("dev"))
    for h in range(2):
        for i in range(1, 7):
            rows = slice(64 * i, 64 * i + 64)
            rdia = 1.0 / dia_ref[h, rows]
            rdia_ref[h, rows] = rdia
            z0_ref[h, rows] = psrc_ref[h, rows] * rdia
        for f, start, sign in ((0, 0, 0.5), (1, 448, -0.5)):
            rows = slice(start, start + 64)
            got = sides[f]
            ln, cd = lane[f][h], code[f][h]
            far = cd == 3
            v_m = jnp.where(far, pick_remote(got[0], ln, 0), 0.0)
            w_m = jnp.where(far, pick_remote(got[0], ln, 1), 0.0)
            src_m = jnp.where(far, pick_remote(got[1], ln, 0), 0.0)
            dia_m = jnp.where(far, pick_remote(got[1], ln, 1), 1.0)
            w = w_ref[rows, lanes(h)]
            dia = edia_ref[f, h] + 0.5 * w_m
            rdia = 1.0 / dia
            dia_ref[h, rows] = dia
            rdia_ref[h, rows] = rdia
            z0_ref[h, rows] = (esrc_ref[f, h] + sign * v_m) * rdia
            rdia_m = 1.0 / (dia_m + 0.5 * w)
            z0_m = (src_m - sign * vxz_ref[0, rows, lanes(h)]) * rdia_m
            xhr_ref[f, h] = rdia_m
            xq_ref[f, h] = jnp.where(far, z0_m, 0.0)
            xsum_ref[f, h] = w + jnp.where(far, w_m, xface_ref[f, h])
    for f, start in ((0, 448), (1, 0)):
        tabs = [z0_ref[h, start : start + 64] for h in range(2)]
        for h in range(2):
            xq_ref[f, h] = pick(tabs[0], tabs[1], lane[f][h], code[f][h], xq_ref[f, h])
    z1f = {}
    for n, f, j, there, inner in ((0, 2, 0, 7, 1), (1, 3, 7, 0, 6)):
        tabs = [face_y(lambda r, m: z0_ref[h, r : r + m], there) for h in range(2)]
        at = slice(8 * j, 8 * j + 8)
        for h in range(2):
            q = face_y(lambda r, m: z0_ref[h, r : r + m], j)
            c = face_y(lambda r, m: aux_ref[0, h, r : r + m], j)[:56]
            c_dn = jnp.concatenate([xsum_ref[0, h, at], c], axis=0)
            c_up = jnp.concatenate([c, xsum_ref[1, h, at]], axis=0)
            dn, up = ends(q, xq_ref[0, h, at], xq_ref[1, h, at])
            total = c_dn * dn + c_up * up
            near = pick(tabs[0], tabs[1], lane[f][h], code[f][h], 0.0)
            next_q = face_y(lambda r, m: z0_ref[h, r : r + m], inner)
            c_near = face_y(lambda r, m: aux_ref[1 + n, h, r : r + m], j)
            c_next = face_y(lambda r, m: aux_ref[2 - n, h, r : r + m], j)
            total = total + (c_near * near + c_next * next_q)
            zf = []
            for g, k in ((4, 7), (5, 0)):
                rows = [z0_ref[e, pl.ds(8 * j + k, 8, stride=64), :] for e in range(2)]
                zf.append(pick(rows[0], rows[1], lane[g][h], code[g][h], 0.0))
            dn, up = zturns(q, zf[0], zf[1])
            c_dn = face_y(lambda r, m: aux_ref[3, h, r : r + m], j)
            c_up = face_y(lambda r, m: aux_ref[4, h, r : r + m], j)
            total = total + (c_dn * dn + c_up * up)
            z1f[n, h] = (0.5 * face_y(lambda r, m: rdia_ref[h, r : r + m], j)) * total
    for n, j in ((0, 0), (1, 7)):
        cl, cc = cidx_ref[2 + n : 3 + n, :], cidx_ref[6 + n : 7 + n, :]
        z0f = [face_y(lambda r, m: z0_ref[h, r : r + m], j) for h in range(2)]
        rdf = [face_y(lambda r, m: rdia_ref[h, r : r + m], j) for h in range(2)]
        slot = slot_of(n, odd_on("grp"))
        send_ref[slot, 0] = packed_pair(z0f, [z1f[n, 0], z1f[n, 1]], cl, cc)
        send_ref[slot, 1] = jnp.where(cc == 2, take(rdf[1], cl), take(rdf[0], cl))


def first_rest_kernel(
    z0_ref, aux_ref, xsum_ref, rdia_ref, xq_ref, idx_ref, pz1_ref, yface, zface,
):
    lane, code = tables(idx_ref)
    for f, j in ((2, 7), (3, 0)):
        tabs = [face_y(lambda r, n: z0_ref[h, r : r + n], j) for h in range(2)]
        for h in range(2):
            yface[f - 2, h] = pick(tabs[0], tabs[1], lane[f][h], code[f][h], 0.0)
    z_faces(z0_ref, lane, code, zface)
    products(z0_ref, aux_ref, xsum_ref, rdia_ref, xq_ref, yface, zface, pz1_ref)


def second_kernel(
    vxz_ref, dens_ref, z0_ref, pz1_ref, rdia_ref, aux_ref, xsum_ref,
    first_ref, second_ref, idx_ref, cidx_ref,
    z1_ref, yq0_ref, yq1_ref, send_ref, pz2_ref, xface, zface,
):
    lane, code = tables(idx_ref)
    sides = both_sides(first_ref, second_ref, odd_on("grp"))
    for h in range(2):
        for f, j in ((2, 0), (3, 7)):
            got = sides[f - 2]
            ln, cd = lane[f][h], code[f][h]
            far = cd == 3
            z0_m = jnp.where(far, pick_remote(got[0], ln, 0), 0.0)
            z1_m = pick_remote(got[0], ln, 1)
            rd_m = pick_remote(got[1], ln, 0)
            yq0_ref[f - 2, h] = z0_m
            w_sum = 0.5 * face_y(lambda r, n: aux_ref[f - 1, h, r : r + n], j)
            z0_l = face_y(lambda r, n: z0_ref[h, r : r + n], j)
            rd_l = face_y(lambda r, n: rdia_ref[h, r : r + n], j)
            yq1_ref[f - 2, h] = jnp.where(far, z1_m + rd_m * w_sum * z0_l, 0.0)
            extra = rd_l * w_sum * z0_m
            for i in range(8):
                rows = slice(64 * i + 8 * j, 64 * i + 8 * j + 8)
                z1_ref[h, rows] = z1_ref[h, rows] + extra[8 * i : 8 * i + 8]
    for f, start in ((0, 448), (1, 0)):
        tabs = [z1_ref[h, start : start + 64] for h in range(2)]
        for h in range(2):
            xface[f, h] = pick(tabs[0], tabs[1], lane[f][h], code[f][h], 0.0)
    for f, j in ((2, 7), (3, 0)):
        for q_ref, out in ((z0_ref, yq0_ref), (z1_ref, yq1_ref)):
            tabs = [face_y(lambda r, n: q_ref[h, r : r + n], j) for h in range(2)]
            for h in range(2):
                out[f - 2, h] = pick(tabs[0], tabs[1], lane[f][h], code[f][h], out[f - 2, h])
    layers = (0, 1, 6, 7)
    z_faces(z1_ref, lane, code, zface, layers)
    products(z1_ref, aux_ref, xsum_ref, rdia_ref, xface, yq1_ref, zface, pz2_ref, layers)
    for n, start, inner in ((0, 0, 64), (1, 448, 384)):
        cl, cc = cidx_ref[n : n + 1, :], cidx_ref[4 + n : 5 + n, :]
        rows, next_rows = slice(start, start + 64), slice(inner, inner + 64)
        z1f = [z1_ref[h, rows] for h in range(2)]
        z2f = [pz2_ref[h, rows] for h in range(2)]
        kf, sums = [], []
        for h in range(2):
            k = aux_ref[5, h, rows]
            parts = [k * q[h, next_rows] for q in (z0_ref, z1_ref, pz2_ref)]
            parts.append(dens_ref[rows, lanes(h)] * vxz_ref[0, rows, lanes(h)])
            summed = [over_j(p) for p in parts]
            kf.append(k)
            sums.append(jnp.concatenate(summed + [jnp.zeros((32, HALF), f32)], axis=0))
        slot = slot_of(n, odd_on("dev"))
        send_ref[slot, 0] = packed_pair(z1f, z2f, cl, cc)
        send_ref[slot, 1] = packed_pair(kf, sums, cl, cc)


def second_rest_kernel(
    z1_ref, aux_ref, xsum_ref, rdia_ref, yq1_ref, idx_ref, pz2_ref, xface, zface,
):
    lane, code = tables(idx_ref)
    for f, start in ((0, 448), (1, 0)):
        tabs = [z1_ref[h, start : start + 64] for h in range(2)]
        for h in range(2):
            xface[f, h] = pick(tabs[0], tabs[1], lane[f][h], code[f][h], 0.0)
    z_faces(z1_ref, lane, code, zface)
    products(z1_ref, aux_ref, xsum_ref, rdia_ref, xface, yq1_ref, zface, pz2_ref)


def third_kernel(
    vy_ref, dens_ref, z0_ref, z1_ref, pz2_ref, rdia_ref, aux_ref, xsum_ref, xhr_ref,
    first_ref, second_ref, idx_ref, cidx_ref, after_ref,
    z2_ref, xq1_ref, xq2_ref, xcol_ref, send_ref,
):
    lane, code = tables(idx_ref)
    sides = both_sides(first_ref, second_ref, odd_on("dev"))
    for h in range(2):
        for f, start in ((0, 0), (1, 448)):
            rows = slice(start, start + 64)
            got = sides[f]
            ln, cd = lane[f][h], code[f][h]
            far = cd == 3
            z1_m = jnp.where(far, pick_remote(got[0], ln, 0), 0.0)
            z2_m = pick_remote(got[0], ln, 1)
            k_m = pick_remote(got[1], ln, 0)
            sums = pick_remote(got[1, 0:32], ln, 1)
            w_sum = 0.5 * xsum_ref[f, h]
            xq1_ref[f, h] = z1_m
            xq2_ref[f, h] = jnp.where(far, z2_m + xhr_ref[f, h] * w_sum * z1_ref[h, rows], 0.0)
            z2_l = z2_ref[h, rows] + rdia_ref[h, rows] * w_sum * z1_m
            z2_ref[h, rows] = z2_l
            sign = 1.0 if f == 0 else -1.0
            for c, q in enumerate((z0_ref[h, rows], z1_ref[h, rows], z2_l)):
                mine = over_j(k_m * q)
                xcol_ref[f, h, 8 * c + 8 : 8 * c + 16] = sign * (sums[8 * c : 8 * c + 8] - mine)
            xcol_ref[f, h, 0:8] = sums[24:32]
    for f, start in ((0, 448), (1, 0)):
        for q_ref, out in ((z1_ref, xq1_ref), (z2_ref, xq2_ref)):
            tabs = [q_ref[h, start : start + 64] for h in range(2)]
            for h in range(2):
                out[f, h] = pick(tabs[0], tabs[1], lane[f][h], code[f][h], out[f, h])
    for n, j, inner in ((0, 0, 1), (1, 7, 6)):
        cl, cc = cidx_ref[2 + n : 3 + n, :], cidx_ref[6 + n : 7 + n, :]
        kf, vf = [], []
        for h in range(2):
            dens = face_y(lambda r, m: dens_ref[r : r + m, lanes(h)], j)
            kf.append(face_y(lambda r, m: aux_ref[5, h, r : r + m], j))
            vf.append(dens * face_y(lambda r, m: vy_ref[ r : r + m, lanes(h)], j))
        z2f = [face_y(lambda r, m: z2_ref[h, r : r + m], j) for h in range(2)]
        inners = [
            [kf[h] * face_y(lambda r, m: q[h, r : r + m], inner) for h in range(2)]
            for q in (z0_ref, z1_ref, z2_ref)
        ]
        slot = slot_of(n, odd_on("grp"))
        send_ref[slot, 0] = packed_pair(z2f, kf, cl, cc)
        send_ref[slot, 1] = packed_pair(inners[0], inners[1], cl, cc)
        send_ref[slot, 2] = packed_pair(inners[2], vf, cl, cc)


def over_j(a):
    return jnp.sum(a.reshape(8, 8, HALF), axis=0)


def column_first_kernel(
    vxz_ref, vy_ref, dens_ref, z0_ref, z1_ref, dia_ref, aux_ref, xq0_ref, yq0_ref, yq1_ref, idx_ref,
    col_ref, xs_ref, mom_ref,
    zface, zsum, fy,
):
    lane, code = tables(idx_ref)
    basis = (z0_ref, z1_ref)
    for c in range(2):
        z_faces(basis[c], lane, code, zface.at[c])
    for h in range(2):
        mu = [jnp.zeros((8, HALF), f32) for _ in range(3)]
        for i in range(8):
            rows = slice(64 * i, 64 * i + 64)
            small = slice(8 * i, 8 * i + 8)
            dens = dens_ref[rows, lanes(h)]
            kk = aux_ref[5, h, rows]
            xs_ref[0, h, small] = over_j(dens * vxz_ref[0, rows, lanes(h)])
            zsum[0, h, small] = over_j(dens * vxz_ref[1, rows, lanes(h)])
            col_ref[0, h, small] = over_j(dens)
            q = [basis[c][h, rows] for c in range(2)]
            dn = xq0_ref[0, h] if i == 0 else z0_ref[h, 64 * i - 64 : 64 * i]
            up = xq0_ref[1, h] if i == 7 else z0_ref[h, 64 * i + 64 : 64 * i + 128]
            xs_ref[1, h, small] = over_j(kk * (dn - up))
            for c in range(2):
                zdn, zup = zturns(q[c], zface[c, 0, h, small], zface[c, 1, h, small])
                zsum[c + 1, h, small] = over_j(kk * (zdn - zup))
            dia = dia_ref[h, rows]
            d0, d1 = dia * q[0], dia * q[1]
            mu[0] = mu[0] + over_j(d0 * q[0])
            mu[1] = mu[1] + over_j(d0 * q[1])
            mu[2] = mu[2] + over_j(d1 * q[1])
        for n in range(3):
            mom_ref[h, n] = mu[n]
    scale = RAY * 0.5 * ADVECT
    yq = (yq0_ref, yq1_ref)
    for h in range(2):
        for n, j, inner in ((0, 0, 1), (1, 7, 6)):
            dens = face_y(lambda r, m: dens_ref[r : r + m, lanes(h)], j)
            kk = face_y(lambda r, m: aux_ref[5, h, r : r + m], j)
            fy[n, 0, h] = dens * face_y(lambda r, m: vy_ref[r : r + m, lanes(h)], j)
            for c in range(2):
                near = face_y(lambda r, m: basis[c][h, r : r + m], inner)
                out = yq[c][n, h]
                fy[n, c + 1, h] = kk * ((out - near) if n == 0 else (near - out))
    for c in range(3):
        for h in range(2):
            change = z_change(zsum, c, h, lane, code) + (fy[1, c, h] - fy[0, c, h])
            for n in range(2):
                value = pick(fy[1 - n, c, 0], fy[1 - n, c, 1], lane[2 + n][h], code[2 + n][h], 0.0)
                change = change + value if n == 1 else change - value
            if c == 0:
                col_ref[c, h] = RAY * col_ref[c, h] - scale * change
            else:
                col_ref[c, h] = -scale * change


def z_change(zsum, c, h, lane, code):
    zf = []
    for f, k in ((4, 7), (5, 0)):
        tabs = [zsum[c, g, pl.ds(k, 8, stride=8), :] for g in range(2)]
        zf.append(pick(tabs[0], tabs[1], lane[f][h], code[f][h], 0.0))
    down, up = turns(zsum[c, h].reshape(8, 8, HALF), zf[0], zf[1])
    return (up - down).reshape(64, HALF)


def column_kernel(
    z1_ref, z2_ref, dia_ref, aux_ref, xsum_ref, xq1_ref, xq2_ref, xcol_ref, part_ref, xs_ref, idx_ref,
    col_ref, mom_ref, ynear_ref,
    zface, zsum, xsum,
):
    lane, code = tables(idx_ref)
    for f, j in ((2, 7), (3, 0)):
        tabs = [face_y(lambda r, n: z2_ref[h, r : r + n], j) for h in range(2)]
        for h in range(2):
            ynear_ref[f - 2, h] = pick(tabs[0], tabs[1], lane[f][h], code[f][h], 0.0)
    z_faces(z2_ref, lane, code, zface)
    for h in range(2):
        mu = [jnp.zeros((8, HALF), f32) for _ in range(3)]
        for i in range(8):
            rows = slice(64 * i, 64 * i + 64)
            small = slice(8 * i, 8 * i + 8)
            kk = aux_ref[5, h, rows]
            dn = xq1_ref[0, h] if i == 0 else z1_ref[h, 64 * i - 64 : 64 * i]
            up = xq1_ref[1, h] if i == 7 else z1_ref[h, 64 * i + 64 : 64 * i + 128]
            xsum[0, h, small] = over_j(kk * (dn - up))
            q = z2_ref[h, rows]
            dn, up, total = x_terms(z2_ref, aux_ref, xsum_ref, xq2_ref, h, i)
            xsum[1, h, small] = over_j(kk * (dn - up))
            dn, up = zturns(q, zface[0, h, small], zface[1, h, small])
            zsum[0, h, small] = over_j(kk * (dn - up))
            total = total + (aux_ref[3, h, rows] * dn + aux_ref[4, h, rows] * up)
            dn, up = ends(q, ynear_ref[0, h, small], ynear_ref[1, h, small])
            total = total + (aux_ref[1, h, rows] * dn + aux_ref[2, h, rows] * up)
            d2 = dia_ref[h, rows] * q
            mu[0] = mu[0] + over_j(d2 * z1_ref[h, rows])
            mu[1] = mu[1] + over_j(d2 * q)
            mu[2] = mu[2] + over_j(0.5 * total * q)
        for n in range(3):
            mom_ref[h, n] = mu[n]
    scale = RAY * 0.5 * ADVECT
    for c in range(4):
        for h in range(2):
            sums = [xs_ref[c, g] if c < 2 else xsum[c - 2, g] for g in range(2)]
            faces = []
            for f, start in ((0, 56), (1, 0)):
                far = jnp.where(code[f][h] == 3, xcol_ref[f, h, 8 * c : 8 * c + 8], 0.0)
                faces.append(pick(sums[0][start : start + 8], sums[1][start : start + 8],
                                  lane[f][h], code[f][h], far))
            down, up = ends(sums[h], faces[0], faces[1])
            if c < 3:
                col_ref[c, h] = part_ref[c, h] - scale * (up - down)
            else:
                col_ref[c, h] = -scale * ((up - down) + z_change(zsum, 0, h, lane, code))


def y_kernel(
    tiles, z0_ref, z1_ref, z2_ref, aux_ref,
    col_ref, mom1_ref, mom_ref, ynear_ref, first_ref, second_ref, idx_ref, ids_ref,
    yq2_ref, send_ref, out_ref, fy,
):
    lane, code = tables(idx_ref)
    basis = (z0_ref, z1_ref, z2_ref)
    sides = both_sides(first_ref, second_ref, odd_on("grp"))
    extra = jnp.zeros((64, HALF), f32)
    for h in range(2):
        for n, j, inner in ((0, 0, 1), (1, 7, 6)):
            ln, cd = lane[2 + n][h], code[2 + n][h]
            far = jnp.where(cd == 3, pick_remote(sides[n][0], ln, 0), 0.0)
            out = ynear_ref[n, h] + far
            yq2_ref[n, h] = out
            z2 = face_y(lambda r, m: z2_ref[h, r : r + m], j)
            w_sum = 0.5 * face_y(lambda r, m: aux_ref[1 + n, h, r : r + m], j)
            extra = extra + w_sum * (far * z2)
            kk = face_y(lambda r, m: aux_ref[5, h, r : r + m], j)
            near = face_y(lambda r, m: z2_ref[h, r : r + m], inner)
            fy[n, h] = kk * ((out - near) if n == 0 else (near - out))
    scale = RAY * 0.5 * ADVECT
    for h in range(2):
        change = [None, None, None, fy[1, h] - fy[0, h]]
        for n, j in ((0, 0), (1, 7)):
            got = sides[n]
            ln, cd = lane[2 + n][h], code[2 + n][h]
            far = cd == 3
            k_m = pick_remote(got[0], ln, 1)
            for c in range(4):
                if c == 0:
                    other = pick_remote(got[2], ln, 1)
                else:
                    inner = pick_remote(got[1 + (c - 1) // 2], ln, (c - 1) % 2)
                    mine = k_m * face_y(lambda r, m: basis[c - 1][h, r : r + m], j)
                    other = (mine - inner) if n == 1 else (inner - mine)
                value = jnp.where(far, other, 0.0)
                if c == 3:
                    value = pick(fy[1 - n, 0], fy[1 - n, 1], ln, cd, value)
                value = value if n == 1 else -value
                change[c] = value if change[c] is None else change[c] + value
        for c in range(4):
            out_ref[c, h] = col_ref[c, h] - scale * change[c]
    parts = [m[0, n] + m[1, n] for m in (mom1_ref, mom_ref) for n in range(3)]
    parts[5] = parts[5] + over_j(extra)
    which = iota((1, HALF), 1)
    row = jnp.zeros((1, HALF), f32)
    for n, m in enumerate(parts):
        total = jnp.sum(jnp.sum(m, axis=0, keepdims=True), axis=1, keepdims=True)
        row = jnp.where(which == n, total, row)
    for t in range(tiles):
        names = pltpu.roll(ids_ref[t : t + 1, :], SLOTS, 1)
        line = jnp.where(which < SLOTS, row, names)
        for g in range(send_ref.shape[0] // tiles):
            send_ref[g * tiles + t] = line


def coefficients(mu):
    def dot(a, b):
        total = None
        for i, x in enumerate(a):
            for j, y in enumerate(b):
                if x is None or y is None:
                    continue
                term = x * y * mu[i + j]
                total = term if total is None else total + term
        return total

    one = jnp.ones_like(mu[0])
    residual = [one]
    direction = [one]
    energy = mu[0]
    pressure = [None, None, None]
    for iteration in range(3):
        image = [direction[0]]
        for n in range(1, len(direction)):
            image.append(direction[n] - direction[n - 1])
        image.append(-direction[-1])
        step = energy / dot(direction, image)
        for n, d in enumerate(direction):
            pressure[n] = step * d if pressure[n] is None else pressure[n] + step * d
        if iteration < 2:
            old = residual + [None]
            residual = []
            for n, im in enumerate(image):
                residual.append(-step * im if old[n] is None else old[n] - step * im)
            fresh = dot(residual, residual)
            beta = fresh / energy
            energy = fresh
            longer = direction + [None]
            direction = [
                r if d is None else r + beta * d for r, d in zip(residual, longer)
            ]
    return pressure


def pack_kernel(tiles, cap, fold, got_ref, col_ref, tidx_ref, send_ref, coef_ref):
    sources = got_ref.shape[0]
    total = got_ref[0]
    for s in range(1, sources):
        total = total + got_ref[s]
    coef = coefficients([jnp.broadcast_to(total[:, n : n + 1], (1, HALF)) for n in range(6)])
    coef_ref[...] = jnp.concatenate(coef + [jnp.zeros((5, HALF), f32)], axis=0)
    full = []
    for h in range(2):
        value = col_ref[0, h]
        for n in range(3):
            value = value + coef[n] * col_ref[n + 1, h]
        full.append(value)
    g_count = sources // tiles
    height = 64 // g_count
    left = iota((1, HALF), 1) < cap
    for t in range(tiles):
        ln = tidx_ref[t : t + 1, :]
        cd = tidx_ref[tiles + t : tiles + t + 1, :]
        value = pick(full[0], full[1], ln, cd, 0.0)
        for g in range(g_count):
            part = value[g * height : g * height + height]
            if fold == 2:
                part = jnp.where(left, part[0:8], part[8:16])
            send_ref[g * tiles + t] = part


def final_kernel(
    fold, got_ref, names_ref, coef_ref, vxz_ref, vy_ref, w_ref, z0_ref, z1_ref, z2_ref,
    xq0_ref, xq1_ref, xq2_ref, yq0_ref, yq1_ref, yq2_ref, idx_ref,
    vout_any, image_ref, vout, p, hot, contrib, sems,
):
    coef = [coef_ref[n : n + 1, :] for n in range(3)]
    lane, code = tables(idx_ref)
    for h in range(2):
        for i in range(8):
            rows = slice(64 * i, 64 * i + 64)
            p[h, rows] = (
                coef[0] * z0_ref[h, rows] + coef[1] * z1_ref[h, rows] + coef[2] * z2_ref[h, rows])
    zf = {}
    for f, k in ((4, 7), (5, 0)):
        tabs = [p[h, pl.ds(k, 64, stride=8), :] for h in range(2)]
        for h in range(2):
            zf[f - 4, h] = pick(tabs[0], tabs[1], lane[f][h], code[f][h], 0.0)

    def blend(a_ref, b_ref, c_ref, n, h):
        return coef[0] * a_ref[n, h] + coef[1] * b_ref[n, h] + coef[2] * c_ref[n, h]

    copies = []
    xf = [[blend(xq0_ref, xq1_ref, xq2_ref, n, h) for n in range(2)] for h in range(2)]
    yf = [[blend(yq0_ref, yq1_ref, yq2_ref, n, h) for n in range(2)] for h in range(2)]
    for i in range(8):
        rows = slice(64 * i, 64 * i + 64)
        small = slice(8 * i, 8 * i + 8)
        for h in range(2):
            w = 0.5 * w_ref[rows, lanes(h)]
            mine = p[h, rows]
            dn = xf[h][0] if i == 0 else p[h, 64 * i - 64 : 64 * i]
            up = xf[h][1] if i == 7 else p[h, 64 * i + 64 : 64 * i + 128]
            vout[0, rows, lanes(h)] = vxz_ref[0, rows, lanes(h)] - w * (up - dn)
            dn, up = ends(mine, yf[h][0][small], yf[h][1][small])
            vout[1, rows, lanes(h)] = vy_ref[rows, lanes(h)] - w * (up - dn)
            dn, up = zturns(mine, zf[0, h][small], zf[1, h][small])
            vout[2, rows, lanes(h)] = vxz_ref[1, rows, lanes(h)] - w * (up - dn)
        if i % 2:
            piece = slice(64 * i - 64, 64 * i + 64)
            copies.append(pltpu.make_async_copy(
                vout.at[:, piece], vout_any.at[:, piece], sems.at[i // 2]))
            copies[-1].start()

    sources, height = got_ref.shape[0], 8 * fold
    left = iota((1, HALF), 1) < HALF // 2
    rows_id = iota((BLOCKS, HALF), 0).astype(f32)
    for s in range(0, sources, fold):
        value = got_ref[s]
        after_ids = names_ref[s + 1] if fold == 2 else -1.0
        ids = jnp.where(left, pltpu.roll(names_ref[s], HALF // 2, 1), after_ids)
        if fold == 2:
            after = got_ref[s + 1]
            value = jnp.concatenate(
                [jnp.where(left, value, pltpu.roll(after, HALF // 2, 1)),
                 jnp.where(left, pltpu.roll(value, HALF // 2, 1), after)], axis=0)
        high = value.astype(bf16)
        rest = value - high.astype(f32)
        middle = rest.astype(bf16)
        low = (rest - middle.astype(f32)).astype(bf16)
        cols = slice(s // fold * HALF, (s // fold + 1) * HALF)
        for n, piece in enumerate((high, middle, low)):
            contrib[16 * n : 16 * n + height, cols] = piece
        hot[:, cols] = (rows_id == ids).astype(bf16)
    if height < 16:
        for n in range(3):
            contrib[16 * n + height : 16 * n + 16, :] = jnp.zeros(
                (16 - height, contrib.shape[1]), bf16)
    product = lax.dot_general(
        hot[...], contrib[...], (((1,), (1,)), ((), ())), preferred_element_type=f32).T
    optical = product[0:16] + (product[16:32] + product[32:48])
    shade = 1.0 - jnp.exp(-optical)
    for m in range(height):
        image_ref[0:1, m * BLOCKS : (m + 1) * BLOCKS] = shade[m : m + 1, :]
    for c in copies:
        c.wait()


def call(kernel, outs, scratch, args, any_args=0, limit=10, final=False, alias=None):
    spaces = [pltpu.HBM if n < any_args else pltpu.VMEM for n in range(len(args))]
    out_specs = [pl.BlockSpec(memory_space=pltpu.VMEM) for _ in outs]
    if final:
        out_specs[0] = pl.BlockSpec(memory_space=pltpu.HBM)
    return pl.pallas_call(
        kernel,
        out_shape=[jax.ShapeDtypeStruct(s, d) if final else pltpu.VMEM(s, d) for s, d in outs],
        in_specs=[pl.BlockSpec(memory_space=space) for space in spaces],
        out_specs=out_specs,
        scratch_shapes=scratch,
        input_output_aliases=alias or {},
        compiler_params=pltpu.CompilerParams(vmem_limit_bytes=limit * 1024 * 1024),
    )(*[pltpu.with_memory_space_constraint(a, space) for a, space in zip(args, spaces)])


def swap(packed, axis):
    count = lax.axis_size(axis)
    results = []
    for start in range(2):
        pairs = [(i, i + 1) for i in range(start, count - 1, 2)]
        results.append(lax.ppermute(packed[start], axis, pairs + [(b, a) for a, b in pairs]))
    return results


def shards(
    velocity, density, inverse_density, neighbours, leaf_layer, leaf_tile, leaf_block, samples
):
    count = density.shape[1]
    tiles = samples.shape[0]
    grp_size, dev_size = lax.axis_size("grp"), lax.axis_size("dev")
    cap = 2 * count // tiles
    height = 64 // grp_size
    fold = min(height // 8, HALF // cap)
    sources = grp_size * dev_size
    everyone = ("grp", "dev")

    field = ((2, 512, HALF), f32)
    sides = ((2, 2, 64, HALF), f32)

    def vm(*shape):
        return pltpu.VMEM(shape, f32)

    vy, inv, nb, send = call(
        functools.partial(load_kernel, dev_size),
        [((512, count), f32), ((512, count), f32), ((6, count), i32), ((2, 64, HALF), f32)],
        [pltpu.SemaphoreType.DMA((3,))],
        (velocity, inverse_density, neighbours),
        any_args=3,
    )
    first, second = swap(send, "grp")
    vxz, dens, idx, cidx, small, limits = call(
        functools.partial(index_kernel, dev_size),
        [((2, 512, count), f32), ((512, count), f32), ((16, count), i32), ((8, HALF), i32),
         ((8, count), i32), ((1, tiles), i32)],
        [pltpu.SemaphoreType.DMA((7,))],
        (velocity, density, leaf_layer.reshape(1, count), leaf_tile.reshape(1, count),
         leaf_block.reshape(1, count), samples.reshape(1, tiles), nb),
        any_args=6,
    )
    esrc, edia, send = call(
        edge_kernel,
        [sides, sides, ((2, 2, 64, HALF), f32)],
        [vm(2, 2, HALF, HALF)],
        (vxz, vy, inv, first, second, idx, cidx),
    )
    got_first, got_second = swap(send, "dev")
    psrc, pdia, aux, xface = call(
        inner_kernel,
        [field, field, ((6, 2, 512, HALF), f32), sides],
        [vm(2, 2, 512, HALF), vm(4, 2, 64, HALF), vm(4, 2, 64, HALF)],
        (vxz, vy, inv, dens, first, second, idx, cidx),
    )
    tidx, ids = call(
        functools.partial(tile_kernel, cap, fold),
        [((2 * tiles, HALF), i32), ((tiles, HALF), f32)],
        [],
        (small, limits, esrc),
    )
    dia, z0, rdia, xsum, xq0, xhr, send = call(
        first_kernel,
        [field, field, field, sides, sides, sides, ((2, 2, 64, HALF), f32)],
        [],
        (vxz, inv, psrc, pdia, esrc, edia, aux, xface, got_first, got_second, idx, cidx, ids),
        alias={3: 0},
    )
    first, second = swap(send, "grp")
    (pz1,) = call(
        first_rest_kernel,
        [field],
        [vm(2, 2, 64, HALF), vm(2, 2, 64, HALF)],
        (z0, aux, xsum, rdia, xq0, idx),
    )
    z1, yq0, yq1, send = call(
        second_kernel,
        [field, sides, sides, ((2, 2, 64, HALF), f32)],
        [vm(2, 512, HALF), vm(2, 2, 64, HALF), vm(2, 2, 64, HALF)],
        (vxz, dens, z0, pz1, rdia, aux, xsum, first, second, idx, cidx),
        alias={3: 0},
    )
    first, second = swap(send, "dev")
    (pz2,) = call(
        second_rest_kernel,
        [field],
        [vm(2, 2, 64, HALF), vm(2, 2, 64, HALF)],
        (z1, aux, xsum, rdia, yq1, idx),
    )
    col1, xs, mom1 = call(
        column_first_kernel,
        [((3, 2, 64, HALF), f32), ((2, 2, 64, HALF), f32), ((2, 3, 8, HALF), f32)],
        [vm(2, 2, 2, 64, HALF), vm(3, 2, 64, HALF), vm(2, 3, 2, 64, HALF)],
        (vxz, vy, dens, z0, z1, dia, aux, xq0, yq0, yq1, idx),
    )
    z2, xq1, xq2, xcol, send = call(
        third_kernel,
        [field, sides, sides, ((2, 2, 32, HALF), f32), ((2, 3, 64, HALF), f32)],
        [],
        (vy, dens, z0, z1, pz2, rdia, aux, xsum, xhr, first, second, idx, cidx, mom1),
        alias={4: 0},
    )
    first, second = swap(send, "grp")
    col, mom, ynear = call(
        column_kernel,
        [((4, 2, 64, HALF), f32), ((2, 3, 8, HALF), f32), sides],
        [vm(2, 2, 64, HALF), vm(1, 2, 64, HALF), vm(2, 2, 64, HALF)],
        (z1, z2, dia, aux, xsum, xq1, xq2, xcol, col1, xs, idx),
    )
    yq2, send, col = call(
        functools.partial(y_kernel, tiles),
        [sides, ((sources, 1, HALF), f32), ((4, 2, 64, HALF), f32)],
        [vm(2, 2, 64, HALF)],
        (z0, z1, z2, aux, col, mom1, mom, ynear, first, second, idx, ids),
    )
    moments = lax.all_to_all(send, everyone, 0, 0, tiled=True)
    send, coef = call(
        functools.partial(pack_kernel, tiles, cap, fold),
        [((sources, 8, HALF), f32), ((8, HALF), f32)],
        [],
        (moments, col, tidx),
    )
    got = lax.all_to_all(send, everyone, 0, 0, tiled=True)
    width = sources // fold * HALF
    vout, image = call(
        functools.partial(final_kernel, fold),
        [((3, 512, count), f32), ((1, height * BLOCKS), f32)],
        [vm(3, 512, count), vm(2, 512, HALF), pltpu.VMEM((BLOCKS, width), bf16),
         pltpu.VMEM((48, width), bf16), pltpu.SemaphoreType.DMA((4,))],
        (got, moments, coef, vxz, vy, inv, z0, z1, z2, xq0, xq1, xq2, yq0, yq1, yq2, idx),
        limit=10 + width // 1024,
        final=True,
    )
    return vout, image


def solution(mesh):
    return jax.shard_map(
        shards,
        mesh=mesh,
        in_specs=(
            P(None, None, ("grp", "dev")),
            P(None, ("grp", "dev")),
            P(None, ("grp", "dev")),
            P(None, ("grp", "dev")),
            P(("grp", "dev")),
            P(("grp", "dev"), None),
            P(("grp", "dev")),
            P(),
        ),
        out_specs=(P(None, None, ("grp", "dev")), P("dev", "grp")),
        check_vma=False,
    )
```

time: 642 us -> 63.9 us (0.10)
  blocking collectives: 211 us -> 23 us
  local copies, waits for them, and re-layouts: 155 us -> 0.06 us
  other arithmetic: 93.4 us -> 0 us
  waiting for transfers between devices: 80.5 us -> 1.79 us
  starting transfers between devices: 74.2 us -> 23 us
  between operations: 22.3 us -> 0.87 us
  Pallas kernels: 0 us -> 14.8 us
    psum x5 -> x0, blocking collectives: 211 us -> none  [the longest x3 126 us: energy_sum(): return lax.psum(jnp.sum(residual * precond), ('grp', 'dev'))]
    reduce_scatter x2 -> x0, waiting for transfers between devices: 80.4 us -> none  [the longest x1 62 us: shards(): lax.psum_scatter(full_image.reshape(64, tile_count, BLOCKS), 'dev', scatt...]
    another operation x74 -> x0, local copies, waits for them, and re-layouts: 52.4 us -> none  [the longest x14 11.5 us: face_values(): jnp.stack([second[:, 0].reshape(64, leaf_count), second[:, 7].reshape(64,...]
    ppermute x28 -> x10, starting transfers between devices: 74.1 us -> 23 us  [swap(): lax.ppermute(packed[start], axis, pairs + [(b, a) for a, b in pairs])]
    gather x42 -> x0, local copies, waits for them, and re-layouts: 39.9 us -> none  [face_values(): jnp.take(tables[face_id], lookup[face_id], axis=1)]
    select_n x40 -> x0, other arithmetic: 28.9 us -> none  [the longest x33 25.5 us: face_values(): jnp.where(present[face_id][None, :], jnp.take(tables[face_id], lookup[fac...]
    slice x30 -> x0, local copies, waits for them, and re-layouts: 26.4 us -> none  [the longest x5 5.1 us: shifted(): first[:-1]]
    concatenate x28 -> x0, other arithmetic: 24 us -> none  [the longest x7 6.73 us: face_values(): jnp.concatenate([y_stack[0], y_rim[3]], axis=1)]
  transfers between devices with their start and end apart: 30 -> 10, of which waited for: 2 -> 3; matrix products, arithmetic and copies ran while one was open for 26% -> 0% of each run, Pallas kernels for 0% -> 11%
where the time goes in v1:
time: 63.9 us; the launch traced here: 63.6 us
  starting transfers between devices  23 us (36%)
  blocking collectives  23 us (36%)
  Pallas kernels  14.8 us (23%)
  waiting for transfers between devices  1.79 us (3%)
  between operations  0.87 us (1%)
    ppermute x10, starting transfers between devices, swap(): lax.ppermute(packed[start], axis, pairs + [(b, a) for a, b in pairs])  23 us
    pallas_call x15, Pallas kernels, call(): pl.pallas_call(kernel, out_shape=[jax.ShapeDtypeStruct(s, d) if final els...  14.8 us
    all_to_all x1, blocking collectives, shards(): moments = lax.all_to_all(send, everyone, 0, 0, tiled=True)  13.6 us
    all_to_all x1, blocking collectives, shards(): got = lax.all_to_all(send, everyone, 0, 0, tiled=True)  9.44 us
    ppermute x10, waiting for transfers between devices, swap(): lax.ppermute(packed[start], axis, pairs + [(b, a) for a, b in pairs])  1.79 us
  transfers between devices with their start and end apart: 10, of which 3 were waited for; matrix products, arithmetic and copies ran while one was open for 0% of the time, Pallas kernels for 11%

profile of v1, /device:TPU:0, one launch (start us, length us, event | category | flops | bytes accessed | tf_op | source)
XLA Modules:
  0.0 63.6 jit_solution(10586294119505462950)
XLA Ops:
  0.6 1.4 %shard_map.95 = (f32[512,256]{1,0:T(8,128)S(1)}, f32[512,256]{1,0:T(8,128)S(1)}, s32[6,256]{1,0:T(8,128)S(1)}, f32[2,64,128]{2,1,0:T(8,128)S(1)}) custom-call(f32[3,512,256]{2,1,0:T(8,128)} %v_any.3, f32[512,256]{1,0:T(8,128)} %w_any.1, s32[6,256]{1,0:T(8,128)} %nb_any.1), custom_call_target="tpu_custom_call" | custom-call | tf_op jit(solution)/shard_map/pallas_call | solution.py:900
  2.0 0.7 %collective-permute-start.1 = (f32[64,128]{1,0:T(8,128)S(1)}, f32[64,128]{1,0:T(8,128)S(1)}, u32[]{:S(2)}, u32[]{:S(2)}) collective-permute-start(f32[64,128]{1,0:T(8,128)S(1)} %get-tuple-element.102), channel_id=1, source_target_pairs={{8,16},{16,8},{9,17},{17,9},{10,18},{18,10},{11,19},{19,11},{12,20... | collective-permute-start | bytes 98312 | tf_op jit(solution)/shard_map/ppermute | solution.py:916
  2.7 4.4 %collective-permute-start = (f32[64,128]{1,0:T(8,128)S(1)}, f32[64,128]{1,0:T(8,128)S(1)}, u32[]{:S(2)}, u32[]{:S(2)}) collective-permute-start(f32[64,128]{1,0:T(8,128)S(1)} %get-tuple-element.103), channel_id=1, source_target_pairs={{0,8},{16,24},{8,0},{24,16},{1,9},{17,25},{9,1},{25,17},{2,10},{18... | collective-permute-start | bytes 98312 | tf_op jit(solution)/shard_map/ppermute | solution.py:916
  7.1 1.5 %shard_map.96 = (f32[2,512,256]{2,1,0:T(8,128)S(1)}, f32[512,256]{1,0:T(8,128)S(1)}, s32[16,256]{1,0:T(8,128)S(1)}, s32[8,128]{1,0:T(8,128)S(1)}, s32[8,256]{1,0:T(8,128)S(1)}, /*index=5*/s32[1,8]{1,0:T(1,128)S(1)}) custom-call(f32[3,512,256]{2,1,0:T(8,128)} %v_any.3, f32[512,256]{1,0:T(8,128)} %dens_any.1, s32[1,256]{1,0:T(1,128)} %bitcast.24, ...), custom_call_target="tpu_custom_call" | custom-call | tf_op jit(solution)/shard_map/pallas_call | solution.py:900
  8.6 0.0 collective-permute-done.1.second_ref
  8.6 0.0 collective-permute-done.first_ref
  8.6 0.6 shard_map.98
  9.3 0.7 %collective-permute-start.3 = (f32[2,64,128]{2,1,0:T(8,128)S(1)}, f32[2,64,128]{2,1,0:T(8,128)S(1)}, u32[]{:S(2)}, u32[]{:S(2)}) collective-permute-start(f32[2,64,128]{2,1,0:T(8,128)S(1)} %get-tuple-element.100), channel_id=1, source_target_pairs={{1,2},{3,4},{5,6},{2,1},{4,3},{6,5},{9,10},{11,12},{13,14},{10,9},... | collective-permute-start | bytes 196616 | tf_op jit(solution)/shard_map/ppermute | solution.py:916
  9.9 4.3 %collective-permute-start.2 = (f32[2,64,128]{2,1,0:T(8,128)S(1)}, f32[2,64,128]{2,1,0:T(8,128)S(1)}, u32[]{:S(2)}, u32[]{:S(2)}) collective-permute-start(f32[2,64,128]{2,1,0:T(8,128)S(1)} %get-tuple-element.101), channel_id=1, source_target_pairs={{0,1},{2,3},{4,5},{6,7},{1,0},{3,2},{5,4},{7,6},{8,9},{10,11},{12,... | collective-permute-start | bytes 196616 | tf_op jit(solution)/shard_map/ppermute | solution.py:916
  14.3 1.0 %shard_map.99 = (s32[16,128]{1,0:T(8,128)S(1)}, f32[8,128]{1,0:T(8,128)S(1)}) custom-call(s32[8,256]{1,0:T(8,128)S(1)} %get-tuple-element.63.small, s32[1,8]{1,0:T(1,128)S(1)} %get-tuple-element.64.samples_ref, f32[2,2,64,128]{3,2,1,0:T(8,128)S(1)} %get-tuple-element.58.after_ref.esrc_ref), custom_call_target="tpu_custom_call" | custom-call | tf_op jit(solution)/shard_map/pallas_call | solution.py:900
  15.3 1.1 %shard_map.97 = (f32[2,512,128]{2,1,0:T(8,128)S(1)}, f32[2,512,128]{2,1,0:T(8,128)S(1)}, f32[6,2,512,128]{3,2,1,0:T(8,128)S(1)}, f32[2,2,64,128]{3,2,1,0:T(8,128)S(1)}) custom-call(f32[2,512,256]{2,1,0:T(8,128)S(1)} %get-tuple-element.49.vxz_ref, f32[512,256]{1,0:T(8,128)S(1)} %get-tuple-element.51.vy_ref, f32[512,256]{1,0:T(8,128)S(1)} %get-tuple-element.50.w_ref, ...), custom_call_target="tpu_custom_call" | custom-call | tf_op jit(solution)/shard_map/pallas_call | solution.py:900
  16.3 0.0 collective-permute-done.3.second_ref
  16.3 0.2 collective-permute-done.2.first_ref
  16.5 0.7 %shard_map.100 = (f32[2,512,128]{2,1,0:T(8,128)S(1)}, f32[2,512,128]{2,1,0:T(8,128)S(1)}, f32[2,512,128]{2,1,0:T(8,128)S(1)}, f32[2,2,64,128]{3,2,1,0:T(8,128)S(...) custom-call(f32[2,512,256]{2,1,0:T(8,128)S(1)} %get-tuple-element.49, ...), custom_call_target="tpu_custom_call", output_to_operand_aliasing={{0}: (3, {})} | custom-call | tf_op jit(solution)/shard_map/pallas_call | solution.py:900
  17.3 0.7 %collective-permute-start.5 = (f32[2,64,128]{2,1,0:T(8,128)S(1)}, f32[2,64,128]{2,1,0:T(8,128)S(1)}, u32[]{:S(2)}, u32[]{:S(2)}) collective-permute-start(f32[2,64,128]{2,1,0:T(8,128)S(1)} %get-tuple-element.98), channel_id=1, source_target_pairs={{8,16},{16,8},{9,17},{17,9},{10,18},{18,10},{11,19},{19,11},{12,20... | collective-permute-start | bytes 196616 | tf_op jit(solution)/shard_map/ppermute | solution.py:916
  17.9 3.0 %collective-permute-start.4 = (f32[2,64,128]{2,1,0:T(8,128)S(1)}, f32[2,64,128]{2,1,0:T(8,128)S(1)}, u32[]{:S(2)}, u32[]{:S(2)}) collective-permute-start(f32[2,64,128]{2,1,0:T(8,128)S(1)} %get-tuple-element.99), channel_id=1, source_target_pairs={{0,8},{16,24},{8,0},{24,16},{1,9},{17,25},{9,1},{25,17},{2,10},{18... | collective-permute-start | bytes 196616 | tf_op jit(solution)/shard_map/ppermute | solution.py:916
  21.0 0.6 shard_map.101.pz1_ref
  21.6 0.0 collective-permute-done.5.second_ref
  21.6 0.3 collective-permute-done.4.first_ref
  21.9 0.8 %shard_map.102 = (f32[2,512,128]{2,1,0:T(8,128)S(1)}, f32[2,2,64,128]{3,2,1,0:T(8,128)S(1)}, f32[2,2,64,128]{3,2,1,0:T(8,128)S(1)}, f32[2,2,64,128]{3,2,1,0:T(8,128)S(1)}) custom-call(f32[2,512,256]{2,1,0:T(8,128)S(1)} %get-tuple-element.49.vxz_ref, f32[512,256]{1,0:T(8,128)S(1)} %get-tuple-element.52.dens_ref, ...), custom_call_target="tpu_custom_call", output_to_operand_aliasing={{0}: (3, {})} | custom-call | tf_op jit(solution)/shard_map/pallas_call | solution.py:900
  22.7 0.7 %collective-permute-start.7 = (f32[2,64,128]{2,1,0:T(8,128)S(1)}, f32[2,64,128]{2,1,0:T(8,128)S(1)}, u32[]{:S(2)}, u32[]{:S(2)}) collective-permute-start(f32[2,64,128]{2,1,0:T(8,128)S(1)} %get-tuple-element.96), channel_id=1, source_target_pairs={{1,2},{3,4},{5,6},{2,1},{4,3},{6,5},{9,10},{11,12},{13,14},{10,9},... | collective-permute-start | bytes 196616 | tf_op jit(solution)/shard_map/ppermute | solution.py:916
  23.4 4.8 %collective-permute-start.6 = (f32[2,64,128]{2,1,0:T(8,128)S(1)}, f32[2,64,128]{2,1,0:T(8,128)S(1)}, u32[]{:S(2)}, u32[]{:S(2)}) collective-permute-start(f32[2,64,128]{2,1,0:T(8,128)S(1)} %get-tuple-element.97), channel_id=1, source_target_pairs={{0,1},{2,3},{4,5},{6,7},{1,0},{3,2},{5,4},{7,6},{8,9},{10,11},{12,... | collective-permute-start | bytes 196616 | tf_op jit(solution)/shard_map/ppermute | solution.py:916
  28.2 0.6 %shard_map.103.pz2_ref = f32[2,512,128]{2,1,0:T(8,128)S(1)} custom-call(f32[2,512,128]{2,1,0:T(8,128)S(1)} %get-tuple-element.71.z1_ref, f32[6,2,512,128]{3,2,1,0:T(8,128)S(1)} %get-tuple-element.60.aux_ref, f32[2,2,64,128]{3,2,1,0:T(8,128)S(1)} %get-tuple-element.67.xsum_ref, f32[2,512,128]{2,1,0:T(8,128)S(1)} %get-tuple-element.68.rdia_ref, ...), custom_call_target="tpu_custom_call" | custom-call | tf_op jit(solution)/shard_map/pallas_call | solution.py:900
  28.9 1.2 %shard_map.104 = (f32[3,2,64,128]{3,2,1,0:T(8,128)S(1)}, f32[2,2,64,128]{3,2,1,0:T(8,128)S(1)}, f32[2,3,8,128]{3,2,1,0:T(8,128)S(1)}) custom-call(f32[2,512,256]{2,1,0:T(8,128)S(1)} %get-tuple-element.49.vxz_ref, f32[512,256]{1,0:T(8,128)S(1)} %get-tuple-element.51.vy_ref, f32[512,256]{1,0:T(8,128)S(1)} %get-tuple-element.52.dens_ref, ...), custom_call_target="tpu_custom_call" | custom-call | tf_op jit(solution)/shard_map/pallas_call | solution.py:900
  30.1 0.0 collective-permute-done.7.second_ref
  30.1 1.3 %collective-permute-done.6.first_ref = f32[2,64,128]{2,1,0:T(8,128)S(1)} collective-permute-done((f32[2,64,128]{2,1,0:T(8,128)S(1)}, f32[2,64,128]{2,1,0:T(8,128)S(1)}, u32[]{:S(2)}, u32[]{:S(2)}) %collective-permute-start.6) | collective-permute-done | bytes 65568 | tf_op jit(solution)/shard_map/ppermute | solution.py:916
  31.4 0.6 shard_map.105
  32.1 0.7 %collective-permute-start.9 = (f32[3,64,128]{2,1,0:T(8,128)S(1)}, f32[3,64,128]{2,1,0:T(8,128)S(1)}, u32[]{:S(2)}, u32[]{:S(2)}) collective-permute-start(f32[3,64,128]{2,1,0:T(8,128)S(1)} %get-tuple-element.94), channel_id=1, source_target_pairs={{8,16},{16,8},{9,17},{17,9},{10,18},{18,10},{11,19},{19,11},{12,20... | collective-permute-start | bytes 294920 | tf_op jit(solution)/shard_map/ppermute | solution.py:916
  32.8 3.1 %collective-permute-start.8 = (f32[3,64,128]{2,1,0:T(8,128)S(1)}, f32[3,64,128]{2,1,0:T(8,128)S(1)}, u32[]{:S(2)}, u32[]{:S(2)}) collective-permute-start(f32[3,64,128]{2,1,0:T(8,128)S(1)} %get-tuple-element.95), channel_id=1, source_target_pairs={{0,8},{16,24},{8,0},{24,16},{1,9},{17,25},{9,1},{25,17},{2,10},{18... | collective-permute-start | bytes 294920 | tf_op jit(solution)/shard_map/ppermute | solution.py:916
  35.8 1.0 %shard_map.106 = (f32[4,2,64,128]{3,2,1,0:T(8,128)S(1)}, f32[2,3,8,128]{3,2,1,0:T(8,128)S(1)}, f32[2,2,64,128]{3,2,1,0:T(8,128)S(1)}) custom-call(f32[2,512,128]{2,1,0:T(8,128)S(1)} %get-tuple-element.71.z1_ref, f32[2,512,128]{2,1,0:T(8,128)S(1)} %get-tuple-element.78.z2_ref, f32[2,512,128]{2,1,0:T(8,128)S(1)} %get-tuple-element.75.dia_ref, ...), custom_call_target="tpu_custom_call" | custom-call | tf_op jit(solution)/shard_map/pallas_call | solution.py:900
  36.9 0.0 collective-permute-done.9.second_ref
  36.9 0.0 collective-permute-done.8.first_ref
  36.9 0.5 shard_map.107
  37.4 13.6 %all_to_all.10.got_ref.names_ref = f32[32,1,128]{2,1,0:T(1,128)S(1)} all-to-all(f32[32,1,128]{2,1,0:T(1,128)S(1)} %get-tuple-element.88), channel_id=1, replica_groups=mesh['grp'=4,'dev'=8] {'grp','dev'}, dimensions={0} | all-to-all | bytes 32768 | tf_op jit(solution)/shard_map/all_to_all | solution.py:1028
  51.0 0.4 shard_map.108
  51.4 9.4 %all_to_all.11.got_ref = f32[32,8,128]{2,1,0:T(8,128)S(1)} all-to-all(f32[32,8,128]{2,1,0:T(8,128)S(1)} %get-tuple-element.91), channel_id=1, replica_groups=mesh['grp'=4,'dev'=8] {'grp','dev'}, dimensions={0} | all-to-all | bytes 262144 | tf_op jit(solution)/shard_map/all_to_all | solution.py:1035
  60.8 2.7 %shard_map.109 = (f32[3,512,256]{2,1,0:T(8,128)}, f32[1,4096]{1,0:T(1,128)}) custom-call(f32[32,8,128]{2,1,0:T(8,128)S(1)} %all_to_all.11.got_ref, f32[32,1,128]{2,1,0:T(1,128)S(1)} %all_to_all.10.got_ref.names_ref, f32[8,128]{1,0:T(8,128)S(1)} %get-tuple-element.92.coef_ref, f32[2,512,256]{2,1,0:T(8,128)S(1)} %get-tuple-element.49.vxz_ref, ...), custom_call_target="tpu_custom_call" | custom-call | tf_op jit(solution)/shard_map/pallas_call | solution.py:900
  (5 shorter events, 0.1 us)
Async XLA Ops:
  2.0 6.6 %collective-permute-start.1 = (f32[64,128]{1,0:T(8,128)S(1)}, f32[64,128]{1,0:T(8,128)S(1)}, u32[]{:S(2)}, u32[]{:S(2)}) collective-permute-start(f32[64,128]{1,0:T(8,128)S(1)} %get-tuple-element.102), channel_id=1, source_target_pairs={{8,16},{16,8},{9,17},{17,9},{10,18},{18,10},{11,19},{19,11},{12,20... | collective-permute-start | bytes 98312 | tf_op jit(solution)/shard_map/ppermute | solution.py:916
  2.7 5.9 %collective-permute-start = (f32[64,128]{1,0:T(8,128)S(1)}, f32[64,128]{1,0:T(8,128)S(1)}, u32[]{:S(2)}, u32[]{:S(2)}) collective-permute-start(f32[64,128]{1,0:T(8,128)S(1)} %get-tuple-element.103), channel_id=1, source_target_pairs={{0,8},{16,24},{8,0},{24,16},{1,9},{17,25},{9,1},{25,17},{2,10},{18... | collective-permute-start | bytes 98312 | tf_op jit(solution)/shard_map/ppermute | solution.py:916
  9.3 7.1 %collective-permute-start.3 = (f32[2,64,128]{2,1,0:T(8,128)S(1)}, f32[2,64,128]{2,1,0:T(8,128)S(1)}, u32[]{:S(2)}, u32[]{:S(2)}) collective-permute-start(f32[2,64,128]{2,1,0:T(8,128)S(1)} %get-tuple-element.100), channel_id=1, source_target_pairs={{1,2},{3,4},{5,6},{2,1},{4,3},{6,5},{9,10},{11,12},{13,14},{10,9},... | collective-permute-start | bytes 196616 | tf_op jit(solution)/shard_map/ppermute | solution.py:916
  9.9 6.6 %collective-permute-start.2 = (f32[2,64,128]{2,1,0:T(8,128)S(1)}, f32[2,64,128]{2,1,0:T(8,128)S(1)}, u32[]{:S(2)}, u32[]{:S(2)}) collective-permute-start(f32[2,64,128]{2,1,0:T(8,128)S(1)} %get-tuple-element.101), channel_id=1, source_target_pairs={{0,1},{2,3},{4,5},{6,7},{1,0},{3,2},{5,4},{7,6},{8,9},{10,11},{12,... | collective-permute-start | bytes 196616 | tf_op jit(solution)/shard_map/ppermute | solution.py:916
  17.3 4.3 %collective-permute-start.5 = (f32[2,64,128]{2,1,0:T(8,128)S(1)}, f32[2,64,128]{2,1,0:T(8,128)S(1)}, u32[]{:S(2)}, u32[]{:S(2)}) collective-permute-start(f32[2,64,128]{2,1,0:T(8,128)S(1)} %get-tuple-element.98), channel_id=1, source_target_pairs={{8,16},{16,8},{9,17},{17,9},{10,18},{18,10},{11,19},{19,11},{12,20... | collective-permute-start | bytes 196616 | tf_op jit(solution)/shard_map/ppermute | solution.py:916
  17.9 4.0 %collective-permute-start.4 = (f32[2,64,128]{2,1,0:T(8,128)S(1)}, f32[2,64,128]{2,1,0:T(8,128)S(1)}, u32[]{:S(2)}, u32[]{:S(2)}) collective-permute-start(f32[2,64,128]{2,1,0:T(8,128)S(1)} %get-tuple-element.99), channel_id=1, source_target_pairs={{0,8},{16,24},{8,0},{24,16},{1,9},{17,25},{9,1},{25,17},{2,10},{18... | collective-permute-start | bytes 196616 | tf_op jit(solution)/shard_map/ppermute | solution.py:916
  22.7 7.4 %collective-permute-start.7 = (f32[2,64,128]{2,1,0:T(8,128)S(1)}, f32[2,64,128]{2,1,0:T(8,128)S(1)}, u32[]{:S(2)}, u32[]{:S(2)}) collective-permute-start(f32[2,64,128]{2,1,0:T(8,128)S(1)} %get-tuple-element.96), channel_id=1, source_target_pairs={{1,2},{3,4},{5,6},{2,1},{4,3},{6,5},{9,10},{11,12},{13,14},{10,9},... | collective-permute-start | bytes 196616 | tf_op jit(solution)/shard_map/ppermute | solution.py:916
  23.4 8.0 %collective-permute-start.6 = (f32[2,64,128]{2,1,0:T(8,128)S(1)}, f32[2,64,128]{2,1,0:T(8,128)S(1)}, u32[]{:S(2)}, u32[]{:S(2)}) collective-permute-start(f32[2,64,128]{2,1,0:T(8,128)S(1)} %get-tuple-element.97), channel_id=1, source_target_pairs={{0,1},{2,3},{4,5},{6,7},{1,0},{3,2},{5,4},{7,6},{8,9},{10,11},{12,... | collective-permute-start | bytes 196616 | tf_op jit(solution)/shard_map/ppermute | solution.py:916
  32.1 4.8 %collective-permute-start.9 = (f32[3,64,128]{2,1,0:T(8,128)S(1)}, f32[3,64,128]{2,1,0:T(8,128)S(1)}, u32[]{:S(2)}, u32[]{:S(2)}) collective-permute-start(f32[3,64,128]{2,1,0:T(8,128)S(1)} %get-tuple-element.94), channel_id=1, source_target_pairs={{8,16},{16,8},{9,17},{17,9},{10,18},{18,10},{11,19},{19,11},{12,20... | collective-permute-start | bytes 294920 | tf_op jit(solution)/shard_map/ppermute | solution.py:916
  32.8 4.1 %collective-permute-start.8 = (f32[3,64,128]{2,1,0:T(8,128)S(1)}, f32[3,64,128]{2,1,0:T(8,128)S(1)}, u32[]{:S(2)}, u32[]{:S(2)}) collective-permute-start(f32[3,64,128]{2,1,0:T(8,128)S(1)} %get-tuple-element.95), channel_id=1, source_target_pairs={{0,8},{16,24},{8,0},{24,16},{1,9},{17,25},{9,1},{25,17},{2,10},{18... | collective-permute-start | bytes 294920 | tf_op jit(solution)/shard_map/ppermute | solution.py:916

commit v2 on v1

--- a/solution.py
+++ b/solution.py
@@ -41,6 +41,15 @@
     gb = jnp.where(code == 2, take(second[1], lane), take(second[0], lane))
     left = iota((1, HALF), 1) < SLOTS
     return jnp.where(left, ga, gb)
+
+
+def packed_fold(parts, lane, code):
+    half = parts[0].shape[0] // 2
+    return packed_pair([p[:half] for p in parts], [p[half:] for p in parts], lane, code)
+
+
+def pick_fold(packed, lane):
+    return jnp.concatenate([take(packed, lane), take(packed, lane + SLOTS)], axis=0)
 
 
 def ends(slab, low, high):
@@ -441,8 +450,10 @@
         z0f = [face_y(lambda r, m: z0_ref[h, r : r + m], j) for h in range(2)]
         rdf = [face_y(lambda r, m: rdia_ref[h, r : r + m], j) for h in range(2)]
         slot = slot_of(n, odd_on("grp"))
-        send_ref[slot, 0] = packed_pair(z0f, [z1f[n, 0], z1f[n, 1]], cl, cc)
-        send_ref[slot, 1] = jnp.where(cc == 2, take(rdf[1], cl), take(rdf[0], cl))
+        kf = [face_y(lambda r, m: aux_ref[5, h, r : r + m], j) for h in range(2)]
+        send_ref[slot, 0:64] = packed_pair(z0f, [z1f[n, 0], z1f[n, 1]], cl, cc)
+        send_ref[slot, 64:96] = packed_fold(rdf, cl, cc)
+        send_ref[slot, 96:128] = packed_fold(kf, cl, cc)
 
 
 def first_rest_kernel(
@@ -460,7 +471,7 @@
 def second_kernel(
     vxz_ref, dens_ref, z0_ref, pz1_ref, rdia_ref, aux_ref, xsum_ref,
     first_ref, second_ref, idx_ref, cidx_ref,
-    z1_ref, yq0_ref, yq1_ref, send_ref, pz2_ref, xface, zface,
+    z1_ref, yq0_ref, yq1_ref, ky_ref, send_ref, pz2_ref, xface, zface,
 ):
     lane, code = tables(idx_ref)
     sides = both_sides(first_ref, second_ref, odd_on("grp"))
@@ -469,9 +480,10 @@
             got = sides[f - 2]
             ln, cd = lane[f][h], code[f][h]
             far = cd == 3
-            z0_m = jnp.where(far, pick_remote(got[0], ln, 0), 0.0)
-            z1_m = pick_remote(got[0], ln, 1)
-            rd_m = pick_remote(got[1], ln, 0)
+            z0_m = jnp.where(far, pick_remote(got[0:64], ln, 0), 0.0)
+            z1_m = pick_remote(got[0:64], ln, 1)
+            rd_m = pick_fold(got[64:96], ln)
+            ky_ref[f - 2, h] = pick_fold(got[96:128], ln)
             yq0_ref[f - 2, h] = z0_m
             w_sum = 0.5 * face_y(lambda r, n: aux_ref[f - 1, h, r : r + n], j)
             z0_l = face_y(lambda r, n: z0_ref[h, r : r + n], j)
@@ -505,10 +517,11 @@
             parts.append(dens_ref[rows, lanes(h)] * vxz_ref[0, rows, lanes(h)])
             summed = [over_j(p) for p in parts]
             kf.append(k)
-            sums.append(jnp.concatenate(summed + [jnp.zeros((32, HALF), f32)], axis=0))
+            sums.append(jnp.concatenate(summed, axis=0))
         slot = slot_of(n, odd_on("dev"))
-        send_ref[slot, 0] = packed_pair(z1f, z2f, cl, cc)
-        send_ref[slot, 1] = packed_pair(kf, sums, cl, cc)
+        send_ref[slot, 0:64] = packed_pair(z1f, z2f, cl, cc)
+        send_ref[slot, 64:96] = packed_fold(kf, cl, cc)
+        send_ref[slot, 96:112] = packed_fold(sums, cl, cc)
 
 
 def second_rest_kernel(
@@ -536,10 +549,10 @@
             got = sides[f]
             ln, cd = lane[f][h], code[f][h]
             far = cd == 3
-            z1_m = jnp.where(far, pick_remote(got[0], ln, 0), 0.0)
-            z2_m = pick_remote(got[0], ln, 1)
-            k_m = pick_remote(got[1], ln, 0)
-            sums = pick_remote(got[1, 0:32], ln, 1)
+            z1_m = jnp.where(far, pick_remote(got[0:64], ln, 0), 0.0)
+            z2_m = pick_remote(got[0:64], ln, 1)
+            k_m = pick_fold(got[64:96], ln)
+            sums = pick_fold(got[96:112], ln)
             w_sum = 0.5 * xsum_ref[f, h]
             xq1_ref[f, h] = z1_m
             xq2_ref[f, h] = jnp.where(far, z2_m + xhr_ref[f, h] * w_sum * z1_ref[h, rows], 0.0)
@@ -568,9 +581,9 @@
             for q in (z0_ref, z1_ref, z2_ref)
         ]
         slot = slot_of(n, odd_on("grp"))
-        send_ref[slot, 0] = packed_pair(z2f, kf, cl, cc)
-        send_ref[slot, 1] = packed_pair(inners[0], inners[1], cl, cc)
-        send_ref[slot, 2] = packed_pair(inners[2], vf, cl, cc)
+        send_ref[slot, 0:64] = packed_pair(z2f, inners[2], cl, cc)
+        send_ref[slot, 64:128] = packed_pair(inners[0], inners[1], cl, cc)
+        send_ref[slot, 128:160] = packed_fold(vf, cl, cc)
 
 
 def over_j(a):
@@ -693,7 +706,7 @@
 
 
 def y_kernel(
-    tiles, z0_ref, z1_ref, z2_ref, aux_ref,
+    tiles, z0_ref, z1_ref, z2_ref, aux_ref, ky_ref,
     col_ref, mom1_ref, mom_ref, ynear_ref, first_ref, second_ref, idx_ref, ids_ref,
     yq2_ref, send_ref, out_ref, fy,
 ):
@@ -704,7 +717,7 @@
     for h in range(2):
         for n, j, inner in ((0, 0, 1), (1, 7, 6)):
             ln, cd = lane[2 + n][h], code[2 + n][h]
-            far = jnp.where(cd == 3, pick_remote(sides[n][0], ln, 0), 0.0)
+            far = jnp.where(cd == 3, pick_remote(sides[n][0:64], ln, 0), 0.0)
             out = ynear_ref[n, h] + far
             yq2_ref[n, h] = out
             z2 = face_y(lambda r, m: z2_ref[h, r : r + m], j)
@@ -720,12 +733,13 @@
             got = sides[n]
             ln, cd = lane[2 + n][h], code[2 + n][h]
             far = cd == 3
-            k_m = pick_remote(got[0], ln, 1)
+            k_m = ky_ref[n, h]
             for c in range(4):
                 if c == 0:
-                    other = pick_remote(got[2], ln, 1)
+                    other = pick_fold(got[128:160], ln)
                 else:
-                    inner = pick_remote(got[1 + (c - 1) // 2], ln, (c - 1) % 2)
+                    at, second = ((64, 0), (64, 1), (0, 1))[c - 1]
+                    inner = pick_remote(got[at : at + 64], ln, second)
                     mine = k_m * face_y(lambda r, m: basis[c - 1][h, r : r + m], j)
                     other = (mine - inner) if n == 1 else (inner - mine)
                 value = jnp.where(far, other, 0.0)
@@ -742,11 +756,12 @@
     for n, m in enumerate(parts):
         total = jnp.sum(jnp.sum(m, axis=0, keepdims=True), axis=1, keepdims=True)
         row = jnp.where(which == n, total, row)
+    g_count = send_ref.shape[0] // tiles
     for t in range(tiles):
         names = pltpu.roll(ids_ref[t : t + 1, :], SLOTS, 1)
         line = jnp.where(which < SLOTS, row, names)
-        for g in range(send_ref.shape[0] // tiles):
-            send_ref[g * tiles + t] = line
+        for g in range(g_count):
+            send_ref[t * g_count + g] = line
 
 
 def coefficients(mu):
@@ -812,79 +827,84 @@
             part = value[g * height : g * height + height]
             if fold == 2:
                 part = jnp.where(left, part[0:8], part[8:16])
-            send_ref[g * tiles + t] = part
+            send_ref[t * g_count + g] = part
 
 
 def final_kernel(
     fold, got_ref, names_ref, coef_ref, vxz_ref, vy_ref, w_ref, z0_ref, z1_ref, z2_ref,
     xq0_ref, xq1_ref, xq2_ref, yq0_ref, yq1_ref, yq2_ref, idx_ref,
-    vout_any, image_ref, vout, p, hot, contrib, sems,
+    vout_any, image_ref, vout, p, sems,
 ):
     coef = [coef_ref[n : n + 1, :] for n in range(3)]
     lane, code = tables(idx_ref)
-    for h in range(2):
-        for i in range(8):
-            rows = slice(64 * i, 64 * i + 64)
+
+    def pressure(i):
+        rows = slice(64 * i, 64 * i + 64)
+        for h in range(2):
             p[h, rows] = (
                 coef[0] * z0_ref[h, rows] + coef[1] * z1_ref[h, rows] + coef[2] * z2_ref[h, rows])
-    zf = {}
-    for f, k in ((4, 7), (5, 0)):
-        tabs = [p[h, pl.ds(k, 64, stride=8), :] for h in range(2)]
-        for h in range(2):
-            zf[f - 4, h] = pick(tabs[0], tabs[1], lane[f][h], code[f][h], 0.0)
-
-    def blend(a_ref, b_ref, c_ref, n, h):
-        return coef[0] * a_ref[n, h] + coef[1] * b_ref[n, h] + coef[2] * c_ref[n, h]
-
+
+    def blend(refs, n, h, at):
+        return coef[0] * refs[0][n, h, at] + coef[1] * refs[1][n, h, at] + coef[2] * refs[2][n, h, at]
+
+    sources, height = got_ref.shape[0], 8 * fold
+    left = iota((1, HALF), 1) < HALF // 2
+    blocks_id = iota((BLOCKS, 2 * HALF), 0).astype(f32).astype(bf16)
+    one, zero = jnp.ones((), bf16), jnp.zeros((), bf16)
+
+    def chunk_image(chunk):
+        pieces, names = [], []
+        for s in range(chunk, chunk + 2 * fold, fold):
+            value = got_ref[s]
+            after_ids = names_ref[s + 1] if fold == 2 else -1.0
+            names.append(jnp.where(left, pltpu.roll(names_ref[s], HALF // 2, 1), after_ids))
+            if fold == 2:
+                after = got_ref[s + 1]
+                value = jnp.concatenate(
+                    [jnp.where(left, value, pltpu.roll(after, HALF // 2, 1)),
+                     jnp.where(left, pltpu.roll(value, HALF // 2, 1), after)], axis=0)
+            high = value.astype(bf16)
+            rest = value - high.astype(f32)
+            middle = rest.astype(bf16)
+            low = (rest - middle.astype(f32)).astype(bf16)
+            pieces.append(jnp.concatenate([high, middle, low], axis=0))
+        ids = jnp.broadcast_to(jnp.concatenate(names, axis=1), (16, 2 * HALF)).astype(bf16)
+        ids = jnp.concatenate([ids] * (BLOCKS // 16), axis=0)
+        hot = jnp.where(blocks_id == ids, one, zero)
+        product = lax.dot_general(
+            jnp.concatenate(pieces, axis=1), hot, (((1,), (1,)), ((), ())),
+            preferred_element_type=f32)
+        return product[0:height] + (
+            product[height : 2 * height] + product[2 * height : 3 * height])
+
+    optical = jnp.zeros((height, BLOCKS), f32)
+    chunks = list(range(0, sources, 2 * fold))
+    turn = -(-len(chunks) // 8)
+    xq, yq = (xq0_ref, xq1_ref, xq2_ref), (yq0_ref, yq1_ref, yq2_ref)
     copies = []
-    xf = [[blend(xq0_ref, xq1_ref, xq2_ref, n, h) for n in range(2)] for h in range(2)]
-    yf = [[blend(yq0_ref, yq1_ref, yq2_ref, n, h) for n in range(2)] for h in range(2)]
+    pressure(0)
     for i in range(8):
+        if i < 7:
+            pressure(i + 1)
         rows = slice(64 * i, 64 * i + 64)
         small = slice(8 * i, 8 * i + 8)
+        tabs = [[p[h, pl.ds(64 * i + k, 8, stride=8), :] for h in range(2)] for k in (7, 0)]
         for h in range(2):
             w = 0.5 * w_ref[rows, lanes(h)]
             mine = p[h, rows]
-            dn = xf[h][0] if i == 0 else p[h, 64 * i - 64 : 64 * i]
-            up = xf[h][1] if i == 7 else p[h, 64 * i + 64 : 64 * i + 128]
+            dn = blend(xq, 0, h, slice(0, 64)) if i == 0 else p[h, 64 * i - 64 : 64 * i]
+            up = blend(xq, 1, h, slice(0, 64)) if i == 7 else p[h, 64 * i + 64 : 64 * i + 128]
             vout[0, rows, lanes(h)] = vxz_ref[0, rows, lanes(h)] - w * (up - dn)
-            dn, up = ends(mine, yf[h][0][small], yf[h][1][small])
+            dn, up = ends(mine, blend(yq, 0, h, small), blend(yq, 1, h, small))
             vout[1, rows, lanes(h)] = vy_ref[rows, lanes(h)] - w * (up - dn)
-            dn, up = zturns(mine, zf[0, h][small], zf[1, h][small])
+            zf = [pick(tabs[n][0], tabs[n][1], lane[4 + n][h], code[4 + n][h], 0.0) for n in range(2)]
+            dn, up = zturns(mine, zf[0], zf[1])
             vout[2, rows, lanes(h)] = vxz_ref[1, rows, lanes(h)] - w * (up - dn)
-        if i % 2:
-            piece = slice(64 * i - 64, 64 * i + 64)
-            copies.append(pltpu.make_async_copy(
-                vout.at[:, piece], vout_any.at[:, piece], sems.at[i // 2]))
-            copies[-1].start()
-
-    sources, height = got_ref.shape[0], 8 * fold
-    left = iota((1, HALF), 1) < HALF // 2
-    rows_id = iota((BLOCKS, HALF), 0).astype(f32)
-    for s in range(0, sources, fold):
-        value = got_ref[s]
-        after_ids = names_ref[s + 1] if fold == 2 else -1.0
-        ids = jnp.where(left, pltpu.roll(names_ref[s], HALF // 2, 1), after_ids)
-        if fold == 2:
-            after = got_ref[s + 1]
-            value = jnp.concatenate(
-                [jnp.where(left, value, pltpu.roll(after, HALF // 2, 1)),
-                 jnp.where(left, pltpu.roll(value, HALF // 2, 1), after)], axis=0)
-        high = value.astype(bf16)
-        rest = value - high.astype(f32)
-        middle = rest.astype(bf16)
-        low = (rest - middle.astype(f32)).astype(bf16)
-        cols = slice(s // fold * HALF, (s // fold + 1) * HALF)
-        for n, piece in enumerate((high, middle, low)):
-            contrib[16 * n : 16 * n + height, cols] = piece
-        hot[:, cols] = (rows_id == ids).astype(bf16)
-    if height < 16:
-        for n in range(3):
-            contrib[16 * n + height : 16 * n + 16, :] = jnp.zeros(
-                (16 - height, contrib.shape[1]), bf16)
-    product = lax.dot_general(
-        hot[...], contrib[...], (((1,), (1,)), ((), ())), preferred_element_type=f32).T
-    optical = product[0:16] + (product[16:32] + product[32:48])
+        copies.append(pltpu.make_async_copy(vout.at[:, rows], vout_any.at[:, rows], sems.at[i]))
+        copies[i].start()
+        for chunk in chunks[i * turn : (i + 1) * turn]:
+            optical = optical + chunk_image(chunk)
+
     shade = 1.0 - jnp.exp(-optical)
     for m in range(height):
         image_ref[0:1, m * BLOCKS : (m + 1) * BLOCKS] = shade[m : m + 1, :]
@@ -927,7 +947,7 @@
     height = 64 // grp_size
     fold = min(height // 8, HALF // cap)
     sources = grp_size * dev_size
-    everyone = ("grp", "dev")
+    everyone = ("dev", "grp")
 
     field = ((2, 512, HALF), f32)
     sides = ((2, 2, 64, HALF), f32)
@@ -973,7 +993,7 @@
     )
     dia, z0, rdia, xsum, xq0, xhr, send = call(
         first_kernel,
-        [field, field, field, sides, sides, sides, ((2, 2, 64, HALF), f32)],
+        [field, field, field, sides, sides, sides, ((2, 128, HALF), f32)],
         [],
         (vxz, inv, psrc, pdia, esrc, edia, aux, xface, got_first, got_second, idx, cidx, ids),
         alias={3: 0},
@@ -985,9 +1005,9 @@
         [vm(2, 2, 64, HALF), vm(2, 2, 64, HALF)],
         (z0, aux, xsum, rdia, xq0, idx),
     )
-    z1, yq0, yq1, send = call(
+    z1, yq0, yq1, ky, send = call(
         second_kernel,
-        [field, sides, sides, ((2, 2, 64, HALF), f32)],
+        [field, sides, sides, sides, ((2, 112, HALF), f32)],
         [vm(2, 512, HALF), vm(2, 2, 64, HALF), vm(2, 2, 64, HALF)],
         (vxz, dens, z0, pz1, rdia, aux, xsum, first, second, idx, cidx),
         alias={3: 0},
@@ -1007,7 +1027,7 @@
     )
     z2, xq1, xq2, xcol, send = call(
         third_kernel,
-        [field, sides, sides, ((2, 2, 32, HALF), f32), ((2, 3, 64, HALF), f32)],
+        [field, sides, sides, ((2, 2, 32, HALF), f32), ((2, 160, HALF), f32)],
         [],
         (vy, dens, z0, z1, pz2, rdia, aux, xsum, xhr, first, second, idx, cidx, mom1),
         alias={4: 0},
@@ -1023,7 +1043,7 @@
         functools.partial(y_kernel, tiles),
         [sides, ((sources, 1, HALF), f32), ((4, 2, 64, HALF), f32)],
         [vm(2, 2, 64, HALF)],
-        (z0, z1, z2, aux, col, mom1, mom, ynear, first, second, idx, ids),
+        (z0, z1, z2, aux, ky, col, mom1, mom, ynear, first, second, idx, ids),
     )
     moments = lax.all_to_all(send, everyone, 0, 0, tiled=True)
     send, coef = call(
@@ -1033,14 +1053,11 @@
         (moments, col, tidx),
     )
     got = lax.all_to_all(send, everyone, 0, 0, tiled=True)
-    width = sources // fold * HALF
     vout, image = call(
         functools.partial(final_kernel, fold),
         [((3, 512, count), f32), ((1, height * BLOCKS), f32)],
-        [vm(3, 512, count), vm(2, 512, HALF), pltpu.VMEM((BLOCKS, width), bf16),
-         pltpu.VMEM((48, width), bf16), pltpu.SemaphoreType.DMA((4,))],
+        [vm(3, 512, count), vm(2, 512, HALF), pltpu.SemaphoreType.DMA((8,))],
         (got, moments, coef, vxz, vy, inv, z0, z1, z2, xq0, xq1, xq2, yq0, yq1, yq2, idx),
-        limit=10 + width // 1024,
         final=True,
     )
     return vout, image

time: 63.9 us -> 63.7 us (level)
  no operation moved by 1% of the time
where the time goes in v2:
time: 63.7 us; the launch traced here: 63.3 us
  starting transfers between devices  23.3 us (37%)
  blocking collectives  23.3 us (37%)
  Pallas kernels  14.3 us (22%)
  waiting for transfers between devices  1.43 us (2%)
  between operations  0.87 us (1%)
    ppermute x10, starting transfers between devices, swap(): lax.ppermute(packed[start], axis, pairs + [(b, a) for a, b in pairs])  23.3 us
    pallas_call x15, Pallas kernels, call(): pl.pallas_call(kernel, out_shape=[jax.ShapeDtypeStruct(s, d) if final els...  14.3 us
    all_to_all x1, blocking collectives, shards(): moments = lax.all_to_all(send, everyone, 0, 0, tiled=True)  13.4 us
    all_to_all x1, blocking collectives, shards(): got = lax.all_to_all(send, everyone, 0, 0, tiled=True)  9.93 us
    ppermute x10, waiting for transfers between devices, swap(): lax.ppermute(packed[start], axis, pairs + [(b, a) for a, b in pairs])  1.43 us
  transfers between devices with their start and end apart: 10, of which 3 were waited for; matrix products, arithmetic and copies ran while one was open for 0% of the time, Pallas kernels for 11%

profile of v2, /device:TPU:0, one launch (start us, length us, event | category | flops | bytes accessed | tf_op | source)
XLA Modules:
  0.0 63.3 jit_solution(5746670123826401149)
XLA Ops:
  0.6 1.4 %shard_map.95 = (f32[512,256]{1,0:T(8,128)S(1)}, f32[512,256]{1,0:T(8,128)S(1)}, s32[6,256]{1,0:T(8,128)S(1)}, f32[2,64,128]{2,1,0:T(8,128)S(1)}) custom-call(f32[3,512,256]{2,1,0:T(8,128)} %v_any.3, f32[512,256]{1,0:T(8,128)} %w_any.1, s32[6,256]{1,0:T(8,128)} %nb_any.1), custom_call_target="tpu_custom_call" | custom-call | tf_op jit(solution)/shard_map/pallas_call | solution.py:920
  2.0 0.7 %collective-permute-start.1 = (f32[64,128]{1,0:T(8,128)S(1)}, f32[64,128]{1,0:T(8,128)S(1)}, u32[]{:S(2)}, u32[]{:S(2)}) collective-permute-start(f32[64,128]{1,0:T(8,128)S(1)} %get-tuple-element.104), channel_id=1, source_target_pairs={{8,16},{16,8},{9,17},{17,9},{10,18},{18,10},{11,19},{19,11},{12,20... | collective-permute-start | bytes 98312 | tf_op jit(solution)/shard_map/ppermute | solution.py:936
  2.7 4.4 %collective-permute-start = (f32[64,128]{1,0:T(8,128)S(1)}, f32[64,128]{1,0:T(8,128)S(1)}, u32[]{:S(2)}, u32[]{:S(2)}) collective-permute-start(f32[64,128]{1,0:T(8,128)S(1)} %get-tuple-element.105), channel_id=1, source_target_pairs={{0,8},{16,24},{8,0},{24,16},{1,9},{17,25},{9,1},{25,17},{2,10},{18... | collective-permute-start | bytes 98312 | tf_op jit(solution)/shard_map/ppermute | solution.py:936
  7.1 1.5 %shard_map.96 = (f32[2,512,256]{2,1,0:T(8,128)S(1)}, f32[512,256]{1,0:T(8,128)S(1)}, s32[16,256]{1,0:T(8,128)S(1)}, s32[8,128]{1,0:T(8,128)S(1)}, s32[8,256]{1,0:T(8,128)S(1)}, /*index=5*/s32[1,8]{1,0:T(1,128)S(1)}) custom-call(f32[3,512,256]{2,1,0:T(8,128)} %v_any.3, f32[512,256]{1,0:T(8,128)} %dens_any.1, s32[1,256]{1,0:T(1,128)} %bitcast.24, ...), custom_call_target="tpu_custom_call" | custom-call | tf_op jit(solution)/shard_map/pallas_call | solution.py:920
  8.6 0.0 collective-permute-done.1.second_ref
  8.6 0.0 collective-permute-done.first_ref
  8.6 0.6 shard_map.98
  9.3 0.7 %collective-permute-start.3 = (f32[2,64,128]{2,1,0:T(8,128)S(1)}, f32[2,64,128]{2,1,0:T(8,128)S(1)}, u32[]{:S(2)}, u32[]{:S(2)}) collective-permute-start(f32[2,64,128]{2,1,0:T(8,128)S(1)} %get-tuple-element.100), channel_id=1, source_target_pairs={{1,2},{3,4},{5,6},{2,1},{4,3},{6,5},{9,10},{11,12},{13,14},{10,9},... | collective-permute-start | bytes 196616 | tf_op jit(solution)/shard_map/ppermute | solution.py:936
  9.9 4.3 %collective-permute-start.2 = (f32[2,64,128]{2,1,0:T(8,128)S(1)}, f32[2,64,128]{2,1,0:T(8,128)S(1)}, u32[]{:S(2)}, u32[]{:S(2)}) collective-permute-start(f32[2,64,128]{2,1,0:T(8,128)S(1)} %get-tuple-element.101), channel_id=1, source_target_pairs={{0,1},{2,3},{4,5},{6,7},{1,0},{3,2},{5,4},{7,6},{8,9},{10,11},{12,... | collective-permute-start | bytes 196616 | tf_op jit(solution)/shard_map/ppermute | solution.py:936
  14.3 1.0 %shard_map.99 = (s32[16,128]{1,0:T(8,128)S(1)}, f32[8,128]{1,0:T(8,128)S(1)}) custom-call(s32[8,256]{1,0:T(8,128)S(1)} %get-tuple-element.64.small, s32[1,8]{1,0:T(1,128)S(1)} %get-tuple-element.65.samples_ref, f32[2,2,64,128]{3,2,1,0:T(8,128)S(1)} %get-tuple-element.59.after_ref.esrc_ref), custom_call_target="tpu_custom_call" | custom-call | tf_op jit(solution)/shard_map/pallas_call | solution.py:920
  15.3 1.1 %shard_map.97 = (f32[2,512,128]{2,1,0:T(8,128)S(1)}, f32[2,512,128]{2,1,0:T(8,128)S(1)}, f32[6,2,512,128]{3,2,1,0:T(8,128)S(1)}, f32[2,2,64,128]{3,2,1,0:T(8,128)S(1)}) custom-call(f32[2,512,256]{2,1,0:T(8,128)S(1)} %get-tuple-element.50.vxz_ref, f32[512,256]{1,0:T(8,128)S(1)} %get-tuple-element.52.vy_ref, f32[512,256]{1,0:T(8,128)S(1)} %get-tuple-element.51.w_ref, ...), custom_call_target="tpu_custom_call" | custom-call | tf_op jit(solution)/shard_map/pallas_call | solution.py:920
  16.3 0.0 collective-permute-done.3.second_ref
  16.3 0.2 collective-permute-done.2.first_ref
  16.5 0.7 %shard_map.100 = (f32[2,512,128]{2,1,0:T(8,128)S(1)}, f32[2,512,128]{2,1,0:T(8,128)S(1)}, f32[2,512,128]{2,1,0:T(8,128)S(1)}, f32[2,2,64,128]{3,2,1,0:T(8,128)S(...) custom-call(f32[2,512,256]{2,1,0:T(8,128)S(1)} %get-tuple-element.50, ...), custom_call_target="tpu_custom_call", output_to_operand_aliasing={{0}: (3, {})} | custom-call | tf_op jit(solution)/shard_map/pallas_call | solution.py:920
  17.3 0.7 %collective-permute-start.5 = (f32[128,128]{1,0:T(8,128)S(1)}, f32[128,128]{1,0:T(8,128)S(1)}, u32[]{:S(2)}, u32[]{:S(2)}) collective-permute-start(f32[128,128]{1,0:T(8,128)S(1)} %get-tuple-element.98), channel_id=1, source_target_pairs={{8,16},{16,8},{9,17},{17,9},{10,18},{18,10},{11,19},{19,11},{12,20... | collective-permute-start | bytes 196616 | tf_op jit(solution)/shard_map/ppermute | solution.py:936
  18.0 3.0 %collective-permute-start.4 = (f32[128,128]{1,0:T(8,128)S(1)}, f32[128,128]{1,0:T(8,128)S(1)}, u32[]{:S(2)}, u32[]{:S(2)}) collective-permute-start(f32[128,128]{1,0:T(8,128)S(1)} %get-tuple-element.99), channel_id=1, source_target_pairs={{0,8},{16,24},{8,0},{24,16},{1,9},{17,25},{9,1},{25,17},{2,10},{18... | collective-permute-start | bytes 196616 | tf_op jit(solution)/shard_map/ppermute | solution.py:936
  21.0 0.6 shard_map.101.pz1_ref
  21.6 0.0 collective-permute-done.5.second_ref
  21.6 0.3 collective-permute-done.4.first_ref
  21.9 0.9 %shard_map.102 = (f32[2,512,128]{2,1,0:T(8,128)S(1)}, f32[2,2,64,128]{3,2,1,0:T(8,128)S(1)}, f32[2,2,64,128]{3,2,1,0:T(8,128)S(1)}, f32[2,2,64,128]{3,2,1,0:T(8,128)S(1)}, f32[2,112,128]{2,1,0:T(8,128)S(1)}) custom-call(f32[2,512,256]{2,1,0:T(8,128)S(1)} %get-tuple-element.50.vxz_ref, ...), custom_call_target="tpu_custom_call", output_to_operand_aliasing={{0}: (3, {})} | custom-call | tf_op jit(solution)/shard_map/pallas_call | solution.py:920
  22.8 0.7 %collective-permute-start.7 = (f32[112,128]{1,0:T(8,128)S(1)}, f32[112,128]{1,0:T(8,128)S(1)}, u32[]{:S(2)}, u32[]{:S(2)}) collective-permute-start(f32[112,128]{1,0:T(8,128)S(1)} %get-tuple-element.102), channel_id=1, source_target_pairs={{1,2},{3,4},{5,6},{2,1},{4,3},{6,5},{9,10},{11,12},{13,14},{10,9},... | collective-permute-start | bytes 172040 | tf_op jit(solution)/shard_map/ppermute | solution.py:936
  23.5 4.8 %collective-permute-start.6 = (f32[112,128]{1,0:T(8,128)S(1)}, f32[112,128]{1,0:T(8,128)S(1)}, u32[]{:S(2)}, u32[]{:S(2)}) collective-permute-start(f32[112,128]{1,0:T(8,128)S(1)} %get-tuple-element.103), channel_id=1, source_target_pairs={{0,1},{2,3},{4,5},{6,7},{1,0},{3,2},{5,4},{7,6},{8,9},{10,11},{12,... | collective-permute-start | bytes 172040 | tf_op jit(solution)/shard_map/ppermute | solution.py:936
  28.3 0.6 %shard_map.103.pz2_ref = f32[2,512,128]{2,1,0:T(8,128)S(1)} custom-call(f32[2,512,128]{2,1,0:T(8,128)S(1)} %get-tuple-element.72.z1_ref, f32[6,2,512,128]{3,2,1,0:T(8,128)S(1)} %get-tuple-element.61.aux_ref, f32[2,2,64,128]{3,2,1,0:T(8,128)S(1)} %get-tuple-element.68.xsum_ref, f32[2,512,128]{2,1,0:T(8,128)S(1)} %get-tuple-element.69.rdia_ref, ...), custom_call_target="tpu_custom_call" | custom-call | tf_op jit(solution)/shard_map/pallas_call | solution.py:920
  29.0 1.2 %shard_map.104 = (f32[3,2,64,128]{3,2,1,0:T(8,128)S(1)}, f32[2,2,64,128]{3,2,1,0:T(8,128)S(1)}, f32[2,3,8,128]{3,2,1,0:T(8,128)S(1)}) custom-call(f32[2,512,256]{2,1,0:T(8,128)S(1)} %get-tuple-element.50.vxz_ref, f32[512,256]{1,0:T(8,128)S(1)} %get-tuple-element.52.vy_ref, f32[512,256]{1,0:T(8,128)S(1)} %get-tuple-element.53.dens_ref, ...), custom_call_target="tpu_custom_call" | custom-call | tf_op jit(solution)/shard_map/pallas_call | solution.py:920
  30.2 0.0 collective-permute-done.7.second_ref
  30.2 1.0 %collective-permute-done.6.first_ref = f32[112,128]{1,0:T(8,128)S(1)} collective-permute-done((f32[112,128]{1,0:T(8,128)S(1)}, f32[112,128]{1,0:T(8,128)S(1)}, u32[]{:S(2)}, u32[]{:S(2)}) %collective-permute-start.6) | collective-permute-done | bytes 57376 | tf_op jit(solution)/shard_map/ppermute | solution.py:936
  31.2 0.6 shard_map.105
  31.8 0.7 %collective-permute-start.9 = (f32[160,128]{1,0:T(8,128)S(1)}, f32[160,128]{1,0:T(8,128)S(1)}, u32[]{:S(2)}, u32[]{:S(2)}) collective-permute-start(f32[160,128]{1,0:T(8,128)S(1)} %get-tuple-element.96), channel_id=1, source_target_pairs={{8,16},{16,8},{9,17},{17,9},{10,18},{18,10},{11,19},{19,11},{12,20... | collective-permute-start | bytes 245768 | tf_op jit(solution)/shard_map/ppermute | solution.py:936
  32.5 3.3 %collective-permute-start.8 = (f32[160,128]{1,0:T(8,128)S(1)}, f32[160,128]{1,0:T(8,128)S(1)}, u32[]{:S(2)}, u32[]{:S(2)}) collective-permute-start(f32[160,128]{1,0:T(8,128)S(1)} %get-tuple-element.97), channel_id=1, source_target_pairs={{0,8},{16,24},{8,0},{24,16},{1,9},{17,25},{9,1},{25,17},{2,10},{18... | collective-permute-start | bytes 245768 | tf_op jit(solution)/shard_map/ppermute | solution.py:936
  35.8 1.0 %shard_map.106 = (f32[4,2,64,128]{3,2,1,0:T(8,128)S(1)}, f32[2,3,8,128]{3,2,1,0:T(8,128)S(1)}, f32[2,2,64,128]{3,2,1,0:T(8,128)S(1)}) custom-call(f32[2,512,128]{2,1,0:T(8,128)S(1)} %get-tuple-element.72.z1_ref, f32[2,512,128]{2,1,0:T(8,128)S(1)} %get-tuple-element.79.z2_ref, f32[2,512,128]{2,1,0:T(8,128)S(1)} %get-tuple-element.76.dia_ref, ...), custom_call_target="tpu_custom_call" | custom-call | tf_op jit(solution)/shard_map/pallas_call | solution.py:920
  36.9 0.0 collective-permute-done.9.second_ref
  36.9 0.0 collective-permute-done.8.first_ref
  36.9 0.4 shard_map.107
  37.3 13.4 %all_to_all.10.got_ref.names_ref = f32[32,1,128]{2,1,0:T(1,128)S(1)} all-to-all(f32[32,1,128]{2,1,0:T(1,128)S(1)} %get-tuple-element.90), channel_id=1, replica_groups=mesh['grp'=4,'dev'=8] {'dev','grp'}, dimensions={0} | all-to-all | bytes 32768 | tf_op jit(solution)/shard_map/all_to_all | solution.py:1048
  50.7 0.4 shard_map.108
  51.2 9.9 %all_to_all.11.got_ref = f32[32,8,128]{2,1,0:T(8,128)S(1)} all-to-all(f32[32,8,128]{2,1,0:T(8,128)S(1)} %get-tuple-element.93), channel_id=1, replica_groups=mesh['grp'=4,'dev'=8] {'dev','grp'}, dimensions={0} | all-to-all | bytes 262144 | tf_op jit(solution)/shard_map/all_to_all | solution.py:1055
  61.1 2.2 %shard_map.109 = (f32[3,512,256]{2,1,0:T(8,128)}, f32[1,4096]{1,0:T(1,128)}) custom-call(f32[32,8,128]{2,1,0:T(8,128)S(1)} %all_to_all.11.got_ref, f32[32,1,128]{2,1,0:T(1,128)S(1)} %all_to_all.10.got_ref.names_ref, f32[8,128]{1,0:T(8,128)S(1)} %get-tuple-element.94.coef_ref, f32[2,512,256]{2,1,0:T(8,128)S(1)} %get-tuple-element.50.vxz_ref, ...), custom_call_target="tpu_custom_call" | custom-call | tf_op jit(solution)/shard_map/pallas_call | solution.py:920
  (5 shorter events, 0.1 us)
Async XLA Ops:
  2.0 6.6 %collective-permute-start.1 = (f32[64,128]{1,0:T(8,128)S(1)}, f32[64,128]{1,0:T(8,128)S(1)}, u32[]{:S(2)}, u32[]{:S(2)}) collective-permute-start(f32[64,128]{1,0:T(8,128)S(1)} %get-tuple-element.104), channel_id=1, source_target_pairs={{8,16},{16,8},{9,17},{17,9},{10,18},{18,10},{11,19},{19,11},{12,20... | collective-permute-start | bytes 98312 | tf_op jit(solution)/shard_map/ppermute | solution.py:936
  2.7 5.9 %collective-permute-start = (f32[64,128]{1,0:T(8,128)S(1)}, f32[64,128]{1,0:T(8,128)S(1)}, u32[]{:S(2)}, u32[]{:S(2)}) collective-permute-start(f32[64,128]{1,0:T(8,128)S(1)} %get-tuple-element.105), channel_id=1, source_target_pairs={{0,8},{16,24},{8,0},{24,16},{1,9},{17,25},{9,1},{25,17},{2,10},{18... | collective-permute-start | bytes 98312 | tf_op jit(solution)/shard_map/ppermute | solution.py:936
  9.3 7.1 %collective-permute-start.3 = (f32[2,64,128]{2,1,0:T(8,128)S(1)}, f32[2,64,128]{2,1,0:T(8,128)S(1)}, u32[]{:S(2)}, u32[]{:S(2)}) collective-permute-start(f32[2,64,128]{2,1,0:T(8,128)S(1)} %get-tuple-element.100), channel_id=1, source_target_pairs={{1,2},{3,4},{5,6},{2,1},{4,3},{6,5},{9,10},{11,12},{13,14},{10,9},... | collective-permute-start | bytes 196616 | tf_op jit(solution)/shard_map/ppermute | solution.py:936
  9.9 6.6 %collective-permute-start.2 = (f32[2,64,128]{2,1,0:T(8,128)S(1)}, f32[2,64,128]{2,1,0:T(8,128)S(1)}, u32[]{:S(2)}, u32[]{:S(2)}) collective-permute-start(f32[2,64,128]{2,1,0:T(8,128)S(1)} %get-tuple-element.101), channel_id=1, source_target_pairs={{0,1},{2,3},{4,5},{6,7},{1,0},{3,2},{5,4},{7,6},{8,9},{10,11},{12,... | collective-permute-start | bytes 196616 | tf_op jit(solution)/shard_map/ppermute | solution.py:936
  17.3 4.3 %collective-permute-start.5 = (f32[128,128]{1,0:T(8,128)S(1)}, f32[128,128]{1,0:T(8,128)S(1)}, u32[]{:S(2)}, u32[]{:S(2)}) collective-permute-start(f32[128,128]{1,0:T(8,128)S(1)} %get-tuple-element.98), channel_id=1, source_target_pairs={{8,16},{16,8},{9,17},{17,9},{10,18},{18,10},{11,19},{19,11},{12,20... | collective-permute-start | bytes 196616 | tf_op jit(solution)/shard_map/ppermute | solution.py:936
  18.0 4.0 %collective-permute-start.4 = (f32[128,128]{1,0:T(8,128)S(1)}, f32[128,128]{1,0:T(8,128)S(1)}, u32[]{:S(2)}, u32[]{:S(2)}) collective-permute-start(f32[128,128]{1,0:T(8,128)S(1)} %get-tuple-element.99), channel_id=1, source_target_pairs={{0,8},{16,24},{8,0},{24,16},{1,9},{17,25},{9,1},{25,17},{2,10},{18... | collective-permute-start | bytes 196616 | tf_op jit(solution)/shard_map/ppermute | solution.py:936
  22.8 7.4 %collective-permute-start.7 = (f32[112,128]{1,0:T(8,128)S(1)}, f32[112,128]{1,0:T(8,128)S(1)}, u32[]{:S(2)}, u32[]{:S(2)}) collective-permute-start(f32[112,128]{1,0:T(8,128)S(1)} %get-tuple-element.102), channel_id=1, source_target_pairs={{1,2},{3,4},{5,6},{2,1},{4,3},{6,5},{9,10},{11,12},{13,14},{10,9},... | collective-permute-start | bytes 172040 | tf_op jit(solution)/shard_map/ppermute | solution.py:936
  23.5 7.7 %collective-permute-start.6 = (f32[112,128]{1,0:T(8,128)S(1)}, f32[112,128]{1,0:T(8,128)S(1)}, u32[]{:S(2)}, u32[]{:S(2)}) collective-permute-start(f32[112,128]{1,0:T(8,128)S(1)} %get-tuple-element.103), channel_id=1, source_target_pairs={{0,1},{2,3},{4,5},{6,7},{1,0},{3,2},{5,4},{7,6},{8,9},{10,11},{12,... | collective-permute-start | bytes 172040 | tf_op jit(solution)/shard_map/ppermute | solution.py:936
  31.8 5.1 %collective-permute-start.9 = (f32[160,128]{1,0:T(8,128)S(1)}, f32[160,128]{1,0:T(8,128)S(1)}, u32[]{:S(2)}, u32[]{:S(2)}) collective-permute-start(f32[160,128]{1,0:T(8,128)S(1)} %get-tuple-element.96), channel_id=1, source_target_pairs={{8,16},{16,8},{9,17},{17,9},{10,18},{18,10},{11,19},{19,11},{12,20... | collective-permute-start | bytes 245768 | tf_op jit(solution)/shard_map/ppermute | solution.py:936
  32.5 4.4 %collective-permute-start.8 = (f32[160,128]{1,0:T(8,128)S(1)}, f32[160,128]{1,0:T(8,128)S(1)}, u32[]{:S(2)}, u32[]{:S(2)}) collective-permute-start(f32[160,128]{1,0:T(8,128)S(1)} %get-tuple-element.97), channel_id=1, source_target_pairs={{0,8},{16,24},{8,0},{24,16},{1,9},{17,25},{9,1},{25,17},{2,10},{18... | collective-permute-start | bytes 245768 | tf_op jit(solution)/shard_map/ppermute | solution.py:936

commit v3 on v2

--- a/solution.py
+++ b/solution.py
@@ -764,16 +764,16 @@
             send_ref[t * g_count + g] = line
 
 
+def pairwise(terms):
+    while len(terms) > 1:
+        odd = terms[len(terms) // 2 * 2 :]
+        terms = [a + b for a, b in zip(terms[0::2], terms[1::2])] + odd
+    return terms[0]
+
+
 def coefficients(mu):
     def dot(a, b):
-        total = None
-        for i, x in enumerate(a):
-            for j, y in enumerate(b):
-                if x is None or y is None:
-                    continue
-                term = x * y * mu[i + j]
-                total = term if total is None else total + term
-        return total
+        return pairwise([x * y * mu[i + j] for i, x in enumerate(a) for j, y in enumerate(b)])
 
     one = jnp.ones_like(mu[0])
     residual = [one]
@@ -805,9 +805,7 @@
 
 def pack_kernel(tiles, cap, fold, got_ref, col_ref, tidx_ref, send_ref, coef_ref):
     sources = got_ref.shape[0]
-    total = got_ref[0]
-    for s in range(1, sources):
-        total = total + got_ref[s]
+    total = pairwise([got_ref[s] for s in range(sources)])
     coef = coefficients([jnp.broadcast_to(total[:, n : n + 1], (1, HALF)) for n in range(6)])
     coef_ref[...] = jnp.concatenate(coef + [jnp.zeros((5, HALF), f32)], axis=0)
     full = []
@@ -879,7 +877,7 @@
 
     optical = jnp.zeros((height, BLOCKS), f32)
     chunks = list(range(0, sources, 2 * fold))
-    turn = -(-len(chunks) // 8)
+    turn = -(-len(chunks) // 16)
     xq, yq = (xq0_ref, xq1_ref, xq2_ref), (yq0_ref, yq1_ref, yq2_ref)
     copies = []
     pressure(0)
@@ -902,8 +900,13 @@
             vout[2, rows, lanes(h)] = vxz_ref[1, rows, lanes(h)] - w * (up - dn)
         copies.append(pltpu.make_async_copy(vout.at[:, rows], vout_any.at[:, rows], sems.at[i]))
         copies[i].start()
-        for chunk in chunks[i * turn : (i + 1) * turn]:
-            optical = optical + chunk_image(chunk)
+        if len(chunks) > 8 or i % 2 == 0:
+            for chunk in chunks[:turn]:
+                optical = optical + chunk_image(chunk)
+            chunks = chunks[turn:]
+
+    for chunk in chunks:
+        optical = optical + chunk_image(chunk)
 
     shade = 1.0 - jnp.exp(-optical)
     for m in range(height):

time: 63.7 us -> 63.6 us (level)
  no operation moved by 1% of the time
where the time goes in v3:
time: 63.6 us; the launch traced here: 63.3 us
  starting transfers between devices  23.3 us (37%)
  blocking collectives  23.3 us (37%)
  Pallas kernels  14.3 us (22%)
  waiting for transfers between devices  1.43 us (2%)
  between operations  0.87 us (1%)
    ppermute x10, starting transfers between devices, swap(): lax.ppermute(packed[start], axis, pairs + [(b, a) for a, b in pairs])  23.3 us
    pallas_call x15, Pallas kernels, call(): pl.pallas_call(kernel, out_shape=[jax.ShapeDtypeStruct(s, d) if final els...  14.3 us
    all_to_all x1, blocking collectives, shards(): moments = lax.all_to_all(send, everyone, 0, 0, tiled=True)  13.4 us
    all_to_all x1, blocking collectives, shards(): got = lax.all_to_all(send, everyone, 0, 0, tiled=True)  9.93 us
    ppermute x10, waiting for transfers between devices, swap(): lax.ppermute(packed[start], axis, pairs + [(b, a) for a, b in pairs])  1.43 us
  transfers between devices with their start and end apart: 10, of which 3 were waited for; matrix products, arithmetic and copies ran while one was open for 0% of the time, Pallas kernels for 11%

profile of v3, /device:TPU:0, one launch (start us, length us, event | category | flops | bytes accessed | tf_op | source)
XLA Modules:
  0.0 63.3 jit_solution(13018000319623496600)
XLA Ops:
  0.6 1.4 %shard_map.95 = (f32[512,256]{1,0:T(8,128)S(1)}, f32[512,256]{1,0:T(8,128)S(1)}, s32[6,256]{1,0:T(8,128)S(1)}, f32[2,64,128]{2,1,0:T(8,128)S(1)}) custom-call(f32[3,512,256]{2,1,0:T(8,128)} %v_any.3, f32[512,256]{1,0:T(8,128)} %w_any.1, s32[6,256]{1,0:T(8,128)} %nb_any.1), custom_call_target="tpu_custom_call" | custom-call | tf_op jit(solution)/shard_map/pallas_call | solution.py:923
  2.0 0.7 %collective-permute-start.1 = (f32[64,128]{1,0:T(8,128)S(1)}, f32[64,128]{1,0:T(8,128)S(1)}, u32[]{:S(2)}, u32[]{:S(2)}) collective-permute-start(f32[64,128]{1,0:T(8,128)S(1)} %get-tuple-element.104), channel_id=1, source_target_pairs={{8,16},{16,8},{9,17},{17,9},{10,18},{18,10},{11,19},{19,11},{12,20... | collective-permute-start | bytes 98312 | tf_op jit(solution)/shard_map/ppermute | solution.py:939
  2.7 4.4 %collective-permute-start = (f32[64,128]{1,0:T(8,128)S(1)}, f32[64,128]{1,0:T(8,128)S(1)}, u32[]{:S(2)}, u32[]{:S(2)}) collective-permute-start(f32[64,128]{1,0:T(8,128)S(1)} %get-tuple-element.105), channel_id=1, source_target_pairs={{0,8},{16,24},{8,0},{24,16},{1,9},{17,25},{9,1},{25,17},{2,10},{18... | collective-permute-start | bytes 98312 | tf_op jit(solution)/shard_map/ppermute | solution.py:939
  7.1 1.5 %shard_map.96 = (f32[2,512,256]{2,1,0:T(8,128)S(1)}, f32[512,256]{1,0:T(8,128)S(1)}, s32[16,256]{1,0:T(8,128)S(1)}, s32[8,128]{1,0:T(8,128)S(1)}, s32[8,256]{1,0:T(8,128)S(1)}, /*index=5*/s32[1,8]{1,0:T(1,128)S(1)}) custom-call(f32[3,512,256]{2,1,0:T(8,128)} %v_any.3, f32[512,256]{1,0:T(8,128)} %dens_any.1, s32[1,256]{1,0:T(1,128)} %bitcast.24, ...), custom_call_target="tpu_custom_call" | custom-call | tf_op jit(solution)/shard_map/pallas_call | solution.py:923
  8.6 0.0 collective-permute-done.1.second_ref
  8.6 0.0 collective-permute-done.first_ref
  8.6 0.6 shard_map.98
  9.3 0.7 %collective-permute-start.3 = (f32[2,64,128]{2,1,0:T(8,128)S(1)}, f32[2,64,128]{2,1,0:T(8,128)S(1)}, u32[]{:S(2)}, u32[]{:S(2)}) collective-permute-start(f32[2,64,128]{2,1,0:T(8,128)S(1)} %get-tuple-element.100), channel_id=1, source_target_pairs={{1,2},{3,4},{5,6},{2,1},{4,3},{6,5},{9,10},{11,12},{13,14},{10,9},... | collective-permute-start | bytes 196616 | tf_op jit(solution)/shard_map/ppermute | solution.py:939
  9.9 4.3 %collective-permute-start.2 = (f32[2,64,128]{2,1,0:T(8,128)S(1)}, f32[2,64,128]{2,1,0:T(8,128)S(1)}, u32[]{:S(2)}, u32[]{:S(2)}) collective-permute-start(f32[2,64,128]{2,1,0:T(8,128)S(1)} %get-tuple-element.101), channel_id=1, source_target_pairs={{0,1},{2,3},{4,5},{6,7},{1,0},{3,2},{5,4},{7,6},{8,9},{10,11},{12,... | collective-permute-start | bytes 196616 | tf_op jit(solution)/shard_map/ppermute | solution.py:939
  14.3 1.0 %shard_map.99 = (s32[16,128]{1,0:T(8,128)S(1)}, f32[8,128]{1,0:T(8,128)S(1)}) custom-call(s32[8,256]{1,0:T(8,128)S(1)} %get-tuple-element.64.small, s32[1,8]{1,0:T(1,128)S(1)} %get-tuple-element.65.samples_ref, f32[2,2,64,128]{3,2,1,0:T(8,128)S(1)} %get-tuple-element.59.after_ref.esrc_ref), custom_call_target="tpu_custom_call" | custom-call | tf_op jit(solution)/shard_map/pallas_call | solution.py:923
  15.3 1.1 %shard_map.97 = (f32[2,512,128]{2,1,0:T(8,128)S(1)}, f32[2,512,128]{2,1,0:T(8,128)S(1)}, f32[6,2,512,128]{3,2,1,0:T(8,128)S(1)}, f32[2,2,64,128]{3,2,1,0:T(8,128)S(1)}) custom-call(f32[2,512,256]{2,1,0:T(8,128)S(1)} %get-tuple-element.50.vxz_ref, f32[512,256]{1,0:T(8,128)S(1)} %get-tuple-element.52.vy_ref, f32[512,256]{1,0:T(8,128)S(1)} %get-tuple-element.51.w_ref, ...), custom_call_target="tpu_custom_call" | custom-call | tf_op jit(solution)/shard_map/pallas_call | solution.py:923
  16.3 0.0 collective-permute-done.3.second_ref
  16.3 0.2 collective-permute-done.2.first_ref
  16.5 0.7 %shard_map.100 = (f32[2,512,128]{2,1,0:T(8,128)S(1)}, f32[2,512,128]{2,1,0:T(8,128)S(1)}, f32[2,512,128]{2,1,0:T(8,128)S(1)}, f32[2,2,64,128]{3,2,1,0:T(8,128)S(...) custom-call(f32[2,512,256]{2,1,0:T(8,128)S(1)} %get-tuple-element.50, ...), custom_call_target="tpu_custom_call", output_to_operand_aliasing={{0}: (3, {})} | custom-call | tf_op jit(solution)/shard_map/pallas_call | solution.py:923
  17.3 0.7 %collective-permute-start.5 = (f32[128,128]{1,0:T(8,128)S(1)}, f32[128,128]{1,0:T(8,128)S(1)}, u32[]{:S(2)}, u32[]{:S(2)}) collective-permute-start(f32[128,128]{1,0:T(8,128)S(1)} %get-tuple-element.98), channel_id=1, source_target_pairs={{8,16},{16,8},{9,17},{17,9},{10,18},{18,10},{11,19},{19,11},{12,20... | collective-permute-start | bytes 196616 | tf_op jit(solution)/shard_map/ppermute | solution.py:939
  18.0 3.0 %collective-permute-start.4 = (f32[128,128]{1,0:T(8,128)S(1)}, f32[128,128]{1,0:T(8,128)S(1)}, u32[]{:S(2)}, u32[]{:S(2)}) collective-permute-start(f32[128,128]{1,0:T(8,128)S(1)} %get-tuple-element.99), channel_id=1, source_target_pairs={{0,8},{16,24},{8,0},{24,16},{1,9},{17,25},{9,1},{25,17},{2,10},{18... | collective-permute-start | bytes 196616 | tf_op jit(solution)/shard_map/ppermute | solution.py:939
  21.0 0.6 shard_map.101.pz1_ref
  21.6 0.0 collective-permute-done.5.second_ref
  21.6 0.3 collective-permute-done.4.first_ref
  21.9 0.9 %shard_map.102 = (f32[2,512,128]{2,1,0:T(8,128)S(1)}, f32[2,2,64,128]{3,2,1,0:T(8,128)S(1)}, f32[2,2,64,128]{3,2,1,0:T(8,128)S(1)}, f32[2,2,64,128]{3,2,1,0:T(8,128)S(1)}, f32[2,112,128]{2,1,0:T(8,128)S(1)}) custom-call(f32[2,512,256]{2,1,0:T(8,128)S(1)} %get-tuple-element.50.vxz_ref, ...), custom_call_target="tpu_custom_call", output_to_operand_aliasing={{0}: (3, {})} | custom-call | tf_op jit(solution)/shard_map/pallas_call | solution.py:923
  22.8 0.7 %collective-permute-start.7 = (f32[112,128]{1,0:T(8,128)S(1)}, f32[112,128]{1,0:T(8,128)S(1)}, u32[]{:S(2)}, u32[]{:S(2)}) collective-permute-start(f32[112,128]{1,0:T(8,128)S(1)} %get-tuple-element.102), channel_id=1, source_target_pairs={{1,2},{3,4},{5,6},{2,1},{4,3},{6,5},{9,10},{11,12},{13,14},{10,9},... | collective-permute-start | bytes 172040 | tf_op jit(solution)/shard_map/ppermute | solution.py:939
  23.5 4.8 %collective-permute-start.6 = (f32[112,128]{1,0:T(8,128)S(1)}, f32[112,128]{1,0:T(8,128)S(1)}, u32[]{:S(2)}, u32[]{:S(2)}) collective-permute-start(f32[112,128]{1,0:T(8,128)S(1)} %get-tuple-element.103), channel_id=1, source_target_pairs={{0,1},{2,3},{4,5},{6,7},{1,0},{3,2},{5,4},{7,6},{8,9},{10,11},{12,... | collective-permute-start | bytes 172040 | tf_op jit(solution)/shard_map/ppermute | solution.py:939
  28.3 0.6 %shard_map.103.pz2_ref = f32[2,512,128]{2,1,0:T(8,128)S(1)} custom-call(f32[2,512,128]{2,1,0:T(8,128)S(1)} %get-tuple-element.72.z1_ref, f32[6,2,512,128]{3,2,1,0:T(8,128)S(1)} %get-tuple-element.61.aux_ref, f32[2,2,64,128]{3,2,1,0:T(8,128)S(1)} %get-tuple-element.68.xsum_ref, f32[2,512,128]{2,1,0:T(8,128)S(1)} %get-tuple-element.69.rdia_ref, ...), custom_call_target="tpu_custom_call" | custom-call | tf_op jit(solution)/shard_map/pallas_call | solution.py:923
  29.0 1.2 %shard_map.104 = (f32[3,2,64,128]{3,2,1,0:T(8,128)S(1)}, f32[2,2,64,128]{3,2,1,0:T(8,128)S(1)}, f32[2,3,8,128]{3,2,1,0:T(8,128)S(1)}) custom-call(f32[2,512,256]{2,1,0:T(8,128)S(1)} %get-tuple-element.50.vxz_ref, f32[512,256]{1,0:T(8,128)S(1)} %get-tuple-element.52.vy_ref, f32[512,256]{1,0:T(8,128)S(1)} %get-tuple-element.53.dens_ref, ...), custom_call_target="tpu_custom_call" | custom-call | tf_op jit(solution)/shard_map/pallas_call | solution.py:923
  30.2 0.0 collective-permute-done.7.second_ref
  30.2 1.0 %collective-permute-done.6.first_ref = f32[112,128]{1,0:T(8,128)S(1)} collective-permute-done((f32[112,128]{1,0:T(8,128)S(1)}, f32[112,128]{1,0:T(8,128)S(1)}, u32[]{:S(2)}, u32[]{:S(2)}) %collective-permute-start.6) | collective-permute-done | bytes 57376 | tf_op jit(solution)/shard_map/ppermute | solution.py:939
  31.2 0.6 shard_map.105
  31.8 0.7 %collective-permute-start.9 = (f32[160,128]{1,0:T(8,128)S(1)}, f32[160,128]{1,0:T(8,128)S(1)}, u32[]{:S(2)}, u32[]{:S(2)}) collective-permute-start(f32[160,128]{1,0:T(8,128)S(1)} %get-tuple-element.96), channel_id=1, source_target_pairs={{8,16},{16,8},{9,17},{17,9},{10,18},{18,10},{11,19},{19,11},{12,20... | collective-permute-start | bytes 245768 | tf_op jit(solution)/shard_map/ppermute | solution.py:939
  32.5 3.3 %collective-permute-start.8 = (f32[160,128]{1,0:T(8,128)S(1)}, f32[160,128]{1,0:T(8,128)S(1)}, u32[]{:S(2)}, u32[]{:S(2)}) collective-permute-start(f32[160,128]{1,0:T(8,128)S(1)} %get-tuple-element.97), channel_id=1, source_target_pairs={{0,8},{16,24},{8,0},{24,16},{1,9},{17,25},{9,1},{25,17},{2,10},{18... | collective-permute-start | bytes 245768 | tf_op jit(solution)/shard_map/ppermute | solution.py:939
  35.8 1.0 %shard_map.106 = (f32[4,2,64,128]{3,2,1,0:T(8,128)S(1)}, f32[2,3,8,128]{3,2,1,0:T(8,128)S(1)}, f32[2,2,64,128]{3,2,1,0:T(8,128)S(1)}) custom-call(f32[2,512,128]{2,1,0:T(8,128)S(1)} %get-tuple-element.72.z1_ref, f32[2,512,128]{2,1,0:T(8,128)S(1)} %get-tuple-element.79.z2_ref, f32[2,512,128]{2,1,0:T(8,128)S(1)} %get-tuple-element.76.dia_ref, ...), custom_call_target="tpu_custom_call" | custom-call | tf_op jit(solution)/shard_map/pallas_call | solution.py:923
  36.9 0.0 collective-permute-done.9.second_ref
  36.9 0.0 collective-permute-done.8.first_ref
  36.9 0.4 shard_map.107
  37.3 13.4 %all_to_all.10.got_ref.names_ref = f32[32,1,128]{2,1,0:T(1,128)S(1)} all-to-all(f32[32,1,128]{2,1,0:T(1,128)S(1)} %get-tuple-element.90), channel_id=1, replica_groups=mesh['grp'=4,'dev'=8] {'dev','grp'}, dimensions={0} | all-to-all | bytes 32768 | tf_op jit(solution)/shard_map/all_to_all | solution.py:1051
  50.7 0.4 shard_map.108
  51.1 9.9 %all_to_all.11.got_ref = f32[32,8,128]{2,1,0:T(8,128)S(1)} all-to-all(f32[32,8,128]{2,1,0:T(8,128)S(1)} %get-tuple-element.93), channel_id=1, replica_groups=mesh['grp'=4,'dev'=8] {'dev','grp'}, dimensions={0} | all-to-all | bytes 262144 | tf_op jit(solution)/shard_map/all_to_all | solution.py:1058
  61.1 2.2 %shard_map.109 = (f32[3,512,256]{2,1,0:T(8,128)}, f32[1,4096]{1,0:T(1,128)}) custom-call(f32[32,8,128]{2,1,0:T(8,128)S(1)} %all_to_all.11.got_ref, f32[32,1,128]{2,1,0:T(1,128)S(1)} %all_to_all.10.got_ref.names_ref, f32[8,128]{1,0:T(8,128)S(1)} %get-tuple-element.94.coef_ref, f32[2,512,256]{2,1,0:T(8,128)S(1)} %get-tuple-element.50.vxz_ref, ...), custom_call_target="tpu_custom_call" | custom-call | tf_op jit(solution)/shard_map/pallas_call | solution.py:923
  (5 shorter events, 0.1 us)
Async XLA Ops:
  2.0 6.6 %collective-permute-start.1 = (f32[64,128]{1,0:T(8,128)S(1)}, f32[64,128]{1,0:T(8,128)S(1)}, u32[]{:S(2)}, u32[]{:S(2)}) collective-permute-start(f32[64,128]{1,0:T(8,128)S(1)} %get-tuple-element.104), channel_id=1, source_target_pairs={{8,16},{16,8},{9,17},{17,9},{10,18},{18,10},{11,19},{19,11},{12,20... | collective-permute-start | bytes 98312 | tf_op jit(solution)/shard_map/ppermute | solution.py:939
  2.7 5.9 %collective-permute-start = (f32[64,128]{1,0:T(8,128)S(1)}, f32[64,128]{1,0:T(8,128)S(1)}, u32[]{:S(2)}, u32[]{:S(2)}) collective-permute-start(f32[64,128]{1,0:T(8,128)S(1)} %get-tuple-element.105), channel_id=1, source_target_pairs={{0,8},{16,24},{8,0},{24,16},{1,9},{17,25},{9,1},{25,17},{2,10},{18... | collective-permute-start | bytes 98312 | tf_op jit(solution)/shard_map/ppermute | solution.py:939
  9.3 7.1 %collective-permute-start.3 = (f32[2,64,128]{2,1,0:T(8,128)S(1)}, f32[2,64,128]{2,1,0:T(8,128)S(1)}, u32[]{:S(2)}, u32[]{:S(2)}) collective-permute-start(f32[2,64,128]{2,1,0:T(8,128)S(1)} %get-tuple-element.100), channel_id=1, source_target_pairs={{1,2},{3,4},{5,6},{2,1},{4,3},{6,5},{9,10},{11,12},{13,14},{10,9},... | collective-permute-start | bytes 196616 | tf_op jit(solution)/shard_map/ppermute | solution.py:939
  9.9 6.6 %collective-permute-start.2 = (f32[2,64,128]{2,1,0:T(8,128)S(1)}, f32[2,64,128]{2,1,0:T(8,128)S(1)}, u32[]{:S(2)}, u32[]{:S(2)}) collective-permute-start(f32[2,64,128]{2,1,0:T(8,128)S(1)} %get-tuple-element.101), channel_id=1, source_target_pairs={{0,1},{2,3},{4,5},{6,7},{1,0},{3,2},{5,4},{7,6},{8,9},{10,11},{12,... | collective-permute-start | bytes 196616 | tf_op jit(solution)/shard_map/ppermute | solution.py:939
  17.3 4.3 %collective-permute-start.5 = (f32[128,128]{1,0:T(8,128)S(1)}, f32[128,128]{1,0:T(8,128)S(1)}, u32[]{:S(2)}, u32[]{:S(2)}) collective-permute-start(f32[128,128]{1,0:T(8,128)S(1)} %get-tuple-element.98), channel_id=1, source_target_pairs={{8,16},{16,8},{9,17},{17,9},{10,18},{18,10},{11,19},{19,11},{12,20... | collective-permute-start | bytes 196616 | tf_op jit(solution)/shard_map/ppermute | solution.py:939
  18.0 4.0 %collective-permute-start.4 = (f32[128,128]{1,0:T(8,128)S(1)}, f32[128,128]{1,0:T(8,128)S(1)}, u32[]{:S(2)}, u32[]{:S(2)}) collective-permute-start(f32[128,128]{1,0:T(8,128)S(1)} %get-tuple-element.99), channel_id=1, source_target_pairs={{0,8},{16,24},{8,0},{24,16},{1,9},{17,25},{9,1},{25,17},{2,10},{18... | collective-permute-start | bytes 196616 | tf_op jit(solution)/shard_map/ppermute | solution.py:939
  22.8 7.4 %collective-permute-start.7 = (f32[112,128]{1,0:T(8,128)S(1)}, f32[112,128]{1,0:T(8,128)S(1)}, u32[]{:S(2)}, u32[]{:S(2)}) collective-permute-start(f32[112,128]{1,0:T(8,128)S(1)} %get-tuple-element.102), channel_id=1, source_target_pairs={{1,2},{3,4},{5,6},{2,1},{4,3},{6,5},{9,10},{11,12},{13,14},{10,9},... | collective-permute-start | bytes 172040 | tf_op jit(solution)/shard_map/ppermute | solution.py:939
  23.5 7.7 %collective-permute-start.6 = (f32[112,128]{1,0:T(8,128)S(1)}, f32[112,128]{1,0:T(8,128)S(1)}, u32[]{:S(2)}, u32[]{:S(2)}) collective-permute-start(f32[112,128]{1,0:T(8,128)S(1)} %get-tuple-element.103), channel_id=1, source_target_pairs={{0,1},{2,3},{4,5},{6,7},{1,0},{3,2},{5,4},{7,6},{8,9},{10,11},{12,... | collective-permute-start | bytes 172040 | tf_op jit(solution)/shard_map/ppermute | solution.py:939
  31.8 5.1 %collective-permute-start.9 = (f32[160,128]{1,0:T(8,128)S(1)}, f32[160,128]{1,0:T(8,128)S(1)}, u32[]{:S(2)}, u32[]{:S(2)}) collective-permute-start(f32[160,128]{1,0:T(8,128)S(1)} %get-tuple-element.96), channel_id=1, source_target_pairs={{8,16},{16,8},{9,17},{17,9},{10,18},{18,10},{11,19},{19,11},{12,20... | collective-permute-start | bytes 245768 | tf_op jit(solution)/shard_map/ppermute | solution.py:939
  32.5 4.4 %collective-permute-start.8 = (f32[160,128]{1,0:T(8,128)S(1)}, f32[160,128]{1,0:T(8,128)S(1)}, u32[]{:S(2)}, u32[]{:S(2)}) collective-permute-start(f32[160,128]{1,0:T(8,128)S(1)} %get-tuple-element.97), channel_id=1, source_target_pairs={{0,8},{16,24},{8,0},{24,16},{1,9},{17,25},{9,1},{25,17},{2,10},{18... | collective-permute-start | bytes 245768 | tf_op jit(solution)/shard_map/ppermute | solution.py:939

commit v4 on v3

--- a/solution.py
+++ b/solution.py
@@ -123,15 +123,17 @@
 ):
     copies = [
         pltpu.make_async_copy(nb_any, nb_ref, sems.at[0]),
-        pltpu.make_async_copy(v_any.at[1], vy_ref, sems.at[1]),
-        pltpu.make_async_copy(w_any, w_ref, sems.at[2]),
     ]
+    for n in range(4):
+        part = slice(128 * n, 128 * n + 128)
+        copies.append(pltpu.make_async_copy(v_any.at[1, part], vy_ref.at[part], sems.at[1 + n]))
+        copies.append(pltpu.make_async_copy(w_any.at[part], w_ref.at[part], sems.at[5 + n]))
     for c in copies:
         c.start()
     copies[0].wait()
     clane, ccode = link_lists(nb_ref[...], (2, 3), dev_size)[-2:]
-    copies[1].wait()
-    copies[2].wait()
+    for c in copies[1:]:
+        c.wait()
     for n, j in ((0, 0), (1, 7)):
         send_ref[slot_of(n, odd_on("grp"))] = packed_pair(
             [face_y(lambda r, m: vy_ref[r : r + m, lanes(h)], j) for h in range(2)],
@@ -761,7 +763,7 @@
         names = pltpu.roll(ids_ref[t : t + 1, :], SLOTS, 1)
         line = jnp.where(which < SLOTS, row, names)
         for g in range(g_count):
-            send_ref[t * g_count + g] = line
+            send_ref[g * tiles + t] = line
 
 
 def pairwise(terms):
@@ -825,7 +827,7 @@
             part = value[g * height : g * height + height]
             if fold == 2:
                 part = jnp.where(left, part[0:8], part[8:16])
-            send_ref[t * g_count + g] = part
+            send_ref[g * tiles + t] = part
 
 
 def final_kernel(
@@ -950,7 +952,7 @@
     height = 64 // grp_size
     fold = min(height // 8, HALF // cap)
     sources = grp_size * dev_size
-    everyone = ("dev", "grp")
+    everyone = ("grp", "dev")
 
     field = ((2, 512, HALF), f32)
     sides = ((2, 2, 64, HALF), f32)
@@ -961,7 +963,7 @@
     vy, inv, nb, send = call(
         functools.partial(load_kernel, dev_size),
         [((512, count), f32), ((512, count), f32), ((6, count), i32), ((2, 64, HALF), f32)],
-        [pltpu.SemaphoreType.DMA((3,))],
+        [pltpu.SemaphoreType.DMA((9,))],
         (velocity, inverse_density, neighbours),
         any_args=3,
     )

time: 63.6 us -> 63.2 us (level)
  no operation moved by 1% of the time
where the time goes in v4:
time: 63.2 us; the launch traced here: 62.9 us
  starting transfers between devices  23.3 us (37%)
  blocking collectives  22.8 us (36%)
  Pallas kernels  14.4 us (23%)
  waiting for transfers between devices  1.43 us (2%)
  between operations  0.87 us (1%)
    ppermute x10, starting transfers between devices, swap(): lax.ppermute(packed[start], axis, pairs + [(b, a) for a, b in pairs])  23.3 us
    pallas_call x15, Pallas kernels, call(): pl.pallas_call(kernel, out_shape=[jax.ShapeDtypeStruct(s, d) if final els...  14.4 us
    all_to_all x1, blocking collectives, shards(): moments = lax.all_to_all(send, everyone, 0, 0, tiled=True)  13.4 us
    all_to_all x1, blocking collectives, shards(): got = lax.all_to_all(send, everyone, 0, 0, tiled=True)  9.44 us
    ppermute x10, waiting for transfers between devices, swap(): lax.ppermute(packed[start], axis, pairs + [(b, a) for a, b in pairs])  1.43 us
  transfers between devices with their start and end apart: 10, of which 3 were waited for; matrix products, arithmetic and copies ran while one was open for 0% of the time, Pallas kernels for 11%

profile of v4, /device:TPU:0, one launch (start us, length us, event | category | flops | bytes accessed | tf_op | source)
XLA Modules:
  0.0 62.9 jit_solution(2551241326067685416)
XLA Ops:
  0.6 1.5 %shard_map.95 = (f32[512,256]{1,0:T(8,128)S(1)}, f32[512,256]{1,0:T(8,128)S(1)}, s32[6,256]{1,0:T(8,128)S(1)}, f32[2,64,128]{2,1,0:T(8,128)S(1)}) custom-call(f32[3,512,256]{2,1,0:T(8,128)} %v_any.3, f32[512,256]{1,0:T(8,128)} %w_any.1, s32[6,256]{1,0:T(8,128)} %nb_any.1), custom_call_target="tpu_custom_call" | custom-call | tf_op jit(solution)/shard_map/pallas_call | solution.py:925
  2.2 0.7 %collective-permute-start.1 = (f32[64,128]{1,0:T(8,128)S(1)}, f32[64,128]{1,0:T(8,128)S(1)}, u32[]{:S(2)}, u32[]{:S(2)}) collective-permute-start(f32[64,128]{1,0:T(8,128)S(1)} %get-tuple-element.104), channel_id=1, source_target_pairs={{8,16},{16,8},{9,17},{17,9},{10,18},{18,10},{11,19},{19,11},{12,20... | collective-permute-start | bytes 98312 | tf_op jit(solution)/shard_map/ppermute | solution.py:941
  2.8 4.4 %collective-permute-start = (f32[64,128]{1,0:T(8,128)S(1)}, f32[64,128]{1,0:T(8,128)S(1)}, u32[]{:S(2)}, u32[]{:S(2)}) collective-permute-start(f32[64,128]{1,0:T(8,128)S(1)} %get-tuple-element.105), channel_id=1, source_target_pairs={{0,8},{16,24},{8,0},{24,16},{1,9},{17,25},{9,1},{25,17},{2,10},{18... | collective-permute-start | bytes 98312 | tf_op jit(solution)/shard_map/ppermute | solution.py:941
  7.2 1.5 %shard_map.96 = (f32[2,512,256]{2,1,0:T(8,128)S(1)}, f32[512,256]{1,0:T(8,128)S(1)}, s32[16,256]{1,0:T(8,128)S(1)}, s32[8,128]{1,0:T(8,128)S(1)}, s32[8,256]{1,0:T(8,128)S(1)}, /*index=5*/s32[1,8]{1,0:T(1,128)S(1)}) custom-call(f32[3,512,256]{2,1,0:T(8,128)} %v_any.3, f32[512,256]{1,0:T(8,128)} %dens_any.1, s32[1,256]{1,0:T(1,128)} %bitcast.24, ...), custom_call_target="tpu_custom_call" | custom-call | tf_op jit(solution)/shard_map/pallas_call | solution.py:925
  8.7 0.0 collective-permute-done.1.second_ref
  8.7 0.0 collective-permute-done.first_ref
  8.7 0.6 shard_map.98
  9.4 0.7 %collective-permute-start.3 = (f32[2,64,128]{2,1,0:T(8,128)S(1)}, f32[2,64,128]{2,1,0:T(8,128)S(1)}, u32[]{:S(2)}, u32[]{:S(2)}) collective-permute-start(f32[2,64,128]{2,1,0:T(8,128)S(1)} %get-tuple-element.100), channel_id=1, source_target_pairs={{1,2},{3,4},{5,6},{2,1},{4,3},{6,5},{9,10},{11,12},{13,14},{10,9},... | collective-permute-start | bytes 196616 | tf_op jit(solution)/shard_map/ppermute | solution.py:941
  10.1 4.3 %collective-permute-start.2 = (f32[2,64,128]{2,1,0:T(8,128)S(1)}, f32[2,64,128]{2,1,0:T(8,128)S(1)}, u32[]{:S(2)}, u32[]{:S(2)}) collective-permute-start(f32[2,64,128]{2,1,0:T(8,128)S(1)} %get-tuple-element.101), channel_id=1, source_target_pairs={{0,1},{2,3},{4,5},{6,7},{1,0},{3,2},{5,4},{7,6},{8,9},{10,11},{12,... | collective-permute-start | bytes 196616 | tf_op jit(solution)/shard_map/ppermute | solution.py:941
  14.4 1.0 %shard_map.99 = (s32[16,128]{1,0:T(8,128)S(1)}, f32[8,128]{1,0:T(8,128)S(1)}) custom-call(s32[8,256]{1,0:T(8,128)S(1)} %get-tuple-element.64.small, s32[1,8]{1,0:T(1,128)S(1)} %get-tuple-element.65.samples_ref, f32[2,2,64,128]{3,2,1,0:T(8,128)S(1)} %get-tuple-element.59.after_ref.esrc_ref), custom_call_target="tpu_custom_call" | custom-call | tf_op jit(solution)/shard_map/pallas_call | solution.py:925
  15.4 1.1 %shard_map.97 = (f32[2,512,128]{2,1,0:T(8,128)S(1)}, f32[2,512,128]{2,1,0:T(8,128)S(1)}, f32[6,2,512,128]{3,2,1,0:T(8,128)S(1)}, f32[2,2,64,128]{3,2,1,0:T(8,128)S(1)}) custom-call(f32[2,512,256]{2,1,0:T(8,128)S(1)} %get-tuple-element.50.vxz_ref, f32[512,256]{1,0:T(8,128)S(1)} %get-tuple-element.52.vy_ref, f32[512,256]{1,0:T(8,128)S(1)} %get-tuple-element.51.w_ref, ...), custom_call_target="tpu_custom_call" | custom-call | tf_op jit(solution)/shard_map/pallas_call | solution.py:925
  16.5 0.0 collective-permute-done.3.second_ref
  16.5 0.2 collective-permute-done.2.first_ref
  16.6 0.7 %shard_map.100 = (f32[2,512,128]{2,1,0:T(8,128)S(1)}, f32[2,512,128]{2,1,0:T(8,128)S(1)}, f32[2,512,128]{2,1,0:T(8,128)S(1)}, f32[2,2,64,128]{3,2,1,0:T(8,128)S(...) custom-call(f32[2,512,256]{2,1,0:T(8,128)S(1)} %get-tuple-element.50, ...), custom_call_target="tpu_custom_call", output_to_operand_aliasing={{0}: (3, {})} | custom-call | tf_op jit(solution)/shard_map/pallas_call | solution.py:925
  17.4 0.7 %collective-permute-start.5 = (f32[128,128]{1,0:T(8,128)S(1)}, f32[128,128]{1,0:T(8,128)S(1)}, u32[]{:S(2)}, u32[]{:S(2)}) collective-permute-start(f32[128,128]{1,0:T(8,128)S(1)} %get-tuple-element.98), channel_id=1, source_target_pairs={{8,16},{16,8},{9,17},{17,9},{10,18},{18,10},{11,19},{19,11},{12,20... | collective-permute-start | bytes 196616 | tf_op jit(solution)/shard_map/ppermute | solution.py:941
  18.1 3.0 %collective-permute-start.4 = (f32[128,128]{1,0:T(8,128)S(1)}, f32[128,128]{1,0:T(8,128)S(1)}, u32[]{:S(2)}, u32[]{:S(2)}) collective-permute-start(f32[128,128]{1,0:T(8,128)S(1)} %get-tuple-element.99), channel_id=1, source_target_pairs={{0,8},{16,24},{8,0},{24,16},{1,9},{17,25},{9,1},{25,17},{2,10},{18... | collective-permute-start | bytes 196616 | tf_op jit(solution)/shard_map/ppermute | solution.py:941
  21.1 0.6 shard_map.101.pz1_ref
  21.8 0.0 collective-permute-done.5.second_ref
  21.8 0.3 collective-permute-done.4.first_ref
  22.0 0.9 %shard_map.102 = (f32[2,512,128]{2,1,0:T(8,128)S(1)}, f32[2,2,64,128]{3,2,1,0:T(8,128)S(1)}, f32[2,2,64,128]{3,2,1,0:T(8,128)S(1)}, f32[2,2,64,128]{3,2,1,0:T(8,128)S(1)}, f32[2,112,128]{2,1,0:T(8,128)S(1)}) custom-call(f32[2,512,256]{2,1,0:T(8,128)S(1)} %get-tuple-element.50.vxz_ref, ...), custom_call_target="tpu_custom_call", output_to_operand_aliasing={{0}: (3, {})} | custom-call | tf_op jit(solution)/shard_map/pallas_call | solution.py:925
  23.0 0.7 %collective-permute-start.7 = (f32[112,128]{1,0:T(8,128)S(1)}, f32[112,128]{1,0:T(8,128)S(1)}, u32[]{:S(2)}, u32[]{:S(2)}) collective-permute-start(f32[112,128]{1,0:T(8,128)S(1)} %get-tuple-element.102), channel_id=1, source_target_pairs={{1,2},{3,4},{5,6},{2,1},{4,3},{6,5},{9,10},{11,12},{13,14},{10,9},... | collective-permute-start | bytes 172040 | tf_op jit(solution)/shard_map/ppermute | solution.py:941
  23.6 4.8 %collective-permute-start.6 = (f32[112,128]{1,0:T(8,128)S(1)}, f32[112,128]{1,0:T(8,128)S(1)}, u32[]{:S(2)}, u32[]{:S(2)}) collective-permute-start(f32[112,128]{1,0:T(8,128)S(1)} %get-tuple-element.103), channel_id=1, source_target_pairs={{0,1},{2,3},{4,5},{6,7},{1,0},{3,2},{5,4},{7,6},{8,9},{10,11},{12,... | collective-permute-start | bytes 172040 | tf_op jit(solution)/shard_map/ppermute | solution.py:941
  28.5 0.6 %shard_map.103.pz2_ref = f32[2,512,128]{2,1,0:T(8,128)S(1)} custom-call(f32[2,512,128]{2,1,0:T(8,128)S(1)} %get-tuple-element.72.z1_ref, f32[6,2,512,128]{3,2,1,0:T(8,128)S(1)} %get-tuple-element.61.aux_ref, f32[2,2,64,128]{3,2,1,0:T(8,128)S(1)} %get-tuple-element.68.xsum_ref, f32[2,512,128]{2,1,0:T(8,128)S(1)} %get-tuple-element.69.rdia_ref, ...), custom_call_target="tpu_custom_call" | custom-call | tf_op jit(solution)/shard_map/pallas_call | solution.py:925
  29.1 1.2 %shard_map.104 = (f32[3,2,64,128]{3,2,1,0:T(8,128)S(1)}, f32[2,2,64,128]{3,2,1,0:T(8,128)S(1)}, f32[2,3,8,128]{3,2,1,0:T(8,128)S(1)}) custom-call(f32[2,512,256]{2,1,0:T(8,128)S(1)} %get-tuple-element.50.vxz_ref, f32[512,256]{1,0:T(8,128)S(1)} %get-tuple-element.52.vy_ref, f32[512,256]{1,0:T(8,128)S(1)} %get-tuple-element.53.dens_ref, ...), custom_call_target="tpu_custom_call" | custom-call | tf_op jit(solution)/shard_map/pallas_call | solution.py:925
  30.3 0.0 collective-permute-done.7.second_ref
  30.3 1.0 %collective-permute-done.6.first_ref = f32[112,128]{1,0:T(8,128)S(1)} collective-permute-done((f32[112,128]{1,0:T(8,128)S(1)}, f32[112,128]{1,0:T(8,128)S(1)}, u32[]{:S(2)}, u32[]{:S(2)}) %collective-permute-start.6) | collective-permute-done | bytes 57376 | tf_op jit(solution)/shard_map/ppermute | solution.py:941
  31.3 0.6 shard_map.105
  31.9 0.7 %collective-permute-start.9 = (f32[160,128]{1,0:T(8,128)S(1)}, f32[160,128]{1,0:T(8,128)S(1)}, u32[]{:S(2)}, u32[]{:S(2)}) collective-permute-start(f32[160,128]{1,0:T(8,128)S(1)} %get-tuple-element.96), channel_id=1, source_target_pairs={{8,16},{16,8},{9,17},{17,9},{10,18},{18,10},{11,19},{19,11},{12,20... | collective-permute-start | bytes 245768 | tf_op jit(solution)/shard_map/ppermute | solution.py:941
  32.6 3.3 %collective-permute-start.8 = (f32[160,128]{1,0:T(8,128)S(1)}, f32[160,128]{1,0:T(8,128)S(1)}, u32[]{:S(2)}, u32[]{:S(2)}) collective-permute-start(f32[160,128]{1,0:T(8,128)S(1)} %get-tuple-element.97), channel_id=1, source_target_pairs={{0,8},{16,24},{8,0},{24,16},{1,9},{17,25},{9,1},{25,17},{2,10},{18... | collective-permute-start | bytes 245768 | tf_op jit(solution)/shard_map/ppermute | solution.py:941
  36.0 1.0 %shard_map.106 = (f32[4,2,64,128]{3,2,1,0:T(8,128)S(1)}, f32[2,3,8,128]{3,2,1,0:T(8,128)S(1)}, f32[2,2,64,128]{3,2,1,0:T(8,128)S(1)}) custom-call(f32[2,512,128]{2,1,0:T(8,128)S(1)} %get-tuple-element.72.z1_ref, f32[2,512,128]{2,1,0:T(8,128)S(1)} %get-tuple-element.79.z2_ref, f32[2,512,128]{2,1,0:T(8,128)S(1)} %get-tuple-element.76.dia_ref, ...), custom_call_target="tpu_custom_call" | custom-call | tf_op jit(solution)/shard_map/pallas_call | solution.py:925
  37.0 0.0 collective-permute-done.9.second_ref
  37.0 0.0 collective-permute-done.8.first_ref
  37.0 0.4 shard_map.107
  37.5 13.4 %all_to_all.10.got_ref.names_ref = f32[32,1,128]{2,1,0:T(1,128)S(1)} all-to-all(f32[32,1,128]{2,1,0:T(1,128)S(1)} %get-tuple-element.90), channel_id=1, replica_groups=mesh['grp'=4,'dev'=8] {'grp','dev'}, dimensions={0} | all-to-all | bytes 32768 | tf_op jit(solution)/shard_map/all_to_all | solution.py:1053
  50.8 0.4 shard_map.108
  51.2 9.4 %all_to_all.11.got_ref = f32[32,8,128]{2,1,0:T(8,128)S(1)} all-to-all(f32[32,8,128]{2,1,0:T(8,128)S(1)} %get-tuple-element.93), channel_id=1, replica_groups=mesh['grp'=4,'dev'=8] {'grp','dev'}, dimensions={0} | all-to-all | bytes 262144 | tf_op jit(solution)/shard_map/all_to_all | solution.py:1060
  60.7 2.2 %shard_map.109 = (f32[3,512,256]{2,1,0:T(8,128)}, f32[1,4096]{1,0:T(1,128)}) custom-call(f32[32,8,128]{2,1,0:T(8,128)S(1)} %all_to_all.11.got_ref, f32[32,1,128]{2,1,0:T(1,128)S(1)} %all_to_all.10.got_ref.names_ref, f32[8,128]{1,0:T(8,128)S(1)} %get-tuple-element.94.coef_ref, f32[2,512,256]{2,1,0:T(8,128)S(1)} %get-tuple-element.50.vxz_ref, ...), custom_call_target="tpu_custom_call" | custom-call | tf_op jit(solution)/shard_map/pallas_call | solution.py:925
  (5 shorter events, 0.1 us)
Async XLA Ops:
  2.2 6.6 %collective-permute-start.1 = (f32[64,128]{1,0:T(8,128)S(1)}, f32[64,128]{1,0:T(8,128)S(1)}, u32[]{:S(2)}, u32[]{:S(2)}) collective-permute-start(f32[64,128]{1,0:T(8,128)S(1)} %get-tuple-element.104), channel_id=1, source_target_pairs={{8,16},{16,8},{9,17},{17,9},{10,18},{18,10},{11,19},{19,11},{12,20... | collective-permute-start | bytes 98312 | tf_op jit(solution)/shard_map/ppermute | solution.py:941
  2.8 5.9 %collective-permute-start = (f32[64,128]{1,0:T(8,128)S(1)}, f32[64,128]{1,0:T(8,128)S(1)}, u32[]{:S(2)}, u32[]{:S(2)}) collective-permute-start(f32[64,128]{1,0:T(8,128)S(1)} %get-tuple-element.105), channel_id=1, source_target_pairs={{0,8},{16,24},{8,0},{24,16},{1,9},{17,25},{9,1},{25,17},{2,10},{18... | collective-permute-start | bytes 98312 | tf_op jit(solution)/shard_map/ppermute | solution.py:941
  9.4 7.1 %collective-permute-start.3 = (f32[2,64,128]{2,1,0:T(8,128)S(1)}, f32[2,64,128]{2,1,0:T(8,128)S(1)}, u32[]{:S(2)}, u32[]{:S(2)}) collective-permute-start(f32[2,64,128]{2,1,0:T(8,128)S(1)} %get-tuple-element.100), channel_id=1, source_target_pairs={{1,2},{3,4},{5,6},{2,1},{4,3},{6,5},{9,10},{11,12},{13,14},{10,9},... | collective-permute-start | bytes 196616 | tf_op jit(solution)/shard_map/ppermute | solution.py:941
  10.1 6.6 %collective-permute-start.2 = (f32[2,64,128]{2,1,0:T(8,128)S(1)}, f32[2,64,128]{2,1,0:T(8,128)S(1)}, u32[]{:S(2)}, u32[]{:S(2)}) collective-permute-start(f32[2,64,128]{2,1,0:T(8,128)S(1)} %get-tuple-element.101), channel_id=1, source_target_pairs={{0,1},{2,3},{4,5},{6,7},{1,0},{3,2},{5,4},{7,6},{8,9},{10,11},{12,... | collective-permute-start | bytes 196616 | tf_op jit(solution)/shard_map/ppermute | solution.py:941
  17.4 4.3 %collective-permute-start.5 = (f32[128,128]{1,0:T(8,128)S(1)}, f32[128,128]{1,0:T(8,128)S(1)}, u32[]{:S(2)}, u32[]{:S(2)}) collective-permute-start(f32[128,128]{1,0:T(8,128)S(1)} %get-tuple-element.98), channel_id=1, source_target_pairs={{8,16},{16,8},{9,17},{17,9},{10,18},{18,10},{11,19},{19,11},{12,20... | collective-permute-start | bytes 196616 | tf_op jit(solution)/shard_map/ppermute | solution.py:941
  18.1 4.0 %collective-permute-start.4 = (f32[128,128]{1,0:T(8,128)S(1)}, f32[128,128]{1,0:T(8,128)S(1)}, u32[]{:S(2)}, u32[]{:S(2)}) collective-permute-start(f32[128,128]{1,0:T(8,128)S(1)} %get-tuple-element.99), channel_id=1, source_target_pairs={{0,8},{16,24},{8,0},{24,16},{1,9},{17,25},{9,1},{25,17},{2,10},{18... | collective-permute-start | bytes 196616 | tf_op jit(solution)/shard_map/ppermute | solution.py:941
  23.0 7.4 %collective-permute-start.7 = (f32[112,128]{1,0:T(8,128)S(1)}, f32[112,128]{1,0:T(8,128)S(1)}, u32[]{:S(2)}, u32[]{:S(2)}) collective-permute-start(f32[112,128]{1,0:T(8,128)S(1)} %get-tuple-element.102), channel_id=1, source_target_pairs={{1,2},{3,4},{5,6},{2,1},{4,3},{6,5},{9,10},{11,12},{13,14},{10,9},... | collective-permute-start | bytes 172040 | tf_op jit(solution)/shard_map/ppermute | solution.py:941
  23.6 7.7 %collective-permute-start.6 = (f32[112,128]{1,0:T(8,128)S(1)}, f32[112,128]{1,0:T(8,128)S(1)}, u32[]{:S(2)}, u32[]{:S(2)}) collective-permute-start(f32[112,128]{1,0:T(8,128)S(1)} %get-tuple-element.103), channel_id=1, source_target_pairs={{0,1},{2,3},{4,5},{6,7},{1,0},{3,2},{5,4},{7,6},{8,9},{10,11},{12,... | collective-permute-start | bytes 172040 | tf_op jit(solution)/shard_map/ppermute | solution.py:941
  31.9 5.1 %collective-permute-start.9 = (f32[160,128]{1,0:T(8,128)S(1)}, f32[160,128]{1,0:T(8,128)S(1)}, u32[]{:S(2)}, u32[]{:S(2)}) collective-permute-start(f32[160,128]{1,0:T(8,128)S(1)} %get-tuple-element.96), channel_id=1, source_target_pairs={{8,16},{16,8},{9,17},{17,9},{10,18},{18,10},{11,19},{19,11},{12,20... | collective-permute-start | bytes 245768 | tf_op jit(solution)/shard_map/ppermute | solution.py:941
  32.6 4.4 %collective-permute-start.8 = (f32[160,128]{1,0:T(8,128)S(1)}, f32[160,128]{1,0:T(8,128)S(1)}, u32[]{:S(2)}, u32[]{:S(2)}) collective-permute-start(f32[160,128]{1,0:T(8,128)S(1)} %get-tuple-element.97), channel_id=1, source_target_pairs={{0,8},{16,24},{8,0},{24,16},{1,9},{17,25},{9,1},{25,17},{2,10},{18... | collective-permute-start | bytes 245768 | tf_op jit(solution)/shard_map/ppermute | solution.py:941
